TPU v7x, 32 devices: a whole 2x2x4 slice. The times are simulated.
32 devices in a mesh: seq: 8 (over z, core), batch: 4 (over y, x).
Axes of the slice: x: 2, y: 2, z: 4, core: 2. Of those that a mesh axis runs over, the one named last changes fastest.
Arguments:
- events: bfloat16 [8, 1024, 1024], P('batch', 'seq'), may hold values from -6 to 6
- w_in: bfloat16 [1024, 4096], P(None, 'batch'), may hold values from -0.1875 to 0.1875
- w_out: bfloat16 [1024, 1024], replicated, may hold values from -0.1875 to 0.1875
- item_table: bfloat16 [4096, 1024], P(('seq', 'batch')), may hold values from -6 to 6
- item_bias: bfloat16 [4096], P(('seq', 'batch')), may hold values from -10 to -6
- segment_lengths: int32 [8, 8], P('batch'), may hold values from 1 to 512, 1024 in all within a row
- listed_pos: int32 [64, 8], P(None, 'batch'), may hold values from 0 to 1023
- labels: int32 [64, 8], P(None, 'batch'), may hold values from 0 to 4095
Outputs:
- layer_out: bfloat16 [8, 1024, 1024], P('batch', 'seq')
- hidden_grad: float32 [64, 8, 1024], P('seq', 'batch')
Inputs may be any that keep to these rules, and one draw needn't show every extreme that they name: `segment_lengths`: each row holds 8 lengths that sum to 1024; its largest is exactly 512.
All inputs are finite; a program needn't handle non-finite values.
Results may differ from a plain program's by a relative error of at most 0.0065.
Values may be sent and summed in bfloat16 or wider, within the bound.
No kernel may reach another device: no remote copies, remote signals or barrier semaphores. Data moves between devices by JAX's collectives and lax.ppermute only.
A program may use at most 64 MiB of HBM per device.

v0:
```python
import jax
import jax.numpy as jnp
from jax import lax
from jax.sharding import PartitionSpec as P

HEADS = 16
HD = 64
D = 1024


def segment_starts(lengths, length):
    ends = jnp.cumsum(lengths, axis=-1)
    positions = jnp.arange(length, dtype=jnp.int32)
    passed = (positions[:, None] >= ends[..., None, :]).astype(jnp.int32)
    return jnp.sum(passed * lengths[..., None, :], axis=-1)


def attend_head(query, key, value, start):
    head_size, length = query.shape
    block = min(512, length)
    count = length // block

    def one_block(number, result):
        number = number.astype(jnp.int32)
        rows = number * block + jnp.arange(block, dtype=jnp.int32)
        query_block = lax.dynamic_slice_in_dim(query, number * block, block, 1)
        row_start = lax.dynamic_slice_in_dim(start, number * block, block, 0)

        def add_tile(other, accum):
            other = other.astype(jnp.int32)
            columns = other * block + jnp.arange(block, dtype=jnp.int32)
            key_block = lax.dynamic_slice_in_dim(key, other * block, block, 1)
            value_block = lax.dynamic_slice_in_dim(value, other * block, block, 1)
            scores = jnp.einsum(
                "dq,dk->qk", query_block, key_block, preferred_element_type=jnp.float32
            )
            allowed = (columns[None, :] <= rows[:, None]) & (columns[None, :] >= row_start[:, None])
            weights = jnp.where(allowed, jax.nn.silu(scores), 0.0).astype(jnp.bfloat16)
            return accum + jnp.einsum(
                "qk,dk->dq", weights, value_block, preferred_element_type=jnp.float32
            )

        first = jnp.int32(0)
        accum = lax.fori_loop(
            first, number + 1, add_tile, jnp.zeros((head_size, block), jnp.float32)
        )
        return lax.dynamic_update_slice_in_dim(result, accum, number * block, 1)

    result = lax.fori_loop(
        jnp.int32(0), jnp.int32(count), one_block, jnp.zeros((head_size, length), jnp.float32)
    )
    return result.astype(jnp.bfloat16)


def on_device(events, w_in, w_out, item_table, item_bias, segment_lengths, listed_pos, labels):
    hist_here, pos_here, width = events.shape
    seq_count = lax.axis_size("seq")
    seq_rank = lax.axis_index("seq")
    projected = jnp.einsum(
        "hpd,dc->hcp",
        events,
        lax.all_gather(w_in, "batch", axis=1, tiled=True),
        preferred_element_type=jnp.float32,
    )
    acts = jax.nn.silu(projected).astype(jnp.bfloat16)
    gate_u = acts[:, :width]
    per_device = hist_here * HEADS // seq_count

    def group_heads(columns):
        return columns.reshape(seq_count, per_device, HD, pos_here)

    queries, keys, values = (
        lax.all_to_all(
            group_heads(acts[:, 2 * width : 3 * width]),
            "seq",
            split_axis=0,
            concat_axis=3,
            tiled=True,
        ),
        lax.all_to_all(
            group_heads(acts[:, 3 * width :]), "seq", split_axis=0, concat_axis=3, tiled=True
        ),
        lax.all_to_all(
            group_heads(acts[:, width : 2 * width]), "seq", split_axis=0, concat_axis=3, tiled=True
        ),
    )
    length = queries.shape[3]
    starts = segment_starts(segment_lengths, length)
    item_hist = (seq_rank * per_device + jnp.arange(per_device, dtype=jnp.int32)) // HEADS
    item_starts = starts[item_hist]
    attended = lax.map(
        lambda quad: attend_head(quad[0], quad[1], quad[2], quad[3]),
        (queries[0], keys[0], values[0], item_starts),
    )
    returned = lax.all_to_all(attended[None], "seq", split_axis=3, concat_axis=0, tiled=True)
    attended_local = returned.reshape(hist_here, width, pos_here).astype(jnp.float32)
    center = attended_local - jnp.mean(attended_local, axis=1, keepdims=True)
    spread = jnp.mean(center * center, axis=1, keepdims=True)
    normed = center * lax.rsqrt(spread + 1e-05)
    mixed = (normed * gate_u.astype(jnp.float32)).astype(jnp.bfloat16)
    output = jnp.einsum("hcp,ce->hpe", mixed, w_out, preferred_element_type=jnp.float32)
    layer_out = (events.astype(jnp.float32) + output).astype(jnp.bfloat16)
    local_pos = listed_pos - seq_rank * pos_here
    present = (local_pos >= 0) & (local_pos < pos_here)
    safe_pos = jnp.clip(local_pos, 0, pos_here - 1)
    picked = layer_out[jnp.arange(hist_here, dtype=jnp.int32)[None, :], safe_pos]
    picked = jnp.where(present[:, :, None], picked.astype(jnp.float32), 0.0)
    rows = lax.psum(picked.astype(jnp.bfloat16), "seq")
    shard_items = item_table.shape[0] * lax.axis_size("batch")
    base_item = seq_rank * shard_items
    scale = D ** (-0.5)
    table = lax.all_gather(item_table, "batch", axis=0, tiled=True)
    bias = lax.all_gather(item_bias, "batch", axis=0, tiled=True)
    item_ids = base_item + jnp.arange(table.shape[0], dtype=jnp.int32)
    logits = jnp.einsum("lhd,kd->lhk", rows, table, preferred_element_type=jnp.float32) * scale
    logits = logits + bias.astype(jnp.float32)
    target = (labels[:, :, None] == item_ids[None, None, :]).astype(jnp.float32)
    coef = (jax.nn.sigmoid(logits) - target).astype(jnp.bfloat16)
    partial_grad = jnp.einsum("lhk,kd->lhd", coef, table, preferred_element_type=jnp.float32)
    share = partial_grad.shape[0] // seq_count
    summed = lax.psum(partial_grad, "seq")
    hidden_grad = lax.dynamic_slice_in_dim(summed, seq_rank * share, share, 0)
    return (layer_out, hidden_grad)


def solution(mesh):
    return jax.shard_map(
        on_device,
        mesh=mesh,
        in_specs=(
            P("batch", "seq", None),
            P(None, "batch"),
            P(),
            P(("seq", "batch"), None),
            P(("seq", "batch")),
            P("batch", None),
            P(None, "batch"),
            P(None, "batch"),
        ),
        out_specs=(P("batch", "seq", None), P("seq", "batch", None)),
        check_vma=False,
    )
```

profile of v0, /device:TPU:0, one launch (start us, length us, event | category | flops | bytes accessed | tf_op | source)
XLA Modules:
  0.0 355.9 jit_solution(11397937475747135988)
XLA Ops:
  7.2 4.1 %copy.47 = bf16[1024,1024]{0,1:T(8,128)(2,1)} copy(bf16[1024,1024]{1,0:T(8,128)(2,1)} %param.15) | data formatting | bytes 4194304 | tf_op args[1]
  11.4 90.5 %all-gather.4.cloned.1.call-done = bf16[1024,4096]{0,1:T(8,128)(2,1)} async-done(((bf16[1024,1024]{0,1:T(8,128)(2,1)}), bf16[1024,4096]{0,1:T(8,128)(2,1)}) %all-gather.4.cloned.1.call-update) | async-done | bytes 8388624 | tf_op jit(solution)/shard_map/all_gather | solution.py:62
  101.8 8.1 %multiply_convert_fusion = bf16[2,4096,128]{2,1,0:T(8,128)(2,1)S(1)} fusion(bf16[2,128,1024]{2,1,0:T(8,128)(2,1)S(1)} %copy-done.2, bf16[1024,4096]{0,1:T(8,128)(2,1)} %all-gather.4.cloned.1.call-done), kind=kOutput, calls=%fused_computation.31 | convolution fusion | flops 2152726528 | bytes 11010048 | tf_op jit(solution)/shard_map/hpd,dc->hcp/dot_general | solution.py:59
  112.2 19.8 %all_to_all.54 = bf16[8,4,64,128]{3,2,1,0:T(8,128)(2,1)} all-to-all(bf16[8,4,64,128]{3,2,1,0:T(8,128)(2,1)S(1)} %bitcast.105), channel_id=1, replica_groups=mesh['seq'=8,'batch'=4] {'seq'}, dimensions={0} | all-to-all | bytes 1048576 | tf_op jit(solution)/shard_map/all_to_all | solution.py:73
  132.1 18.4 %all_to_all.55 = bf16[8,4,64,128]{3,2,1,0:T(8,128)(2,1)} all-to-all(bf16[8,4,64,128]{3,2,1,0:T(8,128)(2,1)S(1)} %bitcast.104), channel_id=1, replica_groups=mesh['seq'=8,'batch'=4] {'seq'}, dimensions={0} | all-to-all | bytes 1048576 | tf_op jit(solution)/shard_map/all_to_all | solution.py:80
  150.5 3.5 all-to-all-start.2
  157.3 2.2 copy.49
  160.8 8.5 %all-to-all-done.2 = bf16[8,4,64,128]{3,2,1,0:T(8,128)(2,1)S(1)} async-done(((bf16[8,4,64,128]{3,2,1,0:T(8,128)(2,1)}), bf16[8,4,64,128]{3,2,1,0:T(8,128)(2,1)S(1)}, u32[]{:S(2)}, u32[]{:S(2)}) %all-to-all-start.2) | async-done | bytes 524320 | tf_op jit(solution)/shard_map/all_to_all | solution.py:83
  170.4 2.1 squeeze.25
  172.5 20.0 %while.33 = (s32[]{:T(128)}, bf16[4,64,1024]{2,1,0:T(8,128)(2,1)}, bf16[4,64,1024]{2,1,0:T(8,128)(2,1)}, s32[4,1024]{1,0:T(4,128)S(1)}, bf16[4,64,1024]{2,1,0:T(...) while((s32[]{:T(128)}, bf16[4,64,1024]{2,1,0:T(8,128)(2,1)}, ...), condition=%wide.region_7.8_spmd, body=%wide.region_2.7_spmd.sunk | while | flops 69501968 | bytes 2187537 | solution.py:91
  174.4 2.4 while.34
  179.4 2.4 while.34
  184.4 2.4 while.34
  189.4 2.4 while.34
  195.5 3.3 reshape.152
  198.8 3.5 all-to-all-start.3
  203.4 14.2 %all-to-all-done.3 = bf16[8,2,16384]{2,1,0:T(2,128)(2,1)S(1)} async-done(((bf16[8,2,16384]{2,1,0:T(2,128)(2,1)}), bf16[8,2,16384]{2,1,0:T(2,128)(2,1)S(1)}, u32[]{:S(2)}, u32[]{:S(2)}) %all-to-all-start.3) | async-done | bytes 524320 | tf_op jit(solution)/shard_map/all_to_all | solution.py:95
  219.2 1.7 copy.52
  221.3 2.8 fusion.29
  224.0 3.9 %gather_fusion.1 = bf16[128,1024]{1,0:T(8,128)(2,1)S(1)} fusion(bf16[2,128,1024]{2,1,0:T(8,128)(2,1)} %fusion.29, s32[128]{0:T(128)S(1)} %reshape.134), kind=kCustom, calls=%fused_computation.1 | custom fusion | bytes 525312 | tf_op jit(solution)/shard_map/gather | solution.py:106
  229.0 7.7 %all-gather = bf16[4,1,128]{2,1,0:T(2,128)(2,1)S(1)} all-gather(bf16[1,1,128]{2,1,0:T(2,128)(2,1)S(1)} %bitcast.111), channel_id=1, replica_groups=mesh['seq'=8,'batch'=4] {'batch'}, dimensions={0}, use_global_device_ids=true | all-gather | bytes 1280 | tf_op jit(solution)/shard_map/all_gather | solution.py:113
  236.7 52.6 %all-reduce.3.cloned.1.call-done = bf16[64,2,1024]{2,0,1:T(8,128)(2,1)} async-done(((bf16[64,2,1024]{2,0,1:T(8,128)(2,1)}), bf16[64,2,1024]{2,0,1:T(8,128)(2,1)}) %all-reduce.3.cloned.1.call-update) | async-done | bytes 262160 | tf_op jit(solution)/shard_map/psum | solution.py:108
  289.3 3.2 fusion.39
  292.6 55.3 %all-reduce.5.cloned.1.call-done = f32[64,2,1024]{2,0,1:T(8,128)} async-done(((f32[64,2,1024]{2,0,1:T(8,128)}), f32[64,2,1024]{2,0,1:T(8,128)}) %all-reduce.5.cloned.1.call-update) | async-done | bytes 524304 | tf_op jit(solution)/shard_map/psum | solution.py:121
  (138 shorter events, 43.9 us)
Async XLA Ops:
  7.2 214.1 %copy-start = (bf16[1024,1024]{1,0:T(8,128)(2,1)S(1)}, bf16[1024,1024]{1,0:T(8,128)(2,1)}, u32[]{:S(2)}) copy-start(bf16[1024,1024]{1,0:T(8,128)(2,1)} %param.16) | copy-start | bytes 6291460
  7.2 94.7 %copy-start.2 = (bf16[2,128,1024]{2,1,0:T(8,128)(2,1)S(1)}, bf16[2,128,1024]{2,1,0:T(8,128)(2,1)}, u32[]{:S(2)}) copy-start(bf16[2,128,1024]{2,1,0:T(8,128)(2,1)} %param.14) | copy-start | bytes 1572868
  7.2 94.6 %all-gather.4.cloned.1.call-start = ((), (), s32[]{:S(2)}) async-start(), calls=%async_computation.4 | async-start | bytes 10485760 | tf_op jit(solution)/shard_map/all_gather | solution.py:62
  110.0 1.3 copy-start.1
  111.3 42.7 %copy-start.3 = (s32[2,8]{1,0:T(2,128)S(1)}, s32[2,8]{1,0:T(2,128)}, u32[]{:S(2)}) copy-start(s32[2,8]{1,0:T(2,128)} %param.19) | copy-start | bytes 196
  150.5 18.8 %all-to-all-start.2 = ((bf16[8,4,64,128]{3,2,1,0:T(8,128)(2,1)}), bf16[8,4,64,128]{3,2,1,0:T(8,128)(2,1)S(1)}, u32[]{:S(2)}, u32[]{:S(2)}) async-start(bf16[8,4,64,128]{3,2,1,0:T(8,128)(2,1)} %bitcast.14), calls=%async_computation.2 | async-start | bytes 1048576 | tf_op jit(solution)/shard_map/all_to_all | solution.py:83
  192.5 10.6 %copy-start.4 = (s32[64,2]{0,1:T(2,128)S(1)}, s32[64,2]{0,1:T(2,128)}, u32[]{:S(2)}) copy-start(s32[64,2]{0,1:T(2,128)} %param.20) | copy-start | bytes 1540
  198.8 18.8 %all-to-all-start.3 = ((bf16[8,2,16384]{2,1,0:T(2,128)(2,1)}), bf16[8,2,16384]{2,1,0:T(2,128)(2,1)S(1)}, u32[]{:S(2)}, u32[]{:S(2)}) async-start(bf16[8,2,16384]{2,1,0:T(2,128)(2,1)} %reshape.152), calls=%async_computation.3 | async-start | bytes 1048576 | tf_op jit(solution)/shard_map/all_to_all | solution.py:95
  202.3 34.4 %all-gather.6.cloned.1.call-start = ((), (), s32[]{:S(2)}) async-start(), calls=%async_computation.6 | async-start | bytes 1310720 | tf_op jit(solution)/shard_map/all_gather | solution.py:112
  203.1 86.2 %all-reduce.3.cloned.1.call-start = ((), (), s32[]{:S(2)}) async-start(), calls=%async_computation.5 | async-start | bytes 524288 | tf_op jit(solution)/shard_map/psum | solution.py:108
  221.2 7.7 %copy-start.5 = (bf16[128]{0:T(256)(128)(2,1)S(1)}, bf16[128]{0:T(256)(128)(2,1)}, u32[]{:S(2)}) copy-start(bf16[128]{0:T(256)(128)(2,1)} %param.18) | copy-start | bytes 772
  221.3 68.1 %copy-start.6 = (s32[64,2]{0,1:T(2,128)S(1)}, s32[64,2]{0,1:T(2,128)}, u32[]{:S(2)}) copy-start(s32[64,2]{0,1:T(2,128)} %param.21) | copy-start | bytes 1540
  228.9 118.9 %all-reduce.5.cloned.1.call-start = ((), (), s32[]{:S(2)}) async-start(), calls=%async_computation.7 | async-start | bytes 1048576 | tf_op jit(solution)/shard_map/psum | solution.py:121
Sparse Core Ops, SparseCore 0:
  11.5 90.2 all-gather.3
  205.0 27.0 all-gather.5
  234.4 54.8 all-reduce.2
  292.7 55.1 all-reduce.4
where the time goes:
time: 357 us; the launch traced here: 356 us
  waiting for transfers between devices  222 us (62%)
  blocking collectives  46 us (13%)
  local copies, waits for them, and re-layouts  42.5 us (12%)
  matrix products  22 us (6%)
  between operations  14 us (4%)
  starting transfers between devices  7.15 us (2%)
    all_gather x1, waiting for transfers between devices, on_device(): lax.all_gather(w_in, 'batch', axis=1, tiled=True)  90.5 us
    psum x1, waiting for transfers between devices, on_device(): summed = lax.psum(partial_grad, 'seq')  55.3 us
    psum x1, waiting for transfers between devices, on_device(): rows = lax.psum(picked.astype(jnp.bfloat16), 'seq')  52.6 us
    all_to_all x1, blocking collectives, on_device(): lax.all_to_all(group_heads(acts[:, 2 * width:3 * width]), 'seq', split_ax...  19.8 us
    all_to_all x1, blocking collectives, on_device(): lax.all_to_all(group_heads(acts[:, 3 * width:]), 'seq', split_axis=0, con...  18.4 us
    all_to_all x1, waiting for transfers between devices, on_device(): lax.all_to_all(attended[None], 'seq', split_axis=3, concat_axis=0, tiled=...  14.2 us
    unnamed x19, local copies, waits for them, and re-layouts  12.5 us
    all_to_all x1, waiting for transfers between devices, on_device(): lax.all_to_all(group_heads(acts[:, width:2 * width]), 'seq', split_axis=0...  8.52 us
  transfers between devices with their start and end apart: 6, of which 5 were waited for; matrix products, arithmetic and copies ran while one was open for 5% of the time, Pallas kernels for 0%

commit v1 on v0

v1 whole, which is shorter than its diff:
```python
import functools

import jax
import jax.numpy as jnp
from jax import lax
from jax.experimental import pallas as pl
from jax.experimental.pallas import tpu as pltpu
from jax.sharding import PartitionSpec as P

HEADS = 16
HD = 64
D = 1024
BF = jnp.bfloat16
F32 = jnp.float32
CHUNKS = (256, 256)
PAD = 16
VMEM_LIMIT = 56 * 1024 * 1024


def silu_half(half):
    return half + half * jnp.tanh(half)


def attend_kernel(blocks, split, tag_ref, seg_ref, *refs):
    events = refs[:blocks]
    weights = refs[blocks : blocks + len(split)]
    keep_ref, send_ref, acts, mask, accum = refs[blocks + len(split) :]
    hist, here, width = events[0].shape
    cols = keep_ref.shape[-1]
    flip, place, core = tag_ref[0], tag_ref[1], tag_ref[2]
    chip = 2 * here

    def positions(shape, dim, back):
        at = lax.broadcasted_iota(jnp.int32, shape, dim)
        first = (at < here).astype(jnp.int32)
        rank = first * core + (1 - first) * (1 - core)
        return (place - back) * chip + rank * here + at - (1 - first) * here

    for h in range(hist):
        row = positions((chip, 1), 0, 0)
        start = jnp.zeros((chip, 1), jnp.int32)
        end = jnp.int32(0)
        for k in range(seg_ref.shape[1]):
            end = end + seg_ref[h, k]
            start = start + jnp.where(row >= end, seg_ref[h, k], 0)
        for back in range(blocks // 2):
            col = positions((1, chip), 1, back)
            allowed = (col <= row) & (col >= start)
            mask[h, back] = jnp.where(allowed, 1.0, 0.0).astype(F32)

    def project(slot, block):
        rows = events[block][...].reshape(hist * here, width)
        total, base = None, 0
        for ref, owner in zip(weights, split):
            if owner == slot:
                depth = ref.shape[0]
                part = jnp.dot(rows[:, base : base + depth], ref[...], preferred_element_type=F32)
                total = part if total is None else total + part
                base += depth
        acts[slot, block] = silu_half(0.5 * total).astype(BF).reshape(hist, here, cols)

    for slot in range(4):
        for block in range(2):
            project(slot, block)

        @pl.when(((flip ^ slot) & 1) == 1)
        def _(slot=slot):
            for block in range(2, blocks):
                project(slot, block)

    gate, value, query, key = flip, flip ^ 1, flip ^ 2, flip ^ 3
    keep_ref[1] = acts[gate, 0]
    send_ref[1] = acts[gate, 1]
    lane = lax.broadcasted_iota(jnp.int32, (1, 128), 1)
    low = (lane < HD).astype(BF)
    high = 1 - low
    for h in range(hist):
        accum[...] = jnp.zeros_like(accum)
        first_row = place * chip
        first_start, end = jnp.int32(0), jnp.int32(0)
        for k in range(seg_ref.shape[1]):
            end = end + seg_ref[h, k]
            first_start = first_start + jnp.where(first_row >= end, seg_ref[h, k], 0)
        for back in range(blocks // 2):

            @pl.when(first_start < (place - back + 1) * chip)
            def _(h=h, back=back):
                allowed = mask[h, back]
                for pair in range(cols // 128):
                    at = slice(pair * 128, pair * 128 + 128)
                    q = jnp.concatenate([acts[query, 0, h, :, at], acts[query, 1, h, :, at]], 0)
                    k = jnp.concatenate(
                        [acts[key, 2 * back, h, :, at], acts[key, 2 * back + 1, h, :, at]], 0
                    )
                    v = jnp.concatenate(
                        [acts[value, 2 * back, h, :, at], acts[value, 2 * back + 1, h, :, at]], 0
                    )
                    q = q * jnp.asarray(0.5, BF)
                    total = accum[:, at]
                    for lanes in (low, high):
                        half = lax.dot_general(
                            q * lanes, k, (((1,), (1,)), ((), ())), preferred_element_type=F32
                        )
                        w = silu_half(half * allowed).astype(BF)
                        total = total + jnp.dot(w, v * lanes, preferred_element_type=F32)
                    accum[:, at] = total

        keep_ref[0, h] = accum[:here].astype(BF)
        send_ref[0, h] = accum[here:].astype(BF)


def attend(tag, lengths, events, weights, split, cols):
    hist, here, width = events[0].shape
    blocks = len(events)
    part = jax.ShapeDtypeStruct((2, hist, here, cols), BF)
    vmem = pl.BlockSpec(memory_space=pltpu.VMEM)
    smem = pl.BlockSpec(memory_space=pltpu.SMEM)
    flops = 2 * hist * here * width * cols * (2 * blocks + 4) + 8 * hist * 2 * here * here * blocks * cols
    return pl.pallas_call(
        functools.partial(attend_kernel, blocks, split),
        out_shape=(part, part),
        in_specs=[smem, smem] + [vmem] * (blocks + len(weights)),
        out_specs=(vmem, vmem),
        scratch_shapes=[
            pltpu.VMEM((4, blocks, hist, here, cols), BF),
            pltpu.VMEM((hist, blocks // 2, 2 * here, 2 * here), F32),
            pltpu.VMEM((2 * here, cols), F32),
        ],
        compiler_params=pltpu.CompilerParams(vmem_limit_bytes=VMEM_LIMIT),
        cost_estimate=pl.CostEstimate(
            flops=flops, bytes_accessed=4 * 1024 * 1024, transcendentals=hist * here * 2 * here * blocks * cols // HD
        ),
        name="attend",
    )(tag, lengths, *events, *weights)


def finish_kernel(count, tag_ref, listed_ref, events_ref, w_out_ref, *refs):
    parts = refs[: 2 * count]
    layer_ref, keep_ref, send_ref = refs[2 * count :]
    hist, here, width = events_ref.shape
    rows = hist * here
    core = tag_ref[2]
    pieces, gates, offsets = [], [], []
    for side in range(2):
        base = (core ^ side) * (width // 2)
        for ref in parts[side * count : (side + 1) * count]:
            cols = ref.shape[-1]
            pieces.append(ref[0].reshape(rows, cols).astype(F32))
            gates.append(ref[1].reshape(rows, cols).astype(F32))
            offsets.append(pl.multiple_of(base, 128))
            base = base + cols
    mean = sum(jnp.sum(p, axis=1, keepdims=True) for p in pieces) * (1.0 / width)
    pieces = [p - mean for p in pieces]
    spread = sum(jnp.sum(p * p, axis=1, keepdims=True) for p in pieces) * (1.0 / width)
    inverse = lax.rsqrt(spread + 1e-05)
    output = events_ref[...].reshape(rows, width).astype(F32)
    for p, g, at in zip(pieces, gates, offsets):
        mixed = (p * inverse * g).astype(BF)
        output = output + jnp.dot(
            mixed, w_out_ref[pl.ds(at, p.shape[1]), :], preferred_element_type=F32
        )
    layer = output.astype(BF)
    layer_ref[...] = layer.reshape(hist, here, width)
    column = lax.broadcasted_iota(jnp.int32, (1, rows), 1)
    for side, out_ref in ((0, keep_ref), (1, send_ref)):
        pick = (listed_ref[side] == column).astype(BF)
        out_ref[...] = jnp.dot(pick, layer, preferred_element_type=F32).astype(BF)


def finish(tag, listed, events, w_out, keeps, received):
    hist, here, width = events.shape
    rows = listed.shape[1]
    vmem = pl.BlockSpec(memory_space=pltpu.VMEM)
    smem = pl.BlockSpec(memory_space=pltpu.SMEM)
    return pl.pallas_call(
        functools.partial(finish_kernel, len(keeps)),
        out_shape=(
            jax.ShapeDtypeStruct((hist, here, width), BF),
            jax.ShapeDtypeStruct((rows, width), BF),
            jax.ShapeDtypeStruct((rows, width), BF),
        ),
        in_specs=[smem] + [vmem] * (3 + len(keeps) + len(received)),
        out_specs=(vmem, vmem, vmem),
        compiler_params=pltpu.CompilerParams(vmem_limit_bytes=VMEM_LIMIT),
        cost_estimate=pl.CostEstimate(
            flops=2 * hist * here * width * width, bytes_accessed=5 * 1024 * 1024, transcendentals=0
        ),
        name="finish",
    )(tag, listed, events, w_out, *keeps, *received)


def score_kernel(sources, tag_ref, base_ref, rows_ref, label_ref, *refs):
    tables = refs[:sources]
    outs = refs[sources:-2]
    total, shares = refs[-2:]
    rows = rows_ref[...]
    label = label_ref[...]
    scale = D ** (-0.5)
    total[...] = jnp.zeros_like(total)
    which = 0
    for ref in tables:
        per = ref.shape[0]
        items = ref.shape[1] - PAD

        def one(i, which=which, ref=ref, items=items):
            table = ref[i, :items, :]
            bias = ref[i, items : items + 1, :items].astype(F32)
            logits = lax.dot_general(
                rows, table, (((1,), (1,)), ((), ())), preferred_element_type=F32
            )
            logits = logits * scale + bias
            ids = base_ref[which + i] + lax.broadcasted_iota(jnp.int32, (1, items), 1)
            target = (label == ids).astype(F32)
            coef = (1.0 / (1.0 + jnp.exp(-logits)) - target).astype(BF)
            total[...] += jnp.dot(coef, table, preferred_element_type=F32)

        if per <= 4:
            for i in range(per):
                one(i)
        else:
            pl.loop(0, per)(one)
        which += per
    count = len(outs)
    share = outs[0].shape[0]
    for chip in range(count):
        shares[chip] = total[chip * share : (chip + 1) * share, :]
    for step, out in enumerate(outs):
        out[...] = shares[lax.rem(tag_ref[1] + step, count)]


def score(tag, bases, rows, labels, tables, chips):
    count, width = rows.shape
    vmem = pl.BlockSpec(memory_space=pltpu.VMEM)
    smem = pl.BlockSpec(memory_space=pltpu.SMEM)
    part = jax.ShapeDtypeStruct((count // chips, width), F32)
    return pl.pallas_call(
        functools.partial(score_kernel, len(tables)),
        out_shape=(part,) * chips,
        in_specs=[smem, smem] + [vmem] * (2 + len(tables)),
        out_specs=(vmem,) * chips,
        scratch_shapes=[
            pltpu.VMEM((count, width), F32),
            pltpu.VMEM((chips, count // chips, width), F32),
        ],
        compiler_params=pltpu.CompilerParams(vmem_limit_bytes=VMEM_LIMIT),
        cost_estimate=pl.CostEstimate(
            flops=4 * count * width * 1024, bytes_accessed=3 * 1024 * 1024, transcendentals=count * 1024
        ),
        name="score",
    )(tag, bases, rows, labels, *tables)


def on_device(events, w_in, w_out, item_table, item_bias, segment_lengths, listed_pos, labels):
    hist, here, width = events.shape
    seq = lax.axis_size("seq")
    batch = lax.axis_size("batch")
    chips = seq // 2
    rank = lax.axis_index("seq").astype(jnp.int32)
    mine = lax.axis_index("batch").astype(jnp.int32)
    place, core = rank // 2, rank % 2
    grid = batch == 4

    def swap(value):
        return lax.ppermute(value, "seq", [(i, i ^ 1) for i in range(seq)])

    def across(value, bit):
        return lax.ppermute(value, "batch", [(i, i ^ bit) for i in range(batch)])

    def ahead(value, by):
        return lax.ppermute(value, "seq", [(i, i + 2 * by) for i in range(seq - 2 * by)])

    half = width // 2
    chunks = []
    if grid:
        offset = core * half
        for cols in CHUNKS:
            own = lax.dynamic_slice_in_dim(w_in, offset, cols, 1)
            over_x, over_y = across(own, 1), across(own, 2)
            top = across(over_y[: width // 2], 1)
            bottom = across(over_x[width // 2 :], 2)
            chunks.append(([own, over_x, over_y, top, bottom], (0, 1, 2, 3, 3)))
            offset = offset + cols
        flip = mine
    else:
        whole = lax.all_gather(w_in, "batch", axis=1, tiled=True)
        offset = core * half
        for cols in CHUNKS:
            chunks.append(
                (
                    [
                        lax.dynamic_slice_in_dim(whole, group * width + offset, cols, 1)
                        for group in range(4)
                    ],
                    (0, 1, 2, 3),
                )
            )
            offset = offset + cols
        flip = jnp.int32(0)

    longest = seq * here // 2
    reach = min(chips - 1, -(-(longest - 1) // (2 * here)))
    blocks = [events, swap(events)]
    for back in range(1, reach + 1):
        earlier = ahead(events, back)
        blocks += [earlier, swap(earlier)]

    tag = jnp.stack([flip, place, core])
    keeps, received = [], []
    for (weights, split), cols in zip(chunks, CHUNKS):
        keep, send = attend(tag, segment_lengths, blocks, weights, split, cols)
        keeps.append(keep)
        received.append(swap(send))

    share = listed_pos.shape[0] // seq
    local = listed_pos - rank * here
    inside = (local >= 0) & (local < here)
    index = jnp.where(inside, local + here * jnp.arange(hist, dtype=jnp.int32)[None, :], -1)

    def halves(value):
        value = value.reshape(chips, 2, share, hist).transpose(1, 0, 2, 3)
        return value.reshape(2, chips * share * hist, 1)

    index = halves(index)
    index = jnp.where(core == 0, index, index[::-1])
    own_labels = halves(labels)
    own_labels = jnp.where(core == 0, own_labels[0], own_labels[1])
    layer_out, rows, rows_send = finish(tag, index, events, w_out, keeps, received)
    rows = rows + swap(rows_send)
    step = 1
    while step < chips:
        rows = rows + lax.ppermute(rows, "seq", [(i, i ^ (2 * step)) for i in range(seq)])
        step *= 2

    items = item_table.shape[0]
    padded = jnp.concatenate(
        [
            item_table,
            jnp.pad(item_bias[None, :], ((0, PAD - 1), (0, width - items))),
        ],
        0,
    )
    if grid:
        over_x = across(padded, 1)
        over_y = across(padded, 2)
        corner = across(padded, 3)
        table = jnp.stack([padded, over_x, over_y, corner])
        holder = mine ^ jnp.arange(4, dtype=jnp.int32)
    else:
        table = lax.all_gather(padded[None], "batch", axis=0, tiled=True)
        holder = jnp.arange(batch, dtype=jnp.int32)
    other_table = swap(table)
    bases = jnp.concatenate(
        [(rank * batch + holder) * items, ((rank ^ 1) * batch + holder) * items]
    )
    parts = score(tag, bases, rows, own_labels, (table, other_table), chips)
    total = parts[0]
    for step in range(1, chips):
        total = total + lax.ppermute(
            parts[step], "seq", [(i, (i + 2 * step) % seq) for i in range(seq)]
        )
    return layer_out, total.reshape(share, hist, width)


def solution(mesh):
    return jax.shard_map(
        on_device,
        mesh=mesh,
        in_specs=(
            P("batch", "seq", None),
            P(None, "batch"),
            P(),
            P(("seq", "batch"), None),
            P(("seq", "batch")),
            P("batch", None),
            P(None, "batch"),
            P(None, "batch"),
        ),
        out_specs=(P("batch", "seq", None), P("seq", "batch", None)),
        check_vma=False,
    )
```

time: 357 us -> 133 us (0.37)
  waiting for transfers between devices: 222 us -> 40.7 us
  blocking collectives: 46 us -> 0 us
  starting transfers between devices: 7.15 us -> 52.9 us
  local copies, waits for them, and re-layouts: 42.5 us -> 7.84 us
  Pallas kernels: 0 us -> 25.4 us
  matrix products: 22 us -> 0 us
  between operations: 14 us -> 0.9 us
  other arithmetic: 1.46 us -> 5.8 us
    psum x2 -> x0, waiting for transfers between devices: 108 us -> none  [the longest x1 55.3 us: on_device(): summed = lax.psum(partial_grad, 'seq')]
    all_gather x2 -> x0, waiting for transfers between devices: 90.5 us -> none  [the longest x1 90.5 us: on_device(): lax.all_gather(w_in, 'batch', axis=1, tiled=True)]
    ppermute x0 -> x25, starting transfers between devices: none -> 52.9 us  [the longest x2 20.3 us: on_device(): lax.ppermute(rows, 'seq', [(i, i ^ 2 * step) for i in range(seq)])]
    ppermute x0 -> x25, waiting for transfers between devices: none -> 40.7 us  [the longest x11 19 us: across(): return lax.ppermute(value, 'batch', [(i, i ^ bit) for i in range(batch)])]
    all_to_all x2 -> x0, blocking collectives: 38.3 us -> none  [the longest x1 19.8 us: on_device(): lax.all_to_all(group_heads(acts[:, 2 * width:3 * width]), 'seq', split_ax...]
    pallas_call x0 -> x4, Pallas kernels: none -> 25.4 us  [the longest x2 17.5 us: attend(): pl.pallas_call(functools.partial(attend_kernel, blocks, split), out_shape...]
    all_to_all x2 -> x0, waiting for transfers between devices: 22.7 us -> none  [the longest x1 14.2 us: on_device(): lax.all_to_all(attended[None], 'seq', split_axis=3, concat_axis=0, tiled=...]
    dot_general x15 -> x0, matrix products: 22 us -> none  [the longest x1 8.13 us: on_device(): jnp.einsum('hpd,dc->hcp', events, lax.all_gather(w_in, 'batch', axis=1, t...]
  transfers between devices with their start and end apart: 6 -> 25, of which waited for: 5 -> 12; matrix products, arithmetic and copies ran while one was open for 5% -> 6% of each run, Pallas kernels for 0% -> 16%
where the time goes in v1:
time: 133 us; the launch traced here: 134 us
  starting transfers between devices  52.9 us (40%)
  waiting for transfers between devices  40.7 us (31%)
  Pallas kernels  25.4 us (19%)
  local copies, waits for them, and re-layouts  7.84 us (6%)
  other arithmetic  5.8 us (4%)
    ppermute x2, starting transfers between devices, on_device(): lax.ppermute(rows, 'seq', [(i, i ^ 2 * step) for i in range(seq)])  20.3 us
    ppermute x11, waiting for transfers between devices, across(): return lax.ppermute(value, 'batch', [(i, i ^ bit) for i in range(batch)])  19 us
    pallas_call x2, Pallas kernels, attend(): pl.pallas_call(functools.partial(attend_kernel, blocks, split), out_shape...  17.5 us
    ppermute x11, starting transfers between devices, across(): return lax.ppermute(value, 'batch', [(i, i ^ bit) for i in range(batch)])  17.2 us
    ppermute x2, starting transfers between devices, ahead(): lax.ppermute(value, 'seq', [(i, i + 2 * by) for i in range(seq - 2 * by)])  9.79 us
    ppermute x2, waiting for transfers between devices, on_device(): lax.ppermute(rows, 'seq', [(i, i ^ 2 * step) for i in range(seq)])  8.87 us
    ppermute x2, waiting for transfers between devices, ahead(): lax.ppermute(value, 'seq', [(i, i + 2 * by) for i in range(seq - 2 * by)])  5.99 us
    ppermute x3, waiting for transfers between devices, on_device(): lax.ppermute(parts[step], 'seq', [(i, (i + 2 * step) % seq) for i in rang...  5.32 us
  transfers between devices with their start and end apart: 25, of which 12 were waited for; matrix products, arithmetic and copies ran while one was open for 6% of the time, Pallas kernels for 16%

profile of v1, /device:TPU:0, one launch (start us, length us, event | category | flops | bytes accessed | tf_op | source)
XLA Modules:
  0.0 133.5 jit_solution(17622093013788679571)
XLA Ops:
  2.1 3.0 %collective-permute-start.10 = (bf16[1024,256]{1,0:T(8,128)(2,1)S(1)}, bf16[1024,256]{1,0:T(8,128)(2,1)S(1)}, u32[]{:S(2)}, u32[]{:S(2)}) collective-permute-start(bf16[1024,256]{1,0:T(8,128)(2,1)S(1)} %get-tuple-element.24.refs_6_), channel_id=1, source_target_pairs={{0,2},{1,3},{2,0},{3,1},{4,6},{5,7},{6,4},{7,5},{8,10},{9,11},{10,... | collective-permute-start | bytes 1572872 | tf_op jit(solution)/shard_map/ppermute | solution.py:267
  5.2 1.6 %collective-permute-start.18 = (bf16[144,1024]{1,0:T(8,128)(2,1)S(1)}, bf16[144,1024]{1,0:T(8,128)(2,1)S(1)}, u32[]{:S(2)}, u32[]{:S(2)}) collective-permute-start(bf16[144,1024]{1,0:T(8,128)(2,1)S(1)} %get-tuple-element.27), channel_id=1, source_target_pairs={{0,1},{1,0},{2,3},{3,2},{4,5},{5,4},{6,7},{7,6},{8,9},{9,8},{10,11... | collective-permute-start | bytes 884744 | tf_op jit(solution)/shard_map/ppermute | solution.py:267
  8.7 1.5 %collective-permute-start.9 = (bf16[1024,256]{1,0:T(8,128)(2,1)S(1)}, bf16[1024,256]{1,0:T(8,128)(2,1)S(1)}, u32[]{:S(2)}, u32[]{:S(2)}) collective-permute-start(bf16[1024,256]{1,0:T(8,128)(2,1)S(1)} %get-tuple-element.24.refs_6_), channel_id=1, source_target_pairs={{0,1},{1,0},{2,3},{3,2},{4,5},{5,4},{6,7},{7,6},{8,9},{9,8},{10,11... | collective-permute-start | bytes 1572872 | tf_op jit(solution)/shard_map/ppermute | solution.py:267
  10.2 5.0 %collective-permute-done.18 = bf16[144,1024]{1,0:T(8,128)(2,1)S(1)} collective-permute-done((bf16[144,1024]{1,0:T(8,128)(2,1)S(1)}, bf16[144,1024]{1,0:T(8,128)(2,1)S(1)}, u32[]{:S(2)}, u32[]{:S(2)}) %collective-permute-start.18) | collective-permute-done | bytes 294944 | tf_op jit(solution)/shard_map/ppermute | solution.py:267
  15.2 4.3 %collective-permute-start.1 = (bf16[2,128,1024]{2,1,0:T(8,128)(2,1)S(1)}, bf16[2,128,1024]{2,1,0:T(8,128)(2,1)}, u32[]{:S(2)}, u32[]{:S(2)}) collective-permute-start(bf16[2,128,1024]{2,1,0:T(8,128)(2,1)S(1)} %copy-done.2), channel_id=1, source_target_pairs={{0,8},{4,12},{8,16},{12,20},{16,24},{20,28},{1,9},{5,13},{9,17},{1... | collective-permute-start | bytes 1572872 | tf_op jit(solution)/shard_map/ppermute | solution.py:270
  19.4 10.2 %collective-permute-done.19 = bf16[144,1024]{1,0:T(8,128)(2,1)S(1)} collective-permute-done((bf16[144,1024]{1,0:T(8,128)(2,1)S(1)}, bf16[144,1024]{1,0:T(8,128)(2,1)S(1)}, u32[]{:S(2)}, u32[]{:S(2)}) %collective-permute-start.19) | collective-permute-done | bytes 294944 | tf_op jit(solution)/shard_map/ppermute | solution.py:267
  29.7 5.5 %collective-permute-start.3 = (bf16[2,128,1024]{2,1,0:T(8,128)(2,1)S(1)}, bf16[2,128,1024]{2,1,0:T(8,128)(2,1)}, u32[]{:S(2)}, u32[]{:S(2)}) collective-permute-start(bf16[2,128,1024]{2,1,0:T(8,128)(2,1)S(1)} %copy-done.2), channel_id=1, source_target_pairs={{0,16},{4,20},{8,24},{12,28},{1,17},{5,21},{9,25},{13,29},{2,18},{... | collective-permute-start | bytes 1572872 | tf_op jit(solution)/shard_map/ppermute | solution.py:270
  35.2 1.5 %collective-permute-start.6 = (bf16[1024,256]{1,0:T(8,128)(2,1)S(1)}, bf16[1024,256]{1,0:T(8,128)(2,1)S(1)}, u32[]{:S(2)}, u32[]{:S(2)}) collective-permute-start(bf16[1024,256]{1,0:T(8,128)(2,1)S(1)} %get-tuple-element.25.refs_6_), channel_id=1, source_target_pairs={{0,2},{1,3},{2,0},{3,1},{4,6},{5,7},{6,4},{7,5},{8,10},{9,11},{10,... | collective-permute-start | bytes 1572872 | tf_op jit(solution)/shard_map/ppermute | solution.py:267
  38.7 6.0 %collective-permute-done.3.refs_4_ = bf16[2,128,1024]{2,1,0:T(8,128)(2,1)} collective-permute-done((bf16[2,128,1024]{2,1,0:T(8,128)(2,1)S(1)}, bf16[2,128,1024]{2,1,0:T(8,128)(2,1)}, u32[]{:S(2)}, u32[]{:S(2)}) %collective-permute-start.3) | collective-permute-done | bytes 524320 | tf_op jit(solution)/shard_map/ppermute | solution.py:270
  46.1 1.6 %collective-permute-done.6.refs_8_ = bf16[1024,256]{1,0:T(8,128)(2,1)S(1)} collective-permute-done((bf16[1024,256]{1,0:T(8,128)(2,1)S(1)}, bf16[1024,256]{1,0:T(8,128)(2,1)S(1)}, u32[]{:S(2)}, u32[]{:S(2)}) %collective-permute-start.6) | collective-permute-done | bytes 524320 | tf_op jit(solution)/shard_map/ppermute | solution.py:267
  49.2 1.6 %collective-permute-start.12 = (bf16[512,256]{1,0:T(8,128)(2,1)}, bf16[512,256]{1,0:T(8,128)(2,1)}, u32[]{:S(2)}, u32[]{:S(2)}) collective-permute-start(bf16[512,256]{1,0:T(8,128)(2,1)} %slice.29), channel_id=1, source_target_pairs={{0,2},{1,3},{2,0},{3,1},{4,6},{5,7},{6,4},{7,5},{8,10},{9,11},{10,... | collective-permute-start | bytes 786440 | tf_op jit(solution)/shard_map/ppermute | solution.py:267
  52.9 2.3 %collective-permute-done.11.refs_9_ = bf16[512,256]{1,0:T(8,128)(2,1)} collective-permute-done((bf16[512,256]{1,0:T(8,128)(2,1)}, bf16[512,256]{1,0:T(8,128)(2,1)}, u32[]{:S(2)}, u32[]{:S(2)}) %collective-permute-start.11) | collective-permute-done | bytes 262176 | tf_op jit(solution)/shard_map/ppermute | solution.py:267
  56.7 1.5 %collective-permute-start.8 = (bf16[512,256]{1,0:T(8,128)(2,1)S(1)}, bf16[512,256]{1,0:T(8,128)(2,1)S(1)}, u32[]{:S(2)}, u32[]{:S(2)}) collective-permute-start(bf16[512,256]{1,0:T(8,128)(2,1)S(1)} %slice.27), channel_id=1, source_target_pairs={{0,2},{1,3},{2,0},{3,1},{4,6},{5,7},{6,4},{7,5},{8,10},{9,11},{10,... | collective-permute-start | bytes 786440 | tf_op jit(solution)/shard_map/ppermute | solution.py:267
  58.2 8.6 %attend.3 = (bf16[2,2,128,256]{3,2,1,0:T(8,128)(2,1)}, bf16[2,2,128,256]{3,2,1,0:T(8,128)(2,1)}) custom-call(s32[3]{0:T(128)} %pad_add_fusion.tag_ref, s32[2,8]{1,0:T(2,128)} %seg_ref.3, bf16[2,128,1024]{2,1,0:T(8,128)(2,1)} %events_ref.1, bf16[2,128,1024]{2,1,0:T(8,128)(2,1)} %collective-permute-done.refs_1_, ...), custom_call_target="tpu_custom_call" | custom-call | flops 2952790016 | bytes 4194304 | tf_op jit(solution)/shard_map/attend/pallas_call | solution.py:119
  68.3 8.8 %attend.2 = (bf16[2,2,128,256]{3,2,1,0:T(8,128)(2,1)}, bf16[2,2,128,256]{3,2,1,0:T(8,128)(2,1)}) custom-call(s32[3]{0:T(128)} %pad_add_fusion.tag_ref, s32[2,8]{1,0:T(2,128)} %seg_ref.3, bf16[2,128,1024]{2,1,0:T(8,128)(2,1)} %events_ref.1, bf16[2,128,1024]{2,1,0:T(8,128)(2,1)} %collective-permute-done.refs_1_, ...), custom_call_target="tpu_custom_call" | custom-call | flops 2952790016 | bytes 4194304 | tf_op jit(solution)/shard_map/attend/pallas_call | solution.py:119
  79.8 3.9 %finish.1 = (bf16[2,128,1024]{2,1,0:T(8,128)(2,1)}, bf16[64,1024]{1,0:T(8,128)(2,1)}, bf16[64,1024]{1,0:T(8,128)(2,1)}) custom-call(s32[3]{0:T(128)} %pad_add_fusion.tag_ref, s32[2,64,1]{2,1,0:T(8,128)} %reverse_select_fusion.listed_ref, bf16[2,128,1024]{2,1,0:T(8,128)(2,1)} %events_ref.1, bf16[1024,1024]{1,0:T(8,128)(2,1)} %w_out_ref.1, ...), custom_call_target="tpu_custom_call" | custom-call | flops 536870912 | bytes 5242880 | tf_op jit(solution)/shard_map/finish/pallas_call | solution.py:175
  86.2 15.4 %collective-permute-start.16 = (bf16[64,1024]{1,0:T(8,128)(2,1)S(1)}, bf16[64,1024]{1,0:T(8,128)(2,1)S(1)}, u32[]{:S(2)}, u32[]{:S(2)}) collective-permute-start(bf16[64,1024]{1,0:T(8,128)(2,1)S(1)} %add.66), channel_id=1, source_target_pairs={{0,8},{4,12},{8,0},{12,4},{16,24},{20,28},{24,16},{28,20},{1,9},{5... | collective-permute-start | bytes 393224 | tf_op jit(solution)/shard_map/ppermute | solution.py:331
  101.6 4.0 %collective-permute-done.16 = bf16[64,1024]{1,0:T(8,128)(2,1)S(1)} collective-permute-done((bf16[64,1024]{1,0:T(8,128)(2,1)S(1)}, bf16[64,1024]{1,0:T(8,128)(2,1)S(1)}, u32[]{:S(2)}, u32[]{:S(2)}) %collective-permute-start.16) | collective-permute-done | bytes 131104 | tf_op jit(solution)/shard_map/ppermute | solution.py:331
  105.7 4.9 %collective-permute-start.17 = (bf16[64,1024]{1,0:T(8,128)(2,1)S(1)}, bf16[64,1024]{1,0:T(8,128)(2,1)S(1)}, u32[]{:S(2)}, u32[]{:S(2)}) collective-permute-start(bf16[64,1024]{1,0:T(8,128)(2,1)S(1)} %add.67), channel_id=1, source_target_pairs={{0,16},{4,20},{8,24},{12,28},{16,0},{20,4},{24,8},{28,12},{1,17},{... | collective-permute-start | bytes 393224 | tf_op jit(solution)/shard_map/ppermute | solution.py:331
  112.0 4.9 %collective-permute-done.17 = bf16[64,1024]{1,0:T(8,128)(2,1)S(1)} collective-permute-done((bf16[64,1024]{1,0:T(8,128)(2,1)S(1)}, bf16[64,1024]{1,0:T(8,128)(2,1)S(1)}, u32[]{:S(2)}, u32[]{:S(2)}) %collective-permute-start.17) | collective-permute-done | bytes 131104 | tf_op jit(solution)/shard_map/ppermute | solution.py:331
  118.6 4.0 %score.1 = (f32[16,1024]{1,0:T(8,128)}, f32[16,1024]{1,0:T(8,128)}, f32[16,1024]{1,0:T(8,128)}, f32[16,1024]{1,0:T(8,128)}) custom-call(s32[3]{0:T(128)} %pad_add_fusion.tag_ref, s32[8]{0:T(128)} %pad_add_fusion.1.base_ref, bf16[64,1024]{1,0:T(8,128)(2,1)} %add.68.rows_ref, s32[64,1]{1,0:T(8,128)} %select_n.49.label_ref, bf16[4,144,1024]{2,1,0:T(8,128)(2,1)} %copy-done, ...), custom_call_target="tpu_custom_call" | custom-call | flops 268435456 | bytes 3145728 | tf_op jit(solution)/shard_map/score/pallas_call | solution.py:236
  123.3 3.4 %collective-permute-start.23 = (f32[16,1024]{1,0:T(8,128)}, f32[16,1024]{1,0:T(8,128)S(1)}, u32[]{:S(2)}, u32[]{:S(2)}) collective-permute-start(f32[16,1024]{1,0:T(8,128)} %get-tuple-element.22), channel_id=1, source_target_pairs={{0,16},{4,20},{8,24},{12,28},{16,0},{20,4},{24,8},{28,12},{1,17},{... | collective-permute-start | bytes 196616 | tf_op jit(solution)/shard_map/ppermute | solution.py:358
  126.7 3.0 %collective-permute-done.22 = f32[16,1024]{1,0:T(8,128)S(1)} collective-permute-done((f32[16,1024]{1,0:T(8,128)}, f32[16,1024]{1,0:T(8,128)S(1)}, u32[]{:S(2)}, u32[]{:S(2)}) %collective-permute-start.22) | collective-permute-done | bytes 65568 | tf_op jit(solution)/shard_map/ppermute | solution.py:358
  129.6 1.8 %collective-permute-done.23 = f32[16,1024]{1,0:T(8,128)S(1)} collective-permute-done((f32[16,1024]{1,0:T(8,128)}, f32[16,1024]{1,0:T(8,128)S(1)}, u32[]{:S(2)}, u32[]{:S(2)}) %collective-permute-start.23) | collective-permute-done | bytes 65568 | tf_op jit(solution)/shard_map/ppermute | solution.py:358
  (97 shorter events, 24.3 us)
Async XLA Ops:
  2.1 34.6 %collective-permute-start.10 = (bf16[1024,256]{1,0:T(8,128)(2,1)S(1)}, bf16[1024,256]{1,0:T(8,128)(2,1)S(1)}, u32[]{:S(2)}, u32[]{:S(2)}) collective-permute-start(bf16[1024,256]{1,0:T(8,128)(2,1)S(1)} %get-tuple-element.24.refs_6_), channel_id=1, source_target_pairs={{0,2},{1,3},{2,0},{3,1},{4,6},{5,7},{6,4},{7,5},{8,10},{9,11},{10,... | collective-permute-start | bytes 1572872 | tf_op jit(solution)/shard_map/ppermute | solution.py:267
  5.2 10.0 %collective-permute-start.18 = (bf16[144,1024]{1,0:T(8,128)(2,1)S(1)}, bf16[144,1024]{1,0:T(8,128)(2,1)S(1)}, u32[]{:S(2)}, u32[]{:S(2)}) collective-permute-start(bf16[144,1024]{1,0:T(8,128)(2,1)S(1)} %get-tuple-element.27), channel_id=1, source_target_pairs={{0,1},{1,0},{2,3},{3,2},{4,5},{5,4},{6,7},{7,6},{8,9},{9,8},{10,11... | collective-permute-start | bytes 884744 | tf_op jit(solution)/shard_map/ppermute | solution.py:267
  6.7 22.9 %collective-permute-start.19 = (bf16[144,1024]{1,0:T(8,128)(2,1)S(1)}, bf16[144,1024]{1,0:T(8,128)(2,1)S(1)}, u32[]{:S(2)}, u32[]{:S(2)}) collective-permute-start(bf16[144,1024]{1,0:T(8,128)(2,1)S(1)} %get-tuple-element.27), channel_id=1, source_target_pairs={{0,2},{1,3},{2,0},{3,1},{4,6},{5,7},{6,4},{7,5},{8,10},{9,11},{10,... | collective-permute-start | bytes 884744 | tf_op jit(solution)/shard_map/ppermute | solution.py:267
  7.2 28.0 %collective-permute-start.20 = (bf16[144,1024]{1,0:T(8,128)(2,1)S(1)}, bf16[144,1024]{1,0:T(8,128)(2,1)S(1)}, u32[]{:S(2)}, u32[]{:S(2)}) collective-permute-start(bf16[144,1024]{1,0:T(8,128)(2,1)S(1)} %get-tuple-element.27), channel_id=1, source_target_pairs={{0,3},{1,2},{2,1},{3,0},{4,7},{5,6},{6,5},{7,4},{8,11},{9,10},{10,... | collective-permute-start | bytes 884744 | tf_op jit(solution)/shard_map/ppermute | solution.py:267
  8.7 29.5 %collective-permute-start.9 = (bf16[1024,256]{1,0:T(8,128)(2,1)S(1)}, bf16[1024,256]{1,0:T(8,128)(2,1)S(1)}, u32[]{:S(2)}, u32[]{:S(2)}) collective-permute-start(bf16[1024,256]{1,0:T(8,128)(2,1)S(1)} %get-tuple-element.24.refs_6_), channel_id=1, source_target_pairs={{0,1},{1,0},{2,3},{3,2},{4,5},{5,4},{6,7},{7,6},{8,9},{9,8},{10,11... | collective-permute-start | bytes 1572872 | tf_op jit(solution)/shard_map/ppermute | solution.py:267
  15.2 23.1 %collective-permute-start.1 = (bf16[2,128,1024]{2,1,0:T(8,128)(2,1)S(1)}, bf16[2,128,1024]{2,1,0:T(8,128)(2,1)}, u32[]{:S(2)}, u32[]{:S(2)}) collective-permute-start(bf16[2,128,1024]{2,1,0:T(8,128)(2,1)S(1)} %copy-done.2), channel_id=1, source_target_pairs={{0,8},{4,12},{8,16},{12,20},{16,24},{20,28},{1,9},{5,13},{9,17},{1... | collective-permute-start | bytes 1572872 | tf_op jit(solution)/shard_map/ppermute | solution.py:270
  29.7 15.0 %collective-permute-start.3 = (bf16[2,128,1024]{2,1,0:T(8,128)(2,1)S(1)}, bf16[2,128,1024]{2,1,0:T(8,128)(2,1)}, u32[]{:S(2)}, u32[]{:S(2)}) collective-permute-start(bf16[2,128,1024]{2,1,0:T(8,128)(2,1)S(1)} %copy-done.2), channel_id=1, source_target_pairs={{0,16},{4,20},{8,24},{12,28},{1,17},{5,21},{9,25},{13,29},{2,18},{... | collective-permute-start | bytes 1572872 | tf_op jit(solution)/shard_map/ppermute | solution.py:270
  35.2 12.5 %collective-permute-start.6 = (bf16[1024,256]{1,0:T(8,128)(2,1)S(1)}, bf16[1024,256]{1,0:T(8,128)(2,1)S(1)}, u32[]{:S(2)}, u32[]{:S(2)}) collective-permute-start(bf16[1024,256]{1,0:T(8,128)(2,1)S(1)} %get-tuple-element.25.refs_6_), channel_id=1, source_target_pairs={{0,2},{1,3},{2,0},{3,1},{4,6},{5,7},{6,4},{7,5},{8,10},{9,11},{10,... | collective-permute-start | bytes 1572872 | tf_op jit(solution)/shard_map/ppermute | solution.py:267
  36.7 12.5 %collective-permute-start.5 = (bf16[1024,256]{1,0:T(8,128)(2,1)S(1)}, bf16[1024,256]{1,0:T(8,128)(2,1)S(1)}, u32[]{:S(2)}, u32[]{:S(2)}) collective-permute-start(bf16[1024,256]{1,0:T(8,128)(2,1)S(1)} %get-tuple-element.25.refs_6_), channel_id=1, source_target_pairs={{0,1},{1,0},{2,3},{3,2},{4,5},{5,4},{6,7},{7,6},{8,9},{9,8},{10,11... | collective-permute-start | bytes 1572872 | tf_op jit(solution)/shard_map/ppermute | solution.py:267
  38.2 14.6 %collective-permute-start = (bf16[2,128,1024]{2,1,0:T(8,128)(2,1)S(1)}, bf16[2,128,1024]{2,1,0:T(8,128)(2,1)}, u32[]{:S(2)}, u32[]{:S(2)}) collective-permute-start(bf16[2,128,1024]{2,1,0:T(8,128)(2,1)S(1)} %copy-done.2), channel_id=1, source_target_pairs={{0,4},{4,0},{8,12},{12,8},{16,20},{20,16},{24,28},{28,24},{1,5},{5... | collective-permute-start | bytes 1572872 | tf_op jit(solution)/shard_map/ppermute | solution.py:264
  38.2 20.0 %collective-permute-start.2 = (bf16[2,128,1024]{2,1,0:T(8,128)(2,1)}, bf16[2,128,1024]{2,1,0:T(8,128)(2,1)}, u32[]{:S(2)}, u32[]{:S(2)}) collective-permute-start(bf16[2,128,1024]{2,1,0:T(8,128)(2,1)} %collective-permute-done.1.refs_2_), channel_id=1, source_target_pairs={{0,4},{4,0},{8,12},{12,8},{16,20},{20,16},{24,28},{28,24},{1,5},{5... | collective-permute-start | bytes 1572872 | tf_op jit(solution)/shard_map/ppermute | solution.py:264
  44.7 13.5 %collective-permute-start.4 = (bf16[2,128,1024]{2,1,0:T(8,128)(2,1)}, bf16[2,128,1024]{2,1,0:T(8,128)(2,1)}, u32[]{:S(2)}, u32[]{:S(2)}) collective-permute-start(bf16[2,128,1024]{2,1,0:T(8,128)(2,1)} %collective-permute-done.3.refs_4_), channel_id=1, source_target_pairs={{0,4},{4,0},{8,12},{12,8},{16,20},{20,16},{24,28},{28,24},{1,5},{5... | collective-permute-start | bytes 1572872 | tf_op jit(solution)/shard_map/ppermute | solution.py:264
  47.7 7.5 %collective-permute-start.11 = (bf16[512,256]{1,0:T(8,128)(2,1)}, bf16[512,256]{1,0:T(8,128)(2,1)}, u32[]{:S(2)}, u32[]{:S(2)}) collective-permute-start(bf16[512,256]{1,0:T(8,128)(2,1)} %slice.28), channel_id=1, source_target_pairs={{0,1},{1,0},{2,3},{3,2},{4,5},{5,4},{6,7},{7,6},{8,9},{9,8},{10,11... | collective-permute-start | bytes 786440 | tf_op jit(solution)/shard_map/ppermute | solution.py:267
  49.2 7.5 %collective-permute-start.12 = (bf16[512,256]{1,0:T(8,128)(2,1)}, bf16[512,256]{1,0:T(8,128)(2,1)}, u32[]{:S(2)}, u32[]{:S(2)}) collective-permute-start(bf16[512,256]{1,0:T(8,128)(2,1)} %slice.29), channel_id=1, source_target_pairs={{0,2},{1,3},{2,0},{3,1},{4,6},{5,7},{6,4},{7,5},{8,10},{9,11},{10,... | collective-permute-start | bytes 786440 | tf_op jit(solution)/shard_map/ppermute | solution.py:267
  52.8 64.7 %collective-permute-start.21 = (bf16[4,144,1024]{2,1,0:T(8,128)(2,1)S(1)}, bf16[4,144,1024]{2,1,0:T(8,128)(2,1)S(1)}, u32[]{:S(2)}, u32[]{:S(2)}) collective-permute-start(bf16[4,144,1024]{2,1,0:T(8,128)(2,1)S(1)} %pad_maximum_fusion.refs_0_), channel_id=1, source_target_pairs={{0,4},{4,0},{8,12},{12,8},{16,20},{20,16},{24,28},{28,24},{1,5},{5... | collective-permute-start | bytes 3538952 | tf_op jit(solution)/shard_map/ppermute | solution.py:264
  55.2 11.8 %collective-permute-start.7 = (bf16[512,256]{1,0:T(8,128)(2,1)S(1)}, bf16[512,256]{1,0:T(8,128)(2,1)S(1)}, u32[]{:S(2)}, u32[]{:S(2)}) collective-permute-start(bf16[512,256]{1,0:T(8,128)(2,1)S(1)} %slice.26), channel_id=1, source_target_pairs={{0,1},{1,0},{2,3},{3,2},{4,5},{5,4},{6,7},{7,6},{8,9},{9,8},{10,11... | collective-permute-start | bytes 786440 | tf_op jit(solution)/shard_map/ppermute | solution.py:267
  56.7 10.3 %collective-permute-start.8 = (bf16[512,256]{1,0:T(8,128)(2,1)S(1)}, bf16[512,256]{1,0:T(8,128)(2,1)S(1)}, u32[]{:S(2)}, u32[]{:S(2)}) collective-permute-start(bf16[512,256]{1,0:T(8,128)(2,1)S(1)} %slice.27), channel_id=1, source_target_pairs={{0,2},{1,3},{2,0},{3,1},{4,6},{5,7},{6,4},{7,5},{8,10},{9,11},{10,... | collective-permute-start | bytes 786440 | tf_op jit(solution)/shard_map/ppermute | solution.py:267
  66.9 11.8 %collective-permute-start.14 = (bf16[2,2,128,256]{3,2,1,0:T(8,128)(2,1)}, bf16[2,2,128,256]{3,2,1,0:T(8,128)(2,1)S(1)}, u32[]{:S(2)}, u32[]{:S(2)}) collective-permute-start(bf16[2,2,128,256]{3,2,1,0:T(8,128)(2,1)} %get-tuple-element.16), channel_id=1, source_target_pairs={{0,4},{4,0},{8,12},{12,8},{16,20},{20,16},{24,28},{28,24},{1,5},{5... | collective-permute-start | bytes 786440 | tf_op jit(solution)/shard_map/ppermute | solution.py:264
  77.2 1.9 %collective-permute-start.13 = (bf16[2,2,128,256]{3,2,1,0:T(8,128)(2,1)}, bf16[2,2,128,256]{3,2,1,0:T(8,128)(2,1)S(1)}, u32[]{:S(2)}, u32[]{:S(2)}) collective-permute-start(bf16[2,2,128,256]{3,2,1,0:T(8,128)(2,1)} %get-tuple-element.15), channel_id=1, source_target_pairs={{0,4},{4,0},{8,12},{12,8},{16,20},{20,16},{24,28},{28,24},{1,5},{5... | collective-permute-start | bytes 786440 | tf_op jit(solution)/shard_map/ppermute | solution.py:264
  86.2 19.4 %collective-permute-start.16 = (bf16[64,1024]{1,0:T(8,128)(2,1)S(1)}, bf16[64,1024]{1,0:T(8,128)(2,1)S(1)}, u32[]{:S(2)}, u32[]{:S(2)}) collective-permute-start(bf16[64,1024]{1,0:T(8,128)(2,1)S(1)} %add.66), channel_id=1, source_target_pairs={{0,8},{4,12},{8,0},{12,4},{16,24},{20,28},{24,16},{28,20},{1,9},{5... | collective-permute-start | bytes 393224 | tf_op jit(solution)/shard_map/ppermute | solution.py:331
  105.7 11.2 %collective-permute-start.17 = (bf16[64,1024]{1,0:T(8,128)(2,1)S(1)}, bf16[64,1024]{1,0:T(8,128)(2,1)S(1)}, u32[]{:S(2)}, u32[]{:S(2)}) collective-permute-start(bf16[64,1024]{1,0:T(8,128)(2,1)S(1)} %add.67), channel_id=1, source_target_pairs={{0,16},{4,20},{8,24},{12,28},{16,0},{20,4},{24,8},{28,12},{1,17},{... | collective-permute-start | bytes 393224 | tf_op jit(solution)/shard_map/ppermute | solution.py:331
  122.6 7.1 %collective-permute-start.22 = (f32[16,1024]{1,0:T(8,128)}, f32[16,1024]{1,0:T(8,128)S(1)}, u32[]{:S(2)}, u32[]{:S(2)}) collective-permute-start(f32[16,1024]{1,0:T(8,128)} %get-tuple-element.21), channel_id=1, source_target_pairs={{0,8},{4,12},{8,16},{12,20},{16,24},{20,28},{24,0},{28,4},{1,9},{5... | collective-permute-start | bytes 196616 | tf_op jit(solution)/shard_map/ppermute | solution.py:358
  123.3 8.2 %collective-permute-start.23 = (f32[16,1024]{1,0:T(8,128)}, f32[16,1024]{1,0:T(8,128)S(1)}, u32[]{:S(2)}, u32[]{:S(2)}) collective-permute-start(f32[16,1024]{1,0:T(8,128)} %get-tuple-element.22), channel_id=1, source_target_pairs={{0,16},{4,20},{8,24},{12,28},{16,0},{20,4},{24,8},{28,12},{1,17},{... | collective-permute-start | bytes 196616 | tf_op jit(solution)/shard_map/ppermute | solution.py:358
  126.7 5.3 %collective-permute-start.24 = (f32[16,1024]{1,0:T(8,128)}, f32[16,1024]{1,0:T(8,128)S(1)}, u32[]{:S(2)}, u32[]{:S(2)}) collective-permute-start(f32[16,1024]{1,0:T(8,128)} %get-tuple-element.23), channel_id=1, source_target_pairs={{0,24},{4,28},{8,0},{12,4},{16,8},{20,12},{24,16},{28,20},{1,25},{... | collective-permute-start | bytes 196616 | tf_op jit(solution)/shard_map/ppermute | solution.py:358
  (22 other events, 230.5 us)

commit v2 on v1

--- a/solution.py
+++ b/solution.py
@@ -12,9 +12,9 @@
 D = 1024
 BF = jnp.bfloat16
 F32 = jnp.float32
-CHUNKS = (256, 256)
+CHUNKS = (384, 128)
 PAD = 16
-VMEM_LIMIT = 56 * 1024 * 1024
+MIB = 1024 * 1024
 
 
 def silu_half(half):
@@ -126,7 +126,7 @@
             pltpu.VMEM((hist, blocks // 2, 2 * here, 2 * here), F32),
             pltpu.VMEM((2 * here, cols), F32),
         ],
-        compiler_params=pltpu.CompilerParams(vmem_limit_bytes=VMEM_LIMIT),
+        compiler_params=pltpu.CompilerParams(vmem_limit_bytes=(8 + 2 * blocks) * MIB),
         cost_estimate=pl.CostEstimate(
             flops=flops, bytes_accessed=4 * 1024 * 1024, transcendentals=hist * here * 2 * here * blocks * cols // HD
         ),
@@ -181,7 +181,7 @@
         ),
         in_specs=[smem] + [vmem] * (3 + len(keeps) + len(received)),
         out_specs=(vmem, vmem, vmem),
-        compiler_params=pltpu.CompilerParams(vmem_limit_bytes=VMEM_LIMIT),
+        compiler_params=pltpu.CompilerParams(vmem_limit_bytes=16 * MIB),
         cost_estimate=pl.CostEstimate(
             flops=2 * hist * here * width * width, bytes_accessed=5 * 1024 * 1024, transcendentals=0
         ),
@@ -242,7 +242,7 @@
             pltpu.VMEM((count, width), F32),
             pltpu.VMEM((chips, count // chips, width), F32),
         ],
-        compiler_params=pltpu.CompilerParams(vmem_limit_bytes=VMEM_LIMIT),
+        compiler_params=pltpu.CompilerParams(vmem_limit_bytes=8 * MIB + 3 * sum(t.size for t in tables)),
         cost_estimate=pl.CostEstimate(
             flops=4 * count * width * 1024, bytes_accessed=3 * 1024 * 1024, transcendentals=count * 1024
         ),
@@ -271,38 +271,51 @@
 
     half = width // 2
     chunks = []
+    offset = core * half
     if grid:
-        offset = core * half
+        first = []
         for cols in CHUNKS:
             own = lax.dynamic_slice_in_dim(w_in, offset, cols, 1)
-            over_x, over_y = across(own, 1), across(own, 2)
-            top = across(over_y[: width // 2], 1)
-            bottom = across(over_x[width // 2 :], 2)
-            chunks.append(([own, over_x, over_y, top, bottom], (0, 1, 2, 3, 3)))
             offset = offset + cols
+            if not chunks:
+                over_x, over_y = across(own, 1), across(own, 2)
+                first = [own, over_x, over_y]
+                top = across(over_y[: width // 2], 1)
+                bottom = across(over_x[width // 2 :], 2)
+                chunks.append((first + [top, bottom], (0, 1, 2, 3, 3)))
+            else:
+                own, _ = lax.optimization_barrier((own, chunks[0][0]))
+                chunks.append(([own] + [across(own, bit) for bit in (1, 2, 3)], (0, 1, 2, 3)))
         flip = mine
     else:
         whole = lax.all_gather(w_in, "batch", axis=1, tiled=True)
-        offset = core * half
         for cols in CHUNKS:
-            chunks.append(
-                (
-                    [
-                        lax.dynamic_slice_in_dim(whole, group * width + offset, cols, 1)
-                        for group in range(4)
-                    ],
-                    (0, 1, 2, 3),
-                )
-            )
+            groups = [
+                lax.dynamic_slice_in_dim(whole, group * width + offset, cols, 1)
+                for group in range(4)
+            ]
+            chunks.append((groups, (0, 1, 2, 3)))
             offset = offset + cols
         flip = jnp.int32(0)
 
     longest = seq * here // 2
     reach = min(chips - 1, -(-(longest - 1) // (2 * here)))
-    blocks = [events, swap(events)]
-    for back in range(1, reach + 1):
-        earlier = ahead(events, back)
-        blocks += [earlier, swap(earlier)]
+    window = [events]
+    for back in range(reach):
+        last = window[-1]
+        if grid and back == 0:
+            last, _ = lax.optimization_barrier((last, first[0]))
+        elif grid and back == 1:
+            last, _ = lax.optimization_barrier((last, first))
+        window.append(ahead(last, 1))
+    blocks = []
+    for back, block in enumerate(window):
+        source = block
+        if back == 0:
+            source, _ = lax.optimization_barrier((block, window[1]))
+        elif grid and back == reach:
+            source, _ = lax.optimization_barrier((block, chunks[0][0]))
+        blocks += [block, swap(source)]
 
     tag = jnp.stack([flip, place, core])
     keeps, received = [], []
@@ -332,6 +345,7 @@
         step *= 2
 
     items = item_table.shape[0]
+    item_table, _ = lax.optimization_barrier((item_table, (chunks[-1][0], keeps[0])))
     padded = jnp.concatenate(
         [
             item_table,
@@ -343,6 +357,7 @@
         over_x = across(padded, 1)
         over_y = across(padded, 2)
         corner = across(padded, 3)
+        over_x, over_y, corner, _ = lax.optimization_barrier((over_x, over_y, corner, rows_send))
         table = jnp.stack([padded, over_x, over_y, corner])
         holder = mine ^ jnp.arange(4, dtype=jnp.int32)
     else:

time: 133 us -> 108 us (0.81)
  starting transfers between devices: 52.9 us -> 34 us
  other arithmetic: 5.8 us -> 1.46 us
  Pallas kernels: 25.4 us -> 22.4 us
  waiting for transfers between devices: 40.7 us -> 42.3 us
    ppermute x2, starting transfers between devices: 20.3 us -> 6.36 us  [on_device(): lax.ppermute(rows, 'seq', [(i, i ^ 2 * step) for i in range(seq)])]
    ppermute x11 -> x10, waiting for transfers between devices: 19 us -> 13.1 us  [across(): return lax.ppermute(value, 'batch', [(i, i ^ bit) for i in range(batch)])]
    ppermute x2, waiting for transfers between devices: 5.99 us -> 9.8 us  [ahead(): lax.ppermute(value, 'seq', [(i, i + 2 * by) for i in range(seq - 2 * by)])]
    ppermute x11 -> x10, starting transfers between devices: 17.2 us -> 13.7 us  [across(): return lax.ppermute(value, 'batch', [(i, i ^ bit) for i in range(batch)])]
    ppermute x7, waiting for transfers between devices: 1.47 us -> 3.61 us  [swap(): return lax.ppermute(value, 'seq', [(i, i ^ 1) for i in range(seq)])]
    unnamed x42 -> x24, local copies, waits for them, and re-layouts: 3.2 us -> 3.86 us
  transfers between devices with their start and end apart: 25 -> 24, of which waited for: 12 -> 12; matrix products, arithmetic and copies ran while one was open for 6% -> 3% of each run, Pallas kernels for 16% -> 18%
where the time goes in v2:
time: 108 us
  waiting for transfers between devices  42.3 us (39%)
  starting transfers between devices  34 us (31%)
  Pallas kernels  22.4 us (21%)
  local copies, waits for them, and re-layouts  6.82 us (6%)
  other arithmetic  1.46 us (1%)
    pallas_call x2, Pallas kernels, attend(): pl.pallas_call(functools.partial(attend_kernel, blocks, split), out_shape...  16.8 us
    ppermute x10, starting transfers between devices, across(): return lax.ppermute(value, 'batch', [(i, i ^ bit) for i in range(batch)])  13.7 us
    ppermute x10, waiting for transfers between devices, across(): return lax.ppermute(value, 'batch', [(i, i ^ bit) for i in range(batch)])  13.1 us
    ppermute x2, waiting for transfers between devices, on_device(): lax.ppermute(rows, 'seq', [(i, i ^ 2 * step) for i in range(seq)])  9.99 us
    ppermute x2, waiting for transfers between devices, ahead(): lax.ppermute(value, 'seq', [(i, i + 2 * by) for i in range(seq - 2 * by)])  9.8 us
    ppermute x2, starting transfers between devices, ahead(): lax.ppermute(value, 'seq', [(i, i + 2 * by) for i in range(seq - 2 * by)])  8.56 us
    ppermute x2, starting transfers between devices, on_device(): lax.ppermute(rows, 'seq', [(i, i ^ 2 * step) for i in range(seq)])  6.36 us
    ppermute x3, waiting for transfers between devices, on_device(): lax.ppermute(parts[step], 'seq', [(i, (i + 2 * step) % seq) for i in rang...  5.8 us
  transfers between devices with their start and end apart: 24, of which 12 were waited for; matrix products, arithmetic and copies ran while one was open for 3% of the time, Pallas kernels for 18%

profile of v2, /device:TPU:0, one launch (start us, length us, event | category | flops | bytes accessed | tf_op | source)
XLA Modules:
  0.0 107.9 jit_solution(3994405804862005987)
XLA Ops:
  0.7 1.6 %copy-done = bf16[1024,1024]{1,0:T(8,128)(2,1)S(1)} copy-done((bf16[1024,1024]{1,0:T(8,128)(2,1)S(1)}, bf16[1024,1024]{1,0:T(8,128)(2,1)}, u32[]{:S(2)}) %copy-start) | copy-done | bytes 2097176
  2.4 3.0 %collective-permute-start.3 = (bf16[1024,384]{1,0:T(8,128)(2,1)S(1)}, bf16[1024,384]{1,0:T(8,128)(2,1)S(1)}, u32[]{:S(2)}, u32[]{:S(2)}) collective-permute-start(bf16[1024,384]{1,0:T(8,128)(2,1)S(1)} %constant_dynamic-slice_fusion.1.refs_6_), channel_id=1, source_target_pairs={{0,1},{1,0},{2,3},{3,2},{4,5},{5,4},{6,7},{7,6},{8,9},{9,8},{10,11... | collective-permute-start | bytes 2359304 | tf_op jit(solution)/shard_map/ppermute | solution.py:267
  5.4 1.5 %collective-permute-start.4 = (bf16[1024,384]{1,0:T(8,128)(2,1)S(1)}, bf16[1024,384]{1,0:T(8,128)(2,1)S(1)}, u32[]{:S(2)}, u32[]{:S(2)}) collective-permute-start(bf16[1024,384]{1,0:T(8,128)(2,1)S(1)} %constant_dynamic-slice_fusion.1.refs_6_), channel_id=1, source_target_pairs={{0,2},{1,3},{2,0},{3,1},{4,6},{5,7},{6,4},{7,5},{8,10},{9,11},{10,... | collective-permute-start | bytes 2359304 | tf_op jit(solution)/shard_map/ppermute | solution.py:267
  6.9 4.3 %collective-permute-start = (bf16[2,128,1024]{2,1,0:T(8,128)(2,1)S(1)}, bf16[2,128,1024]{2,1,0:T(8,128)(2,1)}, u32[]{:S(2)}, u32[]{:S(2)}) collective-permute-start(bf16[2,128,1024]{2,1,0:T(8,128)(2,1)S(1)} %copy-done.2), channel_id=1, source_target_pairs={{0,8},{4,12},{8,16},{12,20},{16,24},{20,28},{1,9},{5,13},{9,17},{1... | collective-permute-start | bytes 1572872 | tf_op jit(solution)/shard_map/ppermute | solution.py:270
  11.2 9.8 %collective-permute-done.refs_2_ = bf16[2,128,1024]{2,1,0:T(8,128)(2,1)} collective-permute-done((bf16[2,128,1024]{2,1,0:T(8,128)(2,1)S(1)}, bf16[2,128,1024]{2,1,0:T(8,128)(2,1)}, u32[]{:S(2)}, u32[]{:S(2)}) %collective-permute-start) | collective-permute-done | bytes 524320 | tf_op jit(solution)/shard_map/ppermute | solution.py:270
  21.0 1.9 %collective-permute-done.3.refs_7_ = bf16[1024,384]{1,0:T(8,128)(2,1)S(1)} collective-permute-done((bf16[1024,384]{1,0:T(8,128)(2,1)S(1)}, bf16[1024,384]{1,0:T(8,128)(2,1)S(1)}, u32[]{:S(2)}, u32[]{:S(2)}) %collective-permute-start.3) | collective-permute-done | bytes 786464 | tf_op jit(solution)/shard_map/ppermute | solution.py:267
  24.4 4.3 %collective-permute-start.5 = (bf16[2,128,1024]{2,1,0:T(8,128)(2,1)}, bf16[2,128,1024]{2,1,0:T(8,128)(2,1)}, u32[]{:S(2)}, u32[]{:S(2)}) collective-permute-start(bf16[2,128,1024]{2,1,0:T(8,128)(2,1)} %collective-permute-done.refs_2_), channel_id=1, source_target_pairs={{0,8},{4,12},{8,16},{12,20},{16,24},{20,28},{1,9},{5,13},{9,17},{1... | collective-permute-start | bytes 1572872 | tf_op jit(solution)/shard_map/ppermute | solution.py:270
  30.8 1.5 %collective-permute-start.7 = (bf16[512,384]{1,0:T(8,128)(2,1)}, bf16[512,384]{1,0:T(8,128)(2,1)}, u32[]{:S(2)}, u32[]{:S(2)}) collective-permute-start(bf16[512,384]{1,0:T(8,128)(2,1)} %slice.19), channel_id=1, source_target_pairs={{0,2},{1,3},{2,0},{3,1},{4,6},{5,7},{6,4},{7,5},{8,10},{9,11},{10,... | collective-permute-start | bytes 1179656 | tf_op jit(solution)/shard_map/ppermute | solution.py:267
  32.8 6.3 %collective-permute-done.6.refs_9_ = bf16[512,384]{1,0:T(8,128)(2,1)} collective-permute-done((bf16[512,384]{1,0:T(8,128)(2,1)}, bf16[512,384]{1,0:T(8,128)(2,1)}, u32[]{:S(2)}, u32[]{:S(2)}) %collective-permute-start.6) | collective-permute-done | bytes 393248 | tf_op jit(solution)/shard_map/ppermute | solution.py:267
  42.3 1.5 %collective-permute-start.10 = (bf16[1024,128]{1,0:T(8,128)(2,1)S(1)}, bf16[1024,128]{1,0:T(8,128)(2,1)S(1)}, u32[]{:S(2)}, u32[]{:S(2)}) collective-permute-start(bf16[1024,128]{1,0:T(8,128)(2,1)S(1)} %constant_dynamic-slice_fusion.refs_6_), channel_id=1, source_target_pairs={{0,2},{1,3},{2,0},{3,1},{4,6},{5,7},{6,4},{7,5},{8,10},{9,11},{10,... | collective-permute-start | bytes 786440 | tf_op jit(solution)/shard_map/ppermute | solution.py:267
  46.6 9.9 %attend.2 = (bf16[2,2,128,384]{3,2,1,0:T(8,128)(2,1)S(1)}, bf16[2,2,128,384]{3,2,1,0:T(8,128)(2,1)S(1)}) custom-call(s32[3]{0:T(128)S(1)} %pad_add_fusion.tag_ref, s32[2,8]{1,0:T(2,128)S(1)} %copy-done.7, bf16[2,128,1024]{2,1,0:T(8,128)(2,1)S(1)} %copy-done.2, bf16[2,128,1024]{2,1,0:T(8,128)(2,1)} %collective-permute-done.1.refs_1_, ...), custom_call_target="tpu_custom_call" | custom-call | flops 4429185024 | bytes 4194304 | tf_op jit(solution)/shard_map/attend/pallas_call | solution.py:119
  58.2 1.5 %collective-permute-start.18 = (bf16[144,1024]{1,0:T(8,128)(2,1)S(1)}, bf16[144,1024]{1,0:T(8,128)(2,1)S(1)}, u32[]{:S(2)}, u32[]{:S(2)}) collective-permute-start(bf16[144,1024]{1,0:T(8,128)(2,1)S(1)} %get-tuple-element.43), channel_id=1, source_target_pairs={{0,2},{1,3},{2,0},{3,1},{4,6},{5,7},{6,4},{7,5},{8,10},{9,11},{10,... | collective-permute-start | bytes 884744 | tf_op jit(solution)/shard_map/ppermute | solution.py:267
  60.3 6.9 %attend.3 = (bf16[2,2,128,128]{3,2,1,0:T(8,128)(2,1)S(1)}, bf16[2,2,128,128]{3,2,1,0:T(8,128)(2,1)S(1)}) custom-call(s32[3]{0:T(128)S(1)} %pad_add_fusion.tag_ref, s32[2,8]{1,0:T(2,128)S(1)} %copy-done.7, bf16[2,128,1024]{2,1,0:T(8,128)(2,1)S(1)} %copy-done.2, bf16[2,128,1024]{2,1,0:T(8,128)(2,1)} %collective-permute-done.1.refs_1_, ...), custom_call_target="tpu_custom_call" | custom-call | flops 1476395008 | bytes 4194304 | tf_op jit(solution)/shard_map/attend/pallas_call | solution.py:119
  68.7 2.7 %finish.1 = (bf16[2,128,1024]{2,1,0:T(8,128)(2,1)}, bf16[64,1024]{1,0:T(8,128)(2,1)S(1)}, bf16[64,1024]{1,0:T(8,128)(2,1)}) custom-call(s32[3]{0:T(128)S(1)} %pad_add_fusion.tag_ref, s32[2,64,1]{2,1,0:T(8,128)S(1)} %reverse_select_fusion.listed_ref, bf16[2,128,1024]{2,1,0:T(8,128)(2,1)S(1)} %copy-done.2, bf16[1024,1024]{1,0:T(8,128)(2,1)S(1)} %copy-done.1, ...), custom_call_target="tpu_custom_call" | custom-call | flops 536870912 | bytes 5242880 | tf_op jit(solution)/shard_map/finish/pallas_call | solution.py:175
  71.4 2.3 %collective-permute-done.18 = bf16[144,1024]{1,0:T(8,128)(2,1)S(1)} collective-permute-done((bf16[144,1024]{1,0:T(8,128)(2,1)S(1)}, bf16[144,1024]{1,0:T(8,128)(2,1)S(1)}, u32[]{:S(2)}, u32[]{:S(2)}) %collective-permute-start.18) | collective-permute-done | bytes 294944 | tf_op jit(solution)/shard_map/ppermute | solution.py:267
  74.5 2.3 %collective-permute-done.14 = bf16[64,1024]{1,0:T(8,128)(2,1)S(1)} collective-permute-done((bf16[64,1024]{1,0:T(8,128)(2,1)}, bf16[64,1024]{1,0:T(8,128)(2,1)S(1)}, u32[]{:S(2)}, u32[]{:S(2)}) %collective-permute-start.14) | collective-permute-done | bytes 131104 | tf_op jit(solution)/shard_map/ppermute | solution.py:264
  76.8 2.5 %collective-permute-start.15 = (bf16[64,1024]{1,0:T(8,128)(2,1)S(1)}, bf16[64,1024]{1,0:T(8,128)(2,1)S(1)}, u32[]{:S(2)}, u32[]{:S(2)}) collective-permute-start(bf16[64,1024]{1,0:T(8,128)(2,1)S(1)} %add.66), channel_id=1, source_target_pairs={{0,8},{4,12},{8,0},{12,4},{16,24},{20,28},{24,16},{28,20},{1,9},{5... | collective-permute-start | bytes 393224 | tf_op jit(solution)/shard_map/ppermute | solution.py:344
  79.3 4.0 %collective-permute-done.15 = bf16[64,1024]{1,0:T(8,128)(2,1)S(1)} collective-permute-done((bf16[64,1024]{1,0:T(8,128)(2,1)S(1)}, bf16[64,1024]{1,0:T(8,128)(2,1)S(1)}, u32[]{:S(2)}, u32[]{:S(2)}) %collective-permute-start.15) | collective-permute-done | bytes 131104 | tf_op jit(solution)/shard_map/ppermute | solution.py:344
  83.3 3.9 %collective-permute-start.16 = (bf16[64,1024]{1,0:T(8,128)(2,1)S(1)}, bf16[64,1024]{1,0:T(8,128)(2,1)}, u32[]{:S(2)}, u32[]{:S(2)}) collective-permute-start(bf16[64,1024]{1,0:T(8,128)(2,1)S(1)} %add.67), channel_id=1, source_target_pairs={{0,16},{4,20},{8,24},{12,28},{16,0},{20,4},{24,8},{28,12},{1,17},{... | collective-permute-start | bytes 393224 | tf_op jit(solution)/shard_map/ppermute | solution.py:344
  87.5 6.0 %collective-permute-done.16 = bf16[64,1024]{1,0:T(8,128)(2,1)} collective-permute-done((bf16[64,1024]{1,0:T(8,128)(2,1)S(1)}, bf16[64,1024]{1,0:T(8,128)(2,1)}, u32[]{:S(2)}, u32[]{:S(2)}) %collective-permute-start.16) | collective-permute-done | bytes 131104 | tf_op jit(solution)/shard_map/ppermute | solution.py:344
  94.4 2.8 %score.1 = (f32[16,1024]{1,0:T(8,128)S(1)}, f32[16,1024]{1,0:T(8,128)S(1)}, f32[16,1024]{1,0:T(8,128)S(1)}, f32[16,1024]{1,0:T(8,128)S(1)}) custom-call(s32[3]{0:T(128)S(1)} %pad_add_fusion.tag_ref, s32[8]{0:T(128)S(1)} %pad_add_fusion.1.base_ref, bf16[64,1024]{1,0:T(8,128)(2,1)S(1)} %add.68.rows_ref, s32[64,1]{1,0:T(8,128)S(1)} %select_n.49.label_ref, ...), custom_call_target="tpu_custom_call" | custom-call | flops 268435456 | bytes 3145728 | tf_op jit(solution)/shard_map/score/pallas_call | solution.py:236
  97.2 3.5 %collective-permute-start.23 = (f32[16,1024]{1,0:T(8,128)S(1)}, f32[16,1024]{1,0:T(8,128)S(1)}, u32[]{:S(2)}, u32[]{:S(2)}) collective-permute-start(f32[16,1024]{1,0:T(8,128)S(1)} %get-tuple-element.41), channel_id=1, source_target_pairs={{0,24},{4,28},{8,0},{12,4},{16,8},{20,12},{24,16},{28,20},{1,25},{... | collective-permute-start | bytes 196616 | tf_op jit(solution)/shard_map/ppermute | solution.py:373
  101.4 1.9 %collective-permute-done.23 = f32[16,1024]{1,0:T(8,128)S(1)} collective-permute-done((f32[16,1024]{1,0:T(8,128)S(1)}, f32[16,1024]{1,0:T(8,128)S(1)}, u32[]{:S(2)}, u32[]{:S(2)}) %collective-permute-start.23) | collective-permute-done | bytes 65568 | tf_op jit(solution)/shard_map/ppermute | solution.py:373
  103.3 3.9 %collective-permute-done.22 = f32[16,1024]{1,0:T(8,128)S(1)} collective-permute-done((f32[16,1024]{1,0:T(8,128)S(1)}, f32[16,1024]{1,0:T(8,128)S(1)}, u32[]{:S(2)}, u32[]{:S(2)}) %collective-permute-start.22) | collective-permute-done | bytes 65568 | tf_op jit(solution)/shard_map/ppermute | solution.py:373
  (76 shorter events, 17.1 us)
Async XLA Ops:
  2.4 20.5 %collective-permute-start.3 = (bf16[1024,384]{1,0:T(8,128)(2,1)S(1)}, bf16[1024,384]{1,0:T(8,128)(2,1)S(1)}, u32[]{:S(2)}, u32[]{:S(2)}) collective-permute-start(bf16[1024,384]{1,0:T(8,128)(2,1)S(1)} %constant_dynamic-slice_fusion.1.refs_6_), channel_id=1, source_target_pairs={{0,1},{1,0},{2,3},{3,2},{4,5},{5,4},{6,7},{7,6},{8,9},{9,8},{10,11... | collective-permute-start | bytes 2359304 | tf_op jit(solution)/shard_map/ppermute | solution.py:267
  5.4 19.0 %collective-permute-start.4 = (bf16[1024,384]{1,0:T(8,128)(2,1)S(1)}, bf16[1024,384]{1,0:T(8,128)(2,1)S(1)}, u32[]{:S(2)}, u32[]{:S(2)}) collective-permute-start(bf16[1024,384]{1,0:T(8,128)(2,1)S(1)} %constant_dynamic-slice_fusion.1.refs_6_), channel_id=1, source_target_pairs={{0,2},{1,3},{2,0},{3,1},{4,6},{5,7},{6,4},{7,5},{8,10},{9,11},{10,... | collective-permute-start | bytes 2359304 | tf_op jit(solution)/shard_map/ppermute | solution.py:267
  6.9 14.1 %collective-permute-start = (bf16[2,128,1024]{2,1,0:T(8,128)(2,1)S(1)}, bf16[2,128,1024]{2,1,0:T(8,128)(2,1)}, u32[]{:S(2)}, u32[]{:S(2)}) collective-permute-start(bf16[2,128,1024]{2,1,0:T(8,128)(2,1)S(1)} %copy-done.2), channel_id=1, source_target_pairs={{0,8},{4,12},{8,16},{12,20},{16,24},{20,28},{1,9},{5,13},{9,17},{1... | collective-permute-start | bytes 1572872 | tf_op jit(solution)/shard_map/ppermute | solution.py:270
  24.4 15.9 %collective-permute-start.5 = (bf16[2,128,1024]{2,1,0:T(8,128)(2,1)}, bf16[2,128,1024]{2,1,0:T(8,128)(2,1)}, u32[]{:S(2)}, u32[]{:S(2)}) collective-permute-start(bf16[2,128,1024]{2,1,0:T(8,128)(2,1)} %collective-permute-done.refs_2_), channel_id=1, source_target_pairs={{0,8},{4,12},{8,16},{12,20},{16,24},{20,28},{1,9},{5,13},{9,17},{1... | collective-permute-start | bytes 1572872 | tf_op jit(solution)/shard_map/ppermute | solution.py:270
  29.4 9.7 %collective-permute-start.6 = (bf16[512,384]{1,0:T(8,128)(2,1)}, bf16[512,384]{1,0:T(8,128)(2,1)}, u32[]{:S(2)}, u32[]{:S(2)}) collective-permute-start(bf16[512,384]{1,0:T(8,128)(2,1)} %slice.18), channel_id=1, source_target_pairs={{0,1},{1,0},{2,3},{3,2},{4,5},{5,4},{6,7},{7,6},{8,9},{9,8},{10,11... | collective-permute-start | bytes 1179656 | tf_op jit(solution)/shard_map/ppermute | solution.py:267
  30.8 9.5 %collective-permute-start.7 = (bf16[512,384]{1,0:T(8,128)(2,1)}, bf16[512,384]{1,0:T(8,128)(2,1)}, u32[]{:S(2)}, u32[]{:S(2)}) collective-permute-start(bf16[512,384]{1,0:T(8,128)(2,1)} %slice.19), channel_id=1, source_target_pairs={{0,2},{1,3},{2,0},{3,1},{4,6},{5,7},{6,4},{7,5},{8,10},{9,11},{10,... | collective-permute-start | bytes 1179656 | tf_op jit(solution)/shard_map/ppermute | solution.py:267
  32.3 11.5 %collective-permute-start.1 = (bf16[2,128,1024]{2,1,0:T(8,128)(2,1)S(1)}, bf16[2,128,1024]{2,1,0:T(8,128)(2,1)}, u32[]{:S(2)}, u32[]{:S(2)}) collective-permute-start(bf16[2,128,1024]{2,1,0:T(8,128)(2,1)S(1)} %copy-done.2), channel_id=1, source_target_pairs={{0,4},{4,0},{8,12},{12,8},{16,20},{20,16},{24,28},{28,24},{1,5},{5... | collective-permute-start | bytes 1572872 | tf_op jit(solution)/shard_map/ppermute | solution.py:264
  32.3 12.1 %collective-permute-start.2 = (bf16[2,128,1024]{2,1,0:T(8,128)(2,1)}, bf16[2,128,1024]{2,1,0:T(8,128)(2,1)}, u32[]{:S(2)}, u32[]{:S(2)}) collective-permute-start(bf16[2,128,1024]{2,1,0:T(8,128)(2,1)} %collective-permute-done.refs_2_), channel_id=1, source_target_pairs={{0,4},{4,0},{8,12},{12,8},{16,20},{20,16},{24,28},{28,24},{1,5},{5... | collective-permute-start | bytes 1572872 | tf_op jit(solution)/shard_map/ppermute | solution.py:264
  40.3 4.1 %collective-permute-start.8 = (bf16[2,128,1024]{2,1,0:T(8,128)(2,1)}, bf16[2,128,1024]{2,1,0:T(8,128)(2,1)}, u32[]{:S(2)}, u32[]{:S(2)}) collective-permute-start(bf16[2,128,1024]{2,1,0:T(8,128)(2,1)} %collective-permute-done.5.refs_4_), channel_id=1, source_target_pairs={{0,4},{4,0},{8,12},{12,8},{16,20},{20,16},{24,28},{28,24},{1,5},{5... | collective-permute-start | bytes 1572872 | tf_op jit(solution)/shard_map/ppermute | solution.py:264
  40.8 15.8 %collective-permute-start.9 = (bf16[1024,128]{1,0:T(8,128)(2,1)S(1)}, bf16[1024,128]{1,0:T(8,128)(2,1)S(1)}, u32[]{:S(2)}, u32[]{:S(2)}) collective-permute-start(bf16[1024,128]{1,0:T(8,128)(2,1)S(1)} %constant_dynamic-slice_fusion.refs_6_), channel_id=1, source_target_pairs={{0,1},{1,0},{2,3},{3,2},{4,5},{5,4},{6,7},{7,6},{8,9},{9,8},{10,11... | collective-permute-start | bytes 786440 | tf_op jit(solution)/shard_map/ppermute | solution.py:267
  42.3 14.4 %collective-permute-start.10 = (bf16[1024,128]{1,0:T(8,128)(2,1)S(1)}, bf16[1024,128]{1,0:T(8,128)(2,1)S(1)}, u32[]{:S(2)}, u32[]{:S(2)}) collective-permute-start(bf16[1024,128]{1,0:T(8,128)(2,1)S(1)} %constant_dynamic-slice_fusion.refs_6_), channel_id=1, source_target_pairs={{0,2},{1,3},{2,0},{3,1},{4,6},{5,7},{6,4},{7,5},{8,10},{9,11},{10,... | collective-permute-start | bytes 786440 | tf_op jit(solution)/shard_map/ppermute | solution.py:267
  43.8 12.8 %collective-permute-start.11 = (bf16[1024,128]{1,0:T(8,128)(2,1)S(1)}, bf16[1024,128]{1,0:T(8,128)(2,1)S(1)}, u32[]{:S(2)}, u32[]{:S(2)}) collective-permute-start(bf16[1024,128]{1,0:T(8,128)(2,1)S(1)} %constant_dynamic-slice_fusion.refs_6_), channel_id=1, source_target_pairs={{0,3},{1,2},{2,1},{3,0},{4,7},{5,6},{6,5},{7,4},{8,11},{9,10},{10,... | collective-permute-start | bytes 786440 | tf_op jit(solution)/shard_map/ppermute | solution.py:267
  56.5 12.1 %collective-permute-start.12 = (bf16[2,2,128,384]{3,2,1,0:T(8,128)(2,1)S(1)}, bf16[2,2,128,384]{3,2,1,0:T(8,128)(2,1)S(1)}, u32[]{:S(2)}, u32[]{:S(2)}) collective-permute-start(bf16[2,2,128,384]{3,2,1,0:T(8,128)(2,1)S(1)} %get-tuple-element.29), channel_id=1, source_target_pairs={{0,4},{4,0},{8,12},{12,8},{16,20},{20,16},{24,28},{28,24},{1,5},{5... | collective-permute-start | bytes 1179656 | tf_op jit(solution)/shard_map/ppermute | solution.py:264
  56.7 14.7 %collective-permute-start.17 = (bf16[144,1024]{1,0:T(8,128)(2,1)S(1)}, bf16[144,1024]{1,0:T(8,128)(2,1)S(1)}, u32[]{:S(2)}, u32[]{:S(2)}) collective-permute-start(bf16[144,1024]{1,0:T(8,128)(2,1)S(1)} %get-tuple-element.43), channel_id=1, source_target_pairs={{0,1},{1,0},{2,3},{3,2},{4,5},{5,4},{6,7},{7,6},{8,9},{9,8},{10,11... | collective-permute-start | bytes 884744 | tf_op jit(solution)/shard_map/ppermute | solution.py:267
  58.2 15.4 %collective-permute-start.18 = (bf16[144,1024]{1,0:T(8,128)(2,1)S(1)}, bf16[144,1024]{1,0:T(8,128)(2,1)S(1)}, u32[]{:S(2)}, u32[]{:S(2)}) collective-permute-start(bf16[144,1024]{1,0:T(8,128)(2,1)S(1)} %get-tuple-element.43), channel_id=1, source_target_pairs={{0,2},{1,3},{2,0},{3,1},{4,6},{5,7},{6,4},{7,5},{8,10},{9,11},{10,... | collective-permute-start | bytes 884744 | tf_op jit(solution)/shard_map/ppermute | solution.py:267
  59.8 13.9 %collective-permute-start.19 = (bf16[144,1024]{1,0:T(8,128)(2,1)S(1)}, bf16[144,1024]{1,0:T(8,128)(2,1)S(1)}, u32[]{:S(2)}, u32[]{:S(2)}) collective-permute-start(bf16[144,1024]{1,0:T(8,128)(2,1)S(1)} %get-tuple-element.43), channel_id=1, source_target_pairs={{0,3},{1,2},{2,1},{3,0},{4,7},{5,6},{6,5},{7,4},{8,11},{9,10},{10,... | collective-permute-start | bytes 884744 | tf_op jit(solution)/shard_map/ppermute | solution.py:267
  67.2 1.4 %collective-permute-start.13 = (bf16[2,2,128,128]{3,2,1,0:T(8,128)(2,1)S(1)}, bf16[2,2,128,128]{3,2,1,0:T(8,128)(2,1)S(1)}, u32[]{:S(2)}, u32[]{:S(2)}) collective-permute-start(bf16[2,2,128,128]{3,2,1,0:T(8,128)(2,1)S(1)} %get-tuple-element.30), channel_id=1, source_target_pairs={{0,4},{4,0},{8,12},{12,8},{16,20},{20,16},{24,28},{28,24},{1,5},{5... | collective-permute-start | bytes 393224 | tf_op jit(solution)/shard_map/ppermute | solution.py:264
  73.8 20.6 %collective-permute-start.20 = (bf16[4,144,1024]{2,1,0:T(8,128)(2,1)S(1)}, bf16[4,144,1024]{2,1,0:T(8,128)(2,1)}, u32[]{:S(2)}, u32[]{:S(2)}) collective-permute-start(bf16[4,144,1024]{2,1,0:T(8,128)(2,1)S(1)} %pad_maximum_fusion.refs_0_), channel_id=1, source_target_pairs={{0,4},{4,0},{8,12},{12,8},{16,20},{20,16},{24,28},{28,24},{1,5},{5... | collective-permute-start | bytes 3538952 | tf_op jit(solution)/shard_map/ppermute | solution.py:264
  73.9 2.9 %collective-permute-start.14 = (bf16[64,1024]{1,0:T(8,128)(2,1)}, bf16[64,1024]{1,0:T(8,128)(2,1)S(1)}, u32[]{:S(2)}, u32[]{:S(2)}) collective-permute-start(bf16[64,1024]{1,0:T(8,128)(2,1)} %get-tuple-element.33), channel_id=1, source_target_pairs={{0,4},{4,0},{8,12},{12,8},{16,20},{20,16},{24,28},{28,24},{1,5},{5... | collective-permute-start | bytes 393224 | tf_op jit(solution)/shard_map/ppermute | solution.py:264
  76.8 6.5 %collective-permute-start.15 = (bf16[64,1024]{1,0:T(8,128)(2,1)S(1)}, bf16[64,1024]{1,0:T(8,128)(2,1)S(1)}, u32[]{:S(2)}, u32[]{:S(2)}) collective-permute-start(bf16[64,1024]{1,0:T(8,128)(2,1)S(1)} %add.66), channel_id=1, source_target_pairs={{0,8},{4,12},{8,0},{12,4},{16,24},{20,28},{24,16},{28,20},{1,9},{5... | collective-permute-start | bytes 393224 | tf_op jit(solution)/shard_map/ppermute | solution.py:344
  83.3 10.1 %collective-permute-start.16 = (bf16[64,1024]{1,0:T(8,128)(2,1)S(1)}, bf16[64,1024]{1,0:T(8,128)(2,1)}, u32[]{:S(2)}, u32[]{:S(2)}) collective-permute-start(bf16[64,1024]{1,0:T(8,128)(2,1)S(1)} %add.67), channel_id=1, source_target_pairs={{0,16},{4,20},{8,24},{12,28},{16,0},{20,4},{24,8},{28,12},{1,17},{... | collective-permute-start | bytes 393224 | tf_op jit(solution)/shard_map/ppermute | solution.py:344
  97.2 6.1 %collective-permute-start.23 = (f32[16,1024]{1,0:T(8,128)S(1)}, f32[16,1024]{1,0:T(8,128)S(1)}, u32[]{:S(2)}, u32[]{:S(2)}) collective-permute-start(f32[16,1024]{1,0:T(8,128)S(1)} %get-tuple-element.41), channel_id=1, source_target_pairs={{0,24},{4,28},{8,0},{12,4},{16,8},{20,12},{24,16},{28,20},{1,25},{... | collective-permute-start | bytes 196616 | tf_op jit(solution)/shard_map/ppermute | solution.py:373
  100.8 6.4 %collective-permute-start.22 = (f32[16,1024]{1,0:T(8,128)S(1)}, f32[16,1024]{1,0:T(8,128)S(1)}, u32[]{:S(2)}, u32[]{:S(2)}) collective-permute-start(f32[16,1024]{1,0:T(8,128)S(1)} %get-tuple-element.40), channel_id=1, source_target_pairs={{0,16},{4,20},{8,24},{12,28},{16,0},{20,4},{24,8},{28,12},{1,17},{... | collective-permute-start | bytes 196616 | tf_op jit(solution)/shard_map/ppermute | solution.py:373
  100.8 6.4 %collective-permute-start.21 = (f32[16,1024]{1,0:T(8,128)S(1)}, f32[16,1024]{1,0:T(8,128)S(1)}, u32[]{:S(2)}, u32[]{:S(2)}) collective-permute-start(f32[16,1024]{1,0:T(8,128)S(1)} %get-tuple-element.39), channel_id=1, source_target_pairs={{0,8},{4,12},{8,16},{12,20},{16,24},{20,28},{24,0},{28,4},{1,9},{5... | collective-permute-start | bytes 196616 | tf_op jit(solution)/shard_map/ppermute | solution.py:373
  (12 other events, 144.5 us)

commit v3 on v2

--- a/solution.py
+++ b/solution.py
@@ -12,7 +12,7 @@
 D = 1024
 BF = jnp.bfloat16
 F32 = jnp.float32
-CHUNKS = (384, 128)
+CHUNKS = (512,)
 PAD = 16
 MIB = 1024 * 1024
 
@@ -22,13 +22,33 @@
 
 
 def attend_kernel(blocks, split, tag_ref, seg_ref, *refs):
-    events = refs[:blocks]
-    weights = refs[blocks : blocks + len(split)]
-    keep_ref, send_ref, acts, mask, accum = refs[blocks + len(split) :]
-    hist, here, width = events[0].shape
+    sources = refs[:blocks]
+    pieces = refs[blocks : blocks + len(split)]
+    keep_ref, send_ref, events, weights, acts, mask, accum, event_sem, weight_sem = refs[blocks + len(split) :]
+    _, hist, here, width = events.shape
     cols = keep_ref.shape[-1]
     flip, place, core = tag_ref[0], tag_ref[1], tag_ref[2]
     chip = 2 * here
+
+    bases, seen = [], {}
+    for ref, slot in zip(pieces, split):
+        bases.append(seen.get(slot, 0))
+        seen[slot] = bases[-1] + ref.shape[0]
+
+    def event_copy(block):
+        return pltpu.make_async_copy(sources[block], events.at[block], event_sem.at[block])
+
+    def weight_copy(at):
+        rows = pl.ds(bases[at], pieces[at].shape[0])
+        return pltpu.make_async_copy(pieces[at], weights.at[split[at], rows], weight_sem.at[at])
+
+    event_copy(0).start()
+    weight_copy(0).start()
+    event_copy(1).start()
+    for at in range(1, len(split)):
+        weight_copy(at).start()
+    for block in range(2, blocks):
+        event_copy(block).start()
 
     def positions(shape, dim, back):
         at = lax.broadcasted_iota(jnp.int32, shape, dim)
@@ -49,19 +69,21 @@
             mask[h, back] = jnp.where(allowed, 1.0, 0.0).astype(F32)
 
     def project(slot, block):
-        rows = events[block][...].reshape(hist * here, width)
-        total, base = None, 0
-        for ref, owner in zip(weights, split):
+        rows = events[block].reshape(hist * here, width)
+        total = jnp.dot(rows, weights[slot], preferred_element_type=F32)
+        acts[slot, block] = silu_half(0.5 * total).astype(BF).reshape(hist, here, cols)
+
+    for slot in range(4):
+        for at, owner in enumerate(split):
             if owner == slot:
-                depth = ref.shape[0]
-                part = jnp.dot(rows[:, base : base + depth], ref[...], preferred_element_type=F32)
-                total = part if total is None else total + part
-                base += depth
-        acts[slot, block] = silu_half(0.5 * total).astype(BF).reshape(hist, here, cols)
-
+                weight_copy(at).wait()
+        for block in range(2):
+            if slot == 0:
+                event_copy(block).wait()
+            project(slot, block)
+    for block in range(2, blocks):
+        event_copy(block).wait()
     for slot in range(4):
-        for block in range(2):
-            project(slot, block)
 
         @pl.when(((flip ^ slot) & 1) == 1)
         def _(slot=slot):
@@ -119,14 +141,18 @@
     return pl.pallas_call(
         functools.partial(attend_kernel, blocks, split),
         out_shape=(part, part),
-        in_specs=[smem, smem] + [vmem] * (blocks + len(weights)),
+        in_specs=[smem, smem] + [pl.BlockSpec(memory_space=pltpu.HBM)] * (blocks + len(weights)),
         out_specs=(vmem, vmem),
         scratch_shapes=[
+            pltpu.VMEM((blocks, hist, here, width), BF),
+            pltpu.VMEM((4, width, cols), BF),
             pltpu.VMEM((4, blocks, hist, here, cols), BF),
             pltpu.VMEM((hist, blocks // 2, 2 * here, 2 * here), F32),
             pltpu.VMEM((2 * here, cols), F32),
+            pltpu.SemaphoreType.DMA((blocks,)),
+            pltpu.SemaphoreType.DMA((len(split),)),
         ],
-        compiler_params=pltpu.CompilerParams(vmem_limit_bytes=(8 + 2 * blocks) * MIB),
+        compiler_params=pltpu.CompilerParams(vmem_limit_bytes=60 * MIB),
         cost_estimate=pl.CostEstimate(
             flops=flops, bytes_accessed=4 * 1024 * 1024, transcendentals=hist * here * 2 * here * blocks * cols // HD
         ),
@@ -136,7 +162,9 @@
 
 def finish_kernel(count, tag_ref, listed_ref, events_ref, w_out_ref, *refs):
     parts = refs[: 2 * count]
-    layer_ref, keep_ref, send_ref = refs[2 * count :]
+    layer_ref, keep_ref, send_ref, matrix, matrix_sem = refs[2 * count :]
+    copy = pltpu.make_async_copy(w_out_ref, matrix, matrix_sem)
+    copy.start()
     hist, here, width = events_ref.shape
     rows = hist * here
     core = tag_ref[2]
@@ -154,10 +182,11 @@
     spread = sum(jnp.sum(p * p, axis=1, keepdims=True) for p in pieces) * (1.0 / width)
     inverse = lax.rsqrt(spread + 1e-05)
     output = events_ref[...].reshape(rows, width).astype(F32)
+    copy.wait()
     for p, g, at in zip(pieces, gates, offsets):
         mixed = (p * inverse * g).astype(BF)
         output = output + jnp.dot(
-            mixed, w_out_ref[pl.ds(at, p.shape[1]), :], preferred_element_type=F32
+            mixed, matrix[pl.ds(at, p.shape[1]), :], preferred_element_type=F32
         )
     layer = output.astype(BF)
     layer_ref[...] = layer.reshape(hist, here, width)
@@ -179,8 +208,9 @@
             jax.ShapeDtypeStruct((rows, width), BF),
             jax.ShapeDtypeStruct((rows, width), BF),
         ),
-        in_specs=[smem] + [vmem] * (3 + len(keeps) + len(received)),
+        in_specs=[smem, vmem, vmem, pl.BlockSpec(memory_space=pltpu.HBM)] + [vmem] * (len(keeps) + len(received)),
         out_specs=(vmem, vmem, vmem),
+        scratch_shapes=[pltpu.VMEM(w_out.shape, BF), pltpu.SemaphoreType.DMA],
         compiler_params=pltpu.CompilerParams(vmem_limit_bytes=16 * MIB),
         cost_estimate=pl.CostEstimate(
             flops=2 * hist * here * width * width, bytes_accessed=5 * 1024 * 1024, transcendentals=0
@@ -189,11 +219,11 @@
     )(tag, listed, events, w_out, *keeps, *received)
 
 
-def score_kernel(sources, tag_ref, base_ref, rows_ref, label_ref, *refs):
+def score_kernel(sources, tag_ref, base_ref, rows_ref, more_ref, label_ref, *refs):
     tables = refs[:sources]
     outs = refs[sources:-2]
     total, shares = refs[-2:]
-    rows = rows_ref[...]
+    rows = rows_ref[...] + more_ref[...]
     label = label_ref[...]
     scale = D ** (-0.5)
     total[...] = jnp.zeros_like(total)
@@ -221,33 +251,37 @@
             pl.loop(0, per)(one)
         which += per
     count = len(outs)
-    share = outs[0].shape[0]
+    share, hist, _ = outs[0].shape
     for chip in range(count):
-        shares[chip] = total[chip * share : (chip + 1) * share, :]
+        for at in range(share):
+            first = (chip * share + at) * hist
+            shares[chip, at] = total[first : first + hist, :]
     for step, out in enumerate(outs):
-        out[...] = shares[lax.rem(tag_ref[1] + step, count)]
-
-
-def score(tag, bases, rows, labels, tables, chips):
+        out[...] = shares[lax.rem(tag_ref[1] + step, count)].astype(out.dtype)
+
+
+def score(tag, bases, rows, more, labels, tables, chips, hist):
     count, width = rows.shape
+    share = count // chips // hist
     vmem = pl.BlockSpec(memory_space=pltpu.VMEM)
     smem = pl.BlockSpec(memory_space=pltpu.SMEM)
-    part = jax.ShapeDtypeStruct((count // chips, width), F32)
+    own = jax.ShapeDtypeStruct((share, hist, width), F32)
+    part = jax.ShapeDtypeStruct((share, hist, width), F32)
     return pl.pallas_call(
         functools.partial(score_kernel, len(tables)),
-        out_shape=(part,) * chips,
-        in_specs=[smem, smem] + [vmem] * (2 + len(tables)),
+        out_shape=(own,) + (part,) * (chips - 1),
+        in_specs=[smem, smem] + [vmem] * (3 + len(tables)),
         out_specs=(vmem,) * chips,
         scratch_shapes=[
             pltpu.VMEM((count, width), F32),
-            pltpu.VMEM((chips, count // chips, width), F32),
+            pltpu.VMEM((chips, share, hist, width), F32),
         ],
         compiler_params=pltpu.CompilerParams(vmem_limit_bytes=8 * MIB + 3 * sum(t.size for t in tables)),
         cost_estimate=pl.CostEstimate(
             flops=4 * count * width * 1024, bytes_accessed=3 * 1024 * 1024, transcendentals=count * 1024
         ),
         name="score",
-    )(tag, bases, rows, labels, *tables)
+    )(tag, bases, rows, more, labels, *tables)
 
 
 def on_device(events, w_in, w_out, item_table, item_bias, segment_lengths, listed_pos, labels):
@@ -305,16 +339,12 @@
         last = window[-1]
         if grid and back == 0:
             last, _ = lax.optimization_barrier((last, first[0]))
-        elif grid and back == 1:
-            last, _ = lax.optimization_barrier((last, first))
         window.append(ahead(last, 1))
     blocks = []
     for back, block in enumerate(window):
         source = block
         if back == 0:
             source, _ = lax.optimization_barrier((block, window[1]))
-        elif grid and back == reach:
-            source, _ = lax.optimization_barrier((block, chunks[0][0]))
         blocks += [block, swap(source)]
 
     tag = jnp.stack([flip, place, core])
@@ -340,12 +370,15 @@
     layer_out, rows, rows_send = finish(tag, index, events, w_out, keeps, received)
     rows = rows + swap(rows_send)
     step = 1
+    near, more = rows, jnp.zeros_like(rows)
     while step < chips:
-        rows = rows + lax.ppermute(rows, "seq", [(i, i ^ (2 * step)) for i in range(seq)])
+        if step > 1:
+            rows = near = rows + more
+        more = lax.ppermute(rows, "seq", [(i, i ^ (2 * step)) for i in range(seq)])
         step *= 2
 
     items = item_table.shape[0]
-    item_table, _ = lax.optimization_barrier((item_table, (chunks[-1][0], keeps[0])))
+    item_table, _ = lax.optimization_barrier((item_table, window[-1]))
     padded = jnp.concatenate(
         [
             item_table,
@@ -354,26 +387,25 @@
         0,
     )
     if grid:
-        over_x = across(padded, 1)
-        over_y = across(padded, 2)
-        corner = across(padded, 3)
-        over_x, over_y, corner, _ = lax.optimization_barrier((over_x, over_y, corner, rows_send))
-        table = jnp.stack([padded, over_x, over_y, corner])
+        tables = [padded, across(padded, 1), across(padded, 2), across(padded, 3)]
+        tables, _ = lax.optimization_barrier((tables, near))
+        tables = [piece[None] for piece in tables]
         holder = mine ^ jnp.arange(4, dtype=jnp.int32)
     else:
-        table = lax.all_gather(padded[None], "batch", axis=0, tiled=True)
+        tables = [lax.all_gather(padded[None], "batch", axis=0, tiled=True)]
         holder = jnp.arange(batch, dtype=jnp.int32)
-    other_table = swap(table)
+    tables = tables + [swap(piece) for piece in tables]
     bases = jnp.concatenate(
         [(rank * batch + holder) * items, ((rank ^ 1) * batch + holder) * items]
     )
-    parts = score(tag, bases, rows, own_labels, (table, other_table), chips)
+    parts = score(tag, bases, rows, more, own_labels, tables, chips, hist)
     total = parts[0]
     for step in range(1, chips):
-        total = total + lax.ppermute(
+        arrived = lax.ppermute(
             parts[step], "seq", [(i, (i + 2 * step) % seq) for i in range(seq)]
         )
-    return layer_out, total.reshape(share, hist, width)
+        total = total + arrived.astype(F32)
+    return layer_out, total
 
 
 def solution(mesh):

time: 108 us -> 101 us (0.935)
  Pallas kernels: 22.4 us -> 17.2 us
  waiting for transfers between devices: 42.3 us -> 39.7 us
    pallas_call x2 -> x1, Pallas kernels: 16.8 us -> 11.2 us  [attend(): pl.pallas_call(functools.partial(attend_kernel, blocks, split), out_shape...]
    ppermute x10 -> x7, waiting for transfers between devices: 13.1 us -> 10.4 us  [across(): return lax.ppermute(value, 'batch', [(i, i ^ bit) for i in range(batch)])]
    ppermute x10 -> x7, starting transfers between devices: 13.7 us -> 11.3 us  [across(): return lax.ppermute(value, 'batch', [(i, i ^ bit) for i in range(batch)])]
    ppermute x7 -> x9, waiting for transfers between devices: 3.61 us -> 1.36 us  [swap(): return lax.ppermute(value, 'seq', [(i, i ^ 1) for i in range(seq)])]
    ppermute x2, waiting for transfers between devices: 9.8 us -> 11.9 us  [ahead(): lax.ppermute(value, 'seq', [(i, i + 2 * by) for i in range(seq - 2 * by)])]
    unnamed x24 -> x22, local copies, waits for them, and re-layouts: 3.86 us -> 4.51 us
  transfers between devices with their start and end apart: 24 -> 23, of which waited for: 12 -> 10; matrix products, arithmetic and copies ran while one was open for 3% -> 3% of each run, Pallas kernels for 18% -> 3%
where the time goes in v3:
time: 101 us; the launch traced here: 100 us
  waiting for transfers between devices  39.7 us (39%)
  starting transfers between devices  33.9 us (34%)
  Pallas kernels  17.2 us (17%)
  local copies, waits for them, and re-layouts  6.93 us (7%)
  other arithmetic  1.57 us (2%)
    ppermute x2, waiting for transfers between devices, ahead(): lax.ppermute(value, 'seq', [(i, i + 2 * by) for i in range(seq - 2 * by)])  11.9 us
    ppermute x7, starting transfers between devices, across(): return lax.ppermute(value, 'batch', [(i, i ^ bit) for i in range(batch)])  11.3 us
    pallas_call x1, Pallas kernels, attend(): pl.pallas_call(functools.partial(attend_kernel, blocks, split), out_shape...  11.2 us
    ppermute x7, waiting for transfers between devices, across(): return lax.ppermute(value, 'batch', [(i, i ^ bit) for i in range(batch)])  10.4 us
    ppermute x2, waiting for transfers between devices, on_device(): more = lax.ppermute(rows, 'seq', [(i, i ^ 2 * step) for i in range(seq)])  10.2 us
    ppermute x2, starting transfers between devices, ahead(): lax.ppermute(value, 'seq', [(i, i + 2 * by) for i in range(seq - 2 * by)])  9.48 us
    ppermute x2, starting transfers between devices, on_device(): more = lax.ppermute(rows, 'seq', [(i, i ^ 2 * step) for i in range(seq)])  7.18 us
    ppermute x3, waiting for transfers between devices, on_device(): lax.ppermute(parts[step], 'seq', [(i, (i + 2 * step) % seq) for i in rang...  5.86 us
  transfers between devices with their start and end apart: 23, of which 10 were waited for; matrix products, arithmetic and copies ran while one was open for 3% of the time, Pallas kernels for 3%

profile of v3, /device:TPU:0, one launch (start us, length us, event | category | flops | bytes accessed | tf_op | source)
XLA Modules:
  0.0 100.2 jit_solution(8871995074232707399)
XLA Ops:
  0.7 1.6 %copy-done = bf16[1024,1024]{1,0:T(8,128)(2,1)S(1)} copy-done((bf16[1024,1024]{1,0:T(8,128)(2,1)S(1)}, bf16[1024,1024]{1,0:T(8,128)(2,1)}, u32[]{:S(2)}) %copy-start) | copy-done | bytes 2097176
  2.3 3.0 %collective-permute-start.6 = (bf16[1024,512]{1,0:T(8,128)(2,1)S(1)}, bf16[1024,512]{1,0:T(8,128)(2,1)S(1)}, u32[]{:S(2)}, u32[]{:S(2)}) collective-permute-start(bf16[1024,512]{1,0:T(8,128)(2,1)S(1)} %constant_dynamic-slice_fusion.refs_6_), channel_id=1, source_target_pairs={{0,2},{1,3},{2,0},{3,1},{4,6},{5,7},{6,4},{7,5},{8,10},{9,11},{10,... | collective-permute-start | bytes 3145736 | tf_op jit(solution)/shard_map/ppermute | solution.py:301
  5.4 1.5 %collective-permute-start.5 = (bf16[1024,512]{1,0:T(8,128)(2,1)S(1)}, bf16[1024,512]{1,0:T(8,128)(2,1)S(1)}, u32[]{:S(2)}, u32[]{:S(2)}) collective-permute-start(bf16[1024,512]{1,0:T(8,128)(2,1)S(1)} %constant_dynamic-slice_fusion.refs_6_), channel_id=1, source_target_pairs={{0,1},{1,0},{2,3},{3,2},{4,5},{5,4},{6,7},{7,6},{8,9},{9,8},{10,11... | collective-permute-start | bytes 3145736 | tf_op jit(solution)/shard_map/ppermute | solution.py:301
  6.9 4.3 %collective-permute-start = (bf16[2,128,1024]{2,1,0:T(8,128)(2,1)}, bf16[2,128,1024]{2,1,0:T(8,128)(2,1)}, u32[]{:S(2)}, u32[]{:S(2)}) collective-permute-start(bf16[2,128,1024]{2,1,0:T(8,128)(2,1)} %events_ref.1), channel_id=1, source_target_pairs={{0,8},{4,12},{8,16},{12,20},{16,24},{20,28},{1,9},{5,13},{9,17},{1... | collective-permute-start | bytes 1572872 | tf_op jit(solution)/shard_map/ppermute | solution.py:304
  11.2 10.1 %collective-permute-done.refs_2_ = bf16[2,128,1024]{2,1,0:T(8,128)(2,1)} collective-permute-done((bf16[2,128,1024]{2,1,0:T(8,128)(2,1)}, bf16[2,128,1024]{2,1,0:T(8,128)(2,1)}, u32[]{:S(2)}, u32[]{:S(2)}) %collective-permute-start) | collective-permute-done | bytes 524320 | tf_op jit(solution)/shard_map/ppermute | solution.py:304
  21.3 5.2 %collective-permute-start.3 = (bf16[2,128,1024]{2,1,0:T(8,128)(2,1)}, bf16[2,128,1024]{2,1,0:T(8,128)(2,1)}, u32[]{:S(2)}, u32[]{:S(2)}) collective-permute-start(bf16[2,128,1024]{2,1,0:T(8,128)(2,1)} %collective-permute-done.refs_2_), channel_id=1, source_target_pairs={{0,8},{4,12},{8,16},{12,20},{16,24},{20,28},{1,9},{5,13},{9,17},{1... | collective-permute-start | bytes 1572872 | tf_op jit(solution)/shard_map/ppermute | solution.py:304
  27.0 1.6 %collective-permute-done.6.refs_8_ = bf16[1024,512]{1,0:T(8,128)(2,1)S(1)} collective-permute-done((bf16[1024,512]{1,0:T(8,128)(2,1)S(1)}, bf16[1024,512]{1,0:T(8,128)(2,1)S(1)}, u32[]{:S(2)}, u32[]{:S(2)}) %collective-permute-start.6) | collective-permute-done | bytes 1048608 | tf_op jit(solution)/shard_map/ppermute | solution.py:301
  29.4 1.7 %collective-permute-start.7 = (bf16[512,512]{1,0:T(8,128)(2,1)}, bf16[512,512]{1,0:T(8,128)(2,1)}, u32[]{:S(2)}, u32[]{:S(2)}) collective-permute-start(bf16[512,512]{1,0:T(8,128)(2,1)} %slice.18), channel_id=1, source_target_pairs={{0,1},{1,0},{2,3},{3,2},{4,5},{5,4},{6,7},{7,6},{8,9},{9,8},{10,11... | collective-permute-start | bytes 1572872 | tf_op jit(solution)/shard_map/ppermute | solution.py:301
  32.3 1.5 %collective-permute-start.8 = (bf16[512,512]{1,0:T(8,128)(2,1)}, bf16[512,512]{1,0:T(8,128)(2,1)}, u32[]{:S(2)}, u32[]{:S(2)}) collective-permute-start(bf16[512,512]{1,0:T(8,128)(2,1)} %slice.19), channel_id=1, source_target_pairs={{0,2},{1,3},{2,0},{3,1},{4,6},{5,7},{6,4},{7,5},{8,10},{9,11},{10,... | collective-permute-start | bytes 1572872 | tf_op jit(solution)/shard_map/ppermute | solution.py:301
  33.8 1.8 %collective-permute-done.3.refs_4_ = bf16[2,128,1024]{2,1,0:T(8,128)(2,1)} collective-permute-done((bf16[2,128,1024]{2,1,0:T(8,128)(2,1)}, bf16[2,128,1024]{2,1,0:T(8,128)(2,1)}, u32[]{:S(2)}, u32[]{:S(2)}) %collective-permute-start.3) | collective-permute-done | bytes 524320 | tf_op jit(solution)/shard_map/ppermute | solution.py:304
  36.3 6.5 %collective-permute-done.7.refs_9_ = bf16[512,512]{1,0:T(8,128)(2,1)} collective-permute-done((bf16[512,512]{1,0:T(8,128)(2,1)}, bf16[512,512]{1,0:T(8,128)(2,1)}, u32[]{:S(2)}, u32[]{:S(2)}) %collective-permute-start.7) | collective-permute-done | bytes 524320 | tf_op jit(solution)/shard_map/ppermute | solution.py:301
  42.9 2.3 %collective-permute-done.8.refs_10_ = bf16[512,512]{1,0:T(8,128)(2,1)} collective-permute-done((bf16[512,512]{1,0:T(8,128)(2,1)}, bf16[512,512]{1,0:T(8,128)(2,1)}, u32[]{:S(2)}, u32[]{:S(2)}) %collective-permute-start.8) | collective-permute-done | bytes 524320 | tf_op jit(solution)/shard_map/ppermute | solution.py:301
  45.1 11.2 %attend.1 = (bf16[2,2,128,512]{3,2,1,0:T(8,128)(2,1)}, bf16[2,2,128,512]{3,2,1,0:T(8,128)(2,1)}) custom-call(s32[3]{0:T(128)} %pad_add_fusion.tag_ref, s32[2,8]{1,0:T(2,128)} %seg_ref.1, bf16[2,128,1024]{2,1,0:T(8,128)(2,1)} %events_ref.1, bf16[2,128,1024]{2,1,0:T(8,128)(2,1)} %collective-permute-done.1.refs_1_, ...), custom_call_target="tpu_custom_call" | custom-call | flops 5905580032 | bytes 4194304 | tf_op jit(solution)/shard_map/attend/pallas_call | solution.py:141
  57.6 1.5 %collective-permute-start.14 = (bf16[144,1024]{1,0:T(8,128)(2,1)S(1)}, bf16[144,1024]{1,0:T(8,128)(2,1)S(1)}, u32[]{:S(2)}, u32[]{:S(2)}) collective-permute-start(bf16[144,1024]{1,0:T(8,128)(2,1)S(1)} %fusion.1), channel_id=1, source_target_pairs={{0,2},{1,3},{2,0},{3,1},{4,6},{5,7},{6,4},{7,5},{8,10},{9,11},{10,... | collective-permute-start | bytes 884744 | tf_op jit(solution)/shard_map/ppermute | solution.py:301
  60.5 1.6 %copy-done.1 = bf16[1024,1024]{1,0:T(8,128)(2,1)S(1)} copy-done((bf16[1024,1024]{1,0:T(8,128)(2,1)S(1)}, bf16[1024,1024]{1,0:T(8,128)(2,1)}, u32[]{:S(2)}) %copy-start.1) | copy-done | bytes 2097176
  63.1 3.1 %finish.1 = (bf16[2,128,1024]{2,1,0:T(8,128)(2,1)}, bf16[64,1024]{1,0:T(8,128)(2,1)S(1)}, bf16[64,1024]{1,0:T(8,128)(2,1)S(1)}) custom-call(s32[3]{0:T(128)S(1)} %copy-done.3, s32[2,64,1]{2,1,0:T(8,128)S(1)} %reverse_select_fusion.listed_ref, bf16[2,128,1024]{2,1,0:T(8,128)(2,1)} %events_ref.1, bf16[1024,1024]{1,0:T(8,128)(2,1)S(1)} %copy-done.1, ...), custom_call_target="tpu_custom_call" | custom-call | flops 536870912 | bytes 5242880 | tf_op jit(solution)/shard_map/finish/pallas_call | solution.py:204
  67.7 3.6 %collective-permute-start.11 = (bf16[64,1024]{1,0:T(8,128)(2,1)S(1)}, bf16[64,1024]{1,0:T(8,128)(2,1)S(1)}, u32[]{:S(2)}, u32[]{:S(2)}) collective-permute-start(bf16[64,1024]{1,0:T(8,128)(2,1)S(1)} %add.53), channel_id=1, source_target_pairs={{0,8},{4,12},{8,0},{12,4},{16,24},{20,28},{24,16},{28,20},{1,9},{5... | collective-permute-start | bytes 393224 | tf_op jit(solution)/shard_map/ppermute | solution.py:377
  71.4 3.7 %collective-permute-done.11 = bf16[64,1024]{1,0:T(8,128)(2,1)S(1)} collective-permute-done((bf16[64,1024]{1,0:T(8,128)(2,1)S(1)}, bf16[64,1024]{1,0:T(8,128)(2,1)S(1)}, u32[]{:S(2)}, u32[]{:S(2)}) %collective-permute-start.11) | collective-permute-done | bytes 131104 | tf_op jit(solution)/shard_map/ppermute | solution.py:377
  76.3 3.5 %collective-permute-start.12 = (bf16[64,1024]{1,0:T(8,128)(2,1)S(1)}, bf16[64,1024]{1,0:T(8,128)(2,1)}, u32[]{:S(2)}, u32[]{:S(2)}) collective-permute-start(bf16[64,1024]{1,0:T(8,128)(2,1)S(1)} %add.54.rows_ref), channel_id=1, source_target_pairs={{0,16},{4,20},{8,24},{12,28},{16,0},{20,4},{24,8},{28,12},{1,17},{... | collective-permute-start | bytes 393224 | tf_op jit(solution)/shard_map/ppermute | solution.py:377
  80.1 6.4 %collective-permute-done.12.more_ref = bf16[64,1024]{1,0:T(8,128)(2,1)} collective-permute-done((bf16[64,1024]{1,0:T(8,128)(2,1)S(1)}, bf16[64,1024]{1,0:T(8,128)(2,1)}, u32[]{:S(2)}, u32[]{:S(2)}) %collective-permute-start.12) | collective-permute-done | bytes 131104 | tf_op jit(solution)/shard_map/ppermute | solution.py:377
  86.5 2.9 %score.1 = (f32[8,2,1024]{2,1,0:T(2,128)S(1)}, f32[8,2,1024]{2,1,0:T(2,128)S(1)}, f32[8,2,1024]{2,1,0:T(2,128)S(1)}, f32[8,2,1024]{2,1,0:T(2,128)S(1)}) custom-call(s32[3]{0:T(128)S(1)} %copy-done.3, s32[8]{0:T(128)S(1)} %pad_add_fusion.1.base_ref, bf16[64,1024]{1,0:T(8,128)(2,1)S(1)} %add.54.rows_ref, bf16[64,1024]{1,0:T(8,128)(2,1)} %collective-permute-done.12.more_ref, ...), custom_call_target="tpu_custom_call" | custom-call | flops 268435456 | bytes 3145728 | tf_op jit(solution)/shard_map/score/pallas_call | solution.py:270
  89.4 3.6 %collective-permute-start.22 = (f32[8,2,1024]{2,1,0:T(2,128)S(1)}, f32[8,2,1024]{2,1,0:T(2,128)S(1)}, u32[]{:S(2)}, u32[]{:S(2)}) collective-permute-start(f32[8,2,1024]{2,1,0:T(2,128)S(1)} %get-tuple-element.33), channel_id=1, source_target_pairs={{0,24},{4,28},{8,0},{12,4},{16,8},{20,12},{24,16},{28,20},{1,25},{... | collective-permute-start | bytes 196616 | tf_op jit(solution)/shard_map/ppermute | solution.py:404
  93.6 1.9 %collective-permute-done.22 = f32[8,2,1024]{2,1,0:T(2,128)S(1)} collective-permute-done((f32[8,2,1024]{2,1,0:T(2,128)S(1)}, f32[8,2,1024]{2,1,0:T(2,128)S(1)}, u32[]{:S(2)}, u32[]{:S(2)}) %collective-permute-start.22) | collective-permute-done | bytes 65568 | tf_op jit(solution)/shard_map/ppermute | solution.py:404
  95.5 4.0 %collective-permute-done.21 = f32[8,2,1024]{2,1,0:T(2,128)S(1)} collective-permute-done((f32[8,2,1024]{2,1,0:T(2,128)S(1)}, f32[8,2,1024]{2,1,0:T(2,128)S(1)}, u32[]{:S(2)}, u32[]{:S(2)}) %collective-permute-start.21) | collective-permute-done | bytes 65568 | tf_op jit(solution)/shard_map/ppermute | solution.py:404
  (67 shorter events, 11.1 us)
Async XLA Ops:
  2.3 42.8 %copy-start.4 = (bf16[1024,512]{1,0:T(8,128)(2,1)}, bf16[1024,512]{1,0:T(8,128)(2,1)S(1)}, u32[]{:S(2)}) copy-start(bf16[1024,512]{1,0:T(8,128)(2,1)S(1)} %constant_dynamic-slice_fusion.refs_6_) | copy-start | bytes 3145732
  2.3 26.2 %collective-permute-start.6 = (bf16[1024,512]{1,0:T(8,128)(2,1)S(1)}, bf16[1024,512]{1,0:T(8,128)(2,1)S(1)}, u32[]{:S(2)}, u32[]{:S(2)}) collective-permute-start(bf16[1024,512]{1,0:T(8,128)(2,1)S(1)} %constant_dynamic-slice_fusion.refs_6_), channel_id=1, source_target_pairs={{0,2},{1,3},{2,0},{3,1},{4,6},{5,7},{6,4},{7,5},{8,10},{9,11},{10,... | collective-permute-start | bytes 3145736 | tf_op jit(solution)/shard_map/ppermute | solution.py:301
  5.4 25.8 %collective-permute-start.5 = (bf16[1024,512]{1,0:T(8,128)(2,1)S(1)}, bf16[1024,512]{1,0:T(8,128)(2,1)S(1)}, u32[]{:S(2)}, u32[]{:S(2)}) collective-permute-start(bf16[1024,512]{1,0:T(8,128)(2,1)S(1)} %constant_dynamic-slice_fusion.refs_6_), channel_id=1, source_target_pairs={{0,1},{1,0},{2,3},{3,2},{4,5},{5,4},{6,7},{7,6},{8,9},{9,8},{10,11... | collective-permute-start | bytes 3145736 | tf_op jit(solution)/shard_map/ppermute | solution.py:301
  6.9 14.4 %collective-permute-start = (bf16[2,128,1024]{2,1,0:T(8,128)(2,1)}, bf16[2,128,1024]{2,1,0:T(8,128)(2,1)}, u32[]{:S(2)}, u32[]{:S(2)}) collective-permute-start(bf16[2,128,1024]{2,1,0:T(8,128)(2,1)} %events_ref.1), channel_id=1, source_target_pairs={{0,8},{4,12},{8,16},{12,20},{16,24},{20,28},{1,9},{5,13},{9,17},{1... | collective-permute-start | bytes 1572872 | tf_op jit(solution)/shard_map/ppermute | solution.py:304
  21.3 14.4 %collective-permute-start.3 = (bf16[2,128,1024]{2,1,0:T(8,128)(2,1)}, bf16[2,128,1024]{2,1,0:T(8,128)(2,1)}, u32[]{:S(2)}, u32[]{:S(2)}) collective-permute-start(bf16[2,128,1024]{2,1,0:T(8,128)(2,1)} %collective-permute-done.refs_2_), channel_id=1, source_target_pairs={{0,8},{4,12},{8,16},{12,20},{16,24},{20,28},{1,9},{5,13},{9,17},{1... | collective-permute-start | bytes 1572872 | tf_op jit(solution)/shard_map/ppermute | solution.py:304
  26.5 9.9 %collective-permute-start.1 = (bf16[2,128,1024]{2,1,0:T(8,128)(2,1)}, bf16[2,128,1024]{2,1,0:T(8,128)(2,1)}, u32[]{:S(2)}, u32[]{:S(2)}) collective-permute-start(bf16[2,128,1024]{2,1,0:T(8,128)(2,1)} %events_ref.1), channel_id=1, source_target_pairs={{0,4},{4,0},{8,12},{12,8},{16,20},{20,16},{24,28},{28,24},{1,5},{5... | collective-permute-start | bytes 1572872 | tf_op jit(solution)/shard_map/ppermute | solution.py:298
  26.5 9.9 %collective-permute-start.2 = (bf16[2,128,1024]{2,1,0:T(8,128)(2,1)}, bf16[2,128,1024]{2,1,0:T(8,128)(2,1)}, u32[]{:S(2)}, u32[]{:S(2)}) collective-permute-start(bf16[2,128,1024]{2,1,0:T(8,128)(2,1)} %collective-permute-done.refs_2_), channel_id=1, source_target_pairs={{0,4},{4,0},{8,12},{12,8},{16,20},{20,16},{24,28},{28,24},{1,5},{5... | collective-permute-start | bytes 1572872 | tf_op jit(solution)/shard_map/ppermute | solution.py:298
  29.4 13.4 %collective-permute-start.7 = (bf16[512,512]{1,0:T(8,128)(2,1)}, bf16[512,512]{1,0:T(8,128)(2,1)}, u32[]{:S(2)}, u32[]{:S(2)}) collective-permute-start(bf16[512,512]{1,0:T(8,128)(2,1)} %slice.18), channel_id=1, source_target_pairs={{0,1},{1,0},{2,3},{3,2},{4,5},{5,4},{6,7},{7,6},{8,9},{9,8},{10,11... | collective-permute-start | bytes 1572872 | tf_op jit(solution)/shard_map/ppermute | solution.py:301
  32.3 12.8 %collective-permute-start.8 = (bf16[512,512]{1,0:T(8,128)(2,1)}, bf16[512,512]{1,0:T(8,128)(2,1)}, u32[]{:S(2)}, u32[]{:S(2)}) collective-permute-start(bf16[512,512]{1,0:T(8,128)(2,1)} %slice.19), channel_id=1, source_target_pairs={{0,2},{1,3},{2,0},{3,1},{4,6},{5,7},{6,4},{7,5},{8,10},{9,11},{10,... | collective-permute-start | bytes 1572872 | tf_op jit(solution)/shard_map/ppermute | solution.py:301
  35.6 9.5 %collective-permute-start.4 = (bf16[2,128,1024]{2,1,0:T(8,128)(2,1)}, bf16[2,128,1024]{2,1,0:T(8,128)(2,1)}, u32[]{:S(2)}, u32[]{:S(2)}) collective-permute-start(bf16[2,128,1024]{2,1,0:T(8,128)(2,1)} %collective-permute-done.3.refs_4_), channel_id=1, source_target_pairs={{0,4},{4,0},{8,12},{12,8},{16,20},{20,16},{24,28},{28,24},{1,5},{5... | collective-permute-start | bytes 1572872 | tf_op jit(solution)/shard_map/ppermute | solution.py:298
  56.4 4.1 %collective-permute-start.9 = (bf16[2,2,128,512]{3,2,1,0:T(8,128)(2,1)}, bf16[2,2,128,512]{3,2,1,0:T(8,128)(2,1)S(1)}, u32[]{:S(2)}, u32[]{:S(2)}) collective-permute-start(bf16[2,2,128,512]{3,2,1,0:T(8,128)(2,1)} %get-tuple-element.21), channel_id=1, source_target_pairs={{0,4},{4,0},{8,12},{12,8},{16,20},{20,16},{24,28},{28,24},{1,5},{5... | collective-permute-start | bytes 1572872 | tf_op jit(solution)/shard_map/ppermute | solution.py:298
  56.9 18.2 %collective-permute-start.13 = (bf16[144,1024]{1,0:T(8,128)(2,1)S(1)}, bf16[144,1024]{1,0:T(8,128)(2,1)S(1)}, u32[]{:S(2)}, u32[]{:S(2)}) collective-permute-start(bf16[144,1024]{1,0:T(8,128)(2,1)S(1)} %fusion.1), channel_id=1, source_target_pairs={{0,1},{1,0},{2,3},{3,2},{4,5},{5,4},{6,7},{7,6},{8,9},{9,8},{10,11... | collective-permute-start | bytes 884744 | tf_op jit(solution)/shard_map/ppermute | solution.py:301
  57.6 17.5 %collective-permute-start.14 = (bf16[144,1024]{1,0:T(8,128)(2,1)S(1)}, bf16[144,1024]{1,0:T(8,128)(2,1)S(1)}, u32[]{:S(2)}, u32[]{:S(2)}) collective-permute-start(bf16[144,1024]{1,0:T(8,128)(2,1)S(1)} %fusion.1), channel_id=1, source_target_pairs={{0,2},{1,3},{2,0},{3,1},{4,6},{5,7},{6,4},{7,5},{8,10},{9,11},{10,... | collective-permute-start | bytes 884744 | tf_op jit(solution)/shard_map/ppermute | solution.py:301
  59.1 16.0 %collective-permute-start.15 = (bf16[144,1024]{1,0:T(8,128)(2,1)S(1)}, bf16[144,1024]{1,0:T(8,128)(2,1)}, u32[]{:S(2)}, u32[]{:S(2)}) collective-permute-start(bf16[144,1024]{1,0:T(8,128)(2,1)S(1)} %fusion.1), channel_id=1, source_target_pairs={{0,3},{1,2},{2,1},{3,0},{4,7},{5,6},{6,5},{7,4},{8,11},{9,10},{10,... | collective-permute-start | bytes 884744 | tf_op jit(solution)/shard_map/ppermute | solution.py:301
  66.2 1.4 %collective-permute-start.10 = (bf16[64,1024]{1,0:T(8,128)(2,1)S(1)}, bf16[64,1024]{1,0:T(8,128)(2,1)S(1)}, u32[]{:S(2)}, u32[]{:S(2)}) collective-permute-start(bf16[64,1024]{1,0:T(8,128)(2,1)S(1)} %get-tuple-element.24), channel_id=1, source_target_pairs={{0,4},{4,0},{8,12},{12,8},{16,20},{20,16},{24,28},{28,24},{1,5},{5... | collective-permute-start | bytes 393224 | tf_op jit(solution)/shard_map/ppermute | solution.py:298
  67.7 7.4 %collective-permute-start.11 = (bf16[64,1024]{1,0:T(8,128)(2,1)S(1)}, bf16[64,1024]{1,0:T(8,128)(2,1)S(1)}, u32[]{:S(2)}, u32[]{:S(2)}) collective-permute-start(bf16[64,1024]{1,0:T(8,128)(2,1)S(1)} %add.53), channel_id=1, source_target_pairs={{0,8},{4,12},{8,0},{12,4},{16,24},{20,28},{24,16},{28,20},{1,9},{5... | collective-permute-start | bytes 393224 | tf_op jit(solution)/shard_map/ppermute | solution.py:377
  75.2 11.3 %collective-permute-start.16 = (bf16[1,144,1024]{2,1,0:T(8,128)(2,1)S(1)}, bf16[1,144,1024]{2,1,0:T(8,128)(2,1)S(1)}, u32[]{:S(2)}, u32[]{:S(2)}) collective-permute-start(bf16[1,144,1024]{2,1,0:T(8,128)(2,1)S(1)} %bitcast.23), channel_id=1, source_target_pairs={{0,4},{4,0},{8,12},{12,8},{16,20},{20,16},{24,28},{28,24},{1,5},{5... | collective-permute-start | bytes 884744 | tf_op jit(solution)/shard_map/ppermute | solution.py:298
  75.3 11.3 %collective-permute-start.17 = (bf16[1,144,1024]{2,1,0:T(8,128)(2,1)S(1)}, bf16[1,144,1024]{2,1,0:T(8,128)(2,1)}, u32[]{:S(2)}, u32[]{:S(2)}) collective-permute-start(bf16[1,144,1024]{2,1,0:T(8,128)(2,1)S(1)} %bitcast.25), channel_id=1, source_target_pairs={{0,4},{4,0},{8,12},{12,8},{16,20},{20,16},{24,28},{28,24},{1,5},{5... | collective-permute-start | bytes 884744 | tf_op jit(solution)/shard_map/ppermute | solution.py:298
  75.8 10.8 %collective-permute-start.18 = (bf16[1,144,1024]{2,1,0:T(8,128)(2,1)S(1)}, bf16[1,144,1024]{2,1,0:T(8,128)(2,1)}, u32[]{:S(2)}, u32[]{:S(2)}) collective-permute-start(bf16[1,144,1024]{2,1,0:T(8,128)(2,1)S(1)} %bitcast.27), channel_id=1, source_target_pairs={{0,4},{4,0},{8,12},{12,8},{16,20},{20,16},{24,28},{28,24},{1,5},{5... | collective-permute-start | bytes 884744 | tf_op jit(solution)/shard_map/ppermute | solution.py:298
  75.8 10.7 %collective-permute-start.19 = (bf16[1,144,1024]{2,1,0:T(8,128)(2,1)}, bf16[1,144,1024]{2,1,0:T(8,128)(2,1)}, u32[]{:S(2)}, u32[]{:S(2)}) collective-permute-start(bf16[1,144,1024]{2,1,0:T(8,128)(2,1)} %bitcast.9.refs_3_), channel_id=1, source_target_pairs={{0,4},{4,0},{8,12},{12,8},{16,20},{20,16},{24,28},{28,24},{1,5},{5... | collective-permute-start | bytes 884744 | tf_op jit(solution)/shard_map/ppermute | solution.py:298
  76.3 10.2 %collective-permute-start.12 = (bf16[64,1024]{1,0:T(8,128)(2,1)S(1)}, bf16[64,1024]{1,0:T(8,128)(2,1)}, u32[]{:S(2)}, u32[]{:S(2)}) collective-permute-start(bf16[64,1024]{1,0:T(8,128)(2,1)S(1)} %add.54.rows_ref), channel_id=1, source_target_pairs={{0,16},{4,20},{8,24},{12,28},{16,0},{20,4},{24,8},{28,12},{1,17},{... | collective-permute-start | bytes 393224 | tf_op jit(solution)/shard_map/ppermute | solution.py:377
  89.4 6.1 %collective-permute-start.22 = (f32[8,2,1024]{2,1,0:T(2,128)S(1)}, f32[8,2,1024]{2,1,0:T(2,128)S(1)}, u32[]{:S(2)}, u32[]{:S(2)}) collective-permute-start(f32[8,2,1024]{2,1,0:T(2,128)S(1)} %get-tuple-element.33), channel_id=1, source_target_pairs={{0,24},{4,28},{8,0},{12,4},{16,8},{20,12},{24,16},{28,20},{1,25},{... | collective-permute-start | bytes 196616 | tf_op jit(solution)/shard_map/ppermute | solution.py:404
  93.0 6.5 %collective-permute-start.21 = (f32[8,2,1024]{2,1,0:T(2,128)S(1)}, f32[8,2,1024]{2,1,0:T(2,128)S(1)}, u32[]{:S(2)}, u32[]{:S(2)}) collective-permute-start(f32[8,2,1024]{2,1,0:T(2,128)S(1)} %get-tuple-element.32), channel_id=1, source_target_pairs={{0,16},{4,20},{8,24},{12,28},{16,0},{20,4},{24,8},{28,12},{1,17},{... | collective-permute-start | bytes 196616 | tf_op jit(solution)/shard_map/ppermute | solution.py:404
  93.0 6.5 %collective-permute-start.20 = (f32[8,2,1024]{2,1,0:T(2,128)S(1)}, f32[8,2,1024]{2,1,0:T(2,128)S(1)}, u32[]{:S(2)}, u32[]{:S(2)}) collective-permute-start(f32[8,2,1024]{2,1,0:T(2,128)S(1)} %get-tuple-element.31), channel_id=1, source_target_pairs={{0,8},{4,12},{8,16},{12,20},{16,24},{20,28},{24,0},{28,4},{1,9},{5... | collective-permute-start | bytes 196616 | tf_op jit(solution)/shard_map/ppermute | solution.py:404
  (10 other events, 107.9 us)

commit v4 on v3

--- a/solution.py
+++ b/solution.py
@@ -160,7 +160,22 @@
     )(tag, lengths, *events, *weights)
 
 
-def finish_kernel(count, tag_ref, listed_ref, events_ref, w_out_ref, *refs):
+def column_of(ref, core, share, count):
+    hist, listed = ref.shape
+    row = lax.broadcasted_iota(jnp.int32, (count, 1), 0)
+    lane = lax.broadcasted_iota(jnp.int32, (1, listed), 1)
+    bits, more = hist.bit_length() - 1, share.bit_length() - 1
+    which = row & (hist - 1)
+    place = (row >> (bits + more)) * (2 * share) + core * share + ((row >> bits) & (share - 1))
+    total = jnp.zeros((count, 1), F32)
+    for h in range(hist):
+        chosen = (lane == place) & (which == h)
+        values = jnp.where(chosen, ref[h : h + 1, :].astype(F32), 0.0)
+        total = total + jnp.sum(values, axis=1, keepdims=True)
+    return total.astype(jnp.int32), which
+
+
+def finish_kernel(count, share, tag_ref, listed_ref, events_ref, w_out_ref, *refs):
     parts = refs[: 2 * count]
     layer_ref, keep_ref, send_ref, matrix, matrix_sem = refs[2 * count :]
     copy = pltpu.make_async_copy(w_out_ref, matrix, matrix_sem)
@@ -192,17 +207,20 @@
     layer_ref[...] = layer.reshape(hist, here, width)
     column = lax.broadcasted_iota(jnp.int32, (1, rows), 1)
     for side, out_ref in ((0, keep_ref), (1, send_ref)):
-        pick = (listed_ref[side] == column).astype(BF)
+        at, which = column_of(listed_ref, core ^ side, share, out_ref.shape[0])
+        local = at - (2 * tag_ref[1] + core) * here
+        inside = (local >= 0) & (local < here)
+        pick = (jnp.where(inside, local + which * here, -1) == column).astype(BF)
         out_ref[...] = jnp.dot(pick, layer, preferred_element_type=F32).astype(BF)
 
 
-def finish(tag, listed, events, w_out, keeps, received):
+def finish(tag, listed, events, w_out, keeps, received, share):
     hist, here, width = events.shape
-    rows = listed.shape[1]
+    rows = listed.size // 2
     vmem = pl.BlockSpec(memory_space=pltpu.VMEM)
     smem = pl.BlockSpec(memory_space=pltpu.SMEM)
     return pl.pallas_call(
-        functools.partial(finish_kernel, len(keeps)),
+        functools.partial(finish_kernel, len(keeps), share),
         out_shape=(
             jax.ShapeDtypeStruct((hist, here, width), BF),
             jax.ShapeDtypeStruct((rows, width), BF),
@@ -219,29 +237,38 @@
     )(tag, listed, events, w_out, *keeps, *received)
 
 
-def score_kernel(sources, tag_ref, base_ref, rows_ref, more_ref, label_ref, *refs):
+def score_kernel(sources, chip_size, batch, tag_ref, rows_ref, more_ref, label_ref, listed_ref, *refs):
     tables = refs[:sources]
     outs = refs[sources:-2]
     total, shares = refs[-2:]
     rows = rows_ref[...] + more_ref[...]
-    label = label_ref[...]
+    share, hist, _ = outs[0].shape
+    label, _ = column_of(label_ref, tag_ref[2], share, rows.shape[0])
+    listed, _ = column_of(listed_ref, tag_ref[2], share, rows.shape[0])
+    here = ((listed & chip_size) > 0) == ((tag_ref[1] & 1) > 0)
     scale = D ** (-0.5)
     total[...] = jnp.zeros_like(total)
     which = 0
-    for ref in tables:
+    for number, ref in enumerate(tables):
         per = ref.shape[0]
+        other = int(number >= sources // 2)
+        if number == sources // 2:
+            which = 0
         items = ref.shape[1] - PAD
 
-        def one(i, which=which, ref=ref, items=items):
+        def one(i, which=which, ref=ref, items=items, other=other):
+            owner = (2 * tag_ref[1] + tag_ref[2]) ^ (other + 2 * ((which + i) & 1))
+            base = (owner * batch + (((which + i) >> 1) ^ tag_ref[0])) * items
             table = ref[i, :items, :]
             bias = ref[i, items : items + 1, :items].astype(F32)
             logits = lax.dot_general(
                 rows, table, (((1,), (1,)), ((), ())), preferred_element_type=F32
             )
             logits = logits * scale + bias
-            ids = base_ref[which + i] + lax.broadcasted_iota(jnp.int32, (1, items), 1)
+            ids = base + lax.broadcasted_iota(jnp.int32, (1, items), 1)
             target = (label == ids).astype(F32)
-            coef = (1.0 / (1.0 + jnp.exp(-logits)) - target).astype(BF)
+            coef = 1.0 / (1.0 + jnp.exp(-logits)) - target
+            coef = jnp.where(here, coef, 0.0).astype(BF)
             total[...] += jnp.dot(coef, table, preferred_element_type=F32)
 
         if per <= 4:
@@ -251,7 +278,6 @@
             pl.loop(0, per)(one)
         which += per
     count = len(outs)
-    share, hist, _ = outs[0].shape
     for chip in range(count):
         for at in range(share):
             first = (chip * share + at) * hist
@@ -260,7 +286,7 @@
         out[...] = shares[lax.rem(tag_ref[1] + step, count)].astype(out.dtype)
 
 
-def score(tag, bases, rows, more, labels, tables, chips, hist):
+def score(tag, rows, more, labels, listed, tables, chips, hist, chip_size, batch):
     count, width = rows.shape
     share = count // chips // hist
     vmem = pl.BlockSpec(memory_space=pltpu.VMEM)
@@ -268,9 +294,9 @@
     own = jax.ShapeDtypeStruct((share, hist, width), F32)
     part = jax.ShapeDtypeStruct((share, hist, width), F32)
     return pl.pallas_call(
-        functools.partial(score_kernel, len(tables)),
+        functools.partial(score_kernel, len(tables), chip_size, batch),
         out_shape=(own,) + (part,) * (chips - 1),
-        in_specs=[smem, smem] + [vmem] * (3 + len(tables)),
+        in_specs=[smem] + [vmem] * (4 + len(tables)),
         out_specs=(vmem,) * chips,
         scratch_shapes=[
             pltpu.VMEM((count, width), F32),
@@ -281,7 +307,7 @@
             flops=4 * count * width * 1024, bytes_accessed=3 * 1024 * 1024, transcendentals=count * 1024
         ),
         name="score",
-    )(tag, bases, rows, more, labels, *tables)
+    )(tag, rows, more, labels, listed, *tables)
 
 
 def on_device(events, w_in, w_out, item_table, item_bias, segment_lengths, listed_pos, labels):
@@ -355,30 +381,9 @@
         received.append(swap(send))
 
     share = listed_pos.shape[0] // seq
-    local = listed_pos - rank * here
-    inside = (local >= 0) & (local < here)
-    index = jnp.where(inside, local + here * jnp.arange(hist, dtype=jnp.int32)[None, :], -1)
-
-    def halves(value):
-        value = value.reshape(chips, 2, share, hist).transpose(1, 0, 2, 3)
-        return value.reshape(2, chips * share * hist, 1)
-
-    index = halves(index)
-    index = jnp.where(core == 0, index, index[::-1])
-    own_labels = halves(labels)
-    own_labels = jnp.where(core == 0, own_labels[0], own_labels[1])
-    layer_out, rows, rows_send = finish(tag, index, events, w_out, keeps, received)
-    rows = rows + swap(rows_send)
-    step = 1
-    near, more = rows, jnp.zeros_like(rows)
-    while step < chips:
-        if step > 1:
-            rows = near = rows + more
-        more = lax.ppermute(rows, "seq", [(i, i ^ (2 * step)) for i in range(seq)])
-        step *= 2
+    listed, wanted = listed_pos.T, labels.T
 
     items = item_table.shape[0]
-    item_table, _ = lax.optimization_barrier((item_table, window[-1]))
     padded = jnp.concatenate(
         [
             item_table,
@@ -386,19 +391,32 @@
         ],
         0,
     )
+    paired = lax.ppermute(padded, "seq", [(i, i ^ 2) for i in range(seq)])
+    both = jnp.stack([padded, paired])
     if grid:
-        tables = [padded, across(padded, 1), across(padded, 2), across(padded, 3)]
-        tables, _ = lax.optimization_barrier((tables, near))
-        tables = [piece[None] for piece in tables]
-        holder = mine ^ jnp.arange(4, dtype=jnp.int32)
+        both, _ = lax.optimization_barrier((both, (top, bottom)))
+        tables = [both, across(both, 1), across(both, 2), across(both, 3)]
+        ready, _ = lax.optimization_barrier((tag, tables[1:3]))
     else:
-        tables = [lax.all_gather(padded[None], "batch", axis=0, tiled=True)]
-        holder = jnp.arange(batch, dtype=jnp.int32)
+        tables = [lax.all_gather(both, "batch", axis=0, tiled=True)]
+        ready = tag
+
+    layer_out, rows, rows_send = finish(ready, listed, events, w_out, keeps, received, share)
+    rows = rows + swap(rows_send)
+    if grid:
+        tables[:3], _ = lax.optimization_barrier((tables[:3], rows))
+    more = jnp.zeros_like(rows)
+    step = 2
+    while step < chips:
+        if step > 2:
+            rows = rows + more
+        more = lax.ppermute(rows, "seq", [(i, i ^ (2 * step)) for i in range(seq)])
+        step *= 2
+    if grid:
+        tables[3], more = lax.optimization_barrier((tables[3], more))
     tables = tables + [swap(piece) for piece in tables]
-    bases = jnp.concatenate(
-        [(rank * batch + holder) * items, ((rank ^ 1) * batch + holder) * items]
-    )
-    parts = score(tag, bases, rows, more, own_labels, tables, chips, hist)
+
+    parts = score(tag, rows, more, wanted, listed, tables, chips, hist, 2 * here, batch)
     total = parts[0]
     for step in range(1, chips):
         arrived = lax.ppermute(

time: 101 us -> 94.5 us (0.936)
  waiting for transfers between devices: 39.7 us -> 36 us
  starting transfers between devices: 33.9 us -> 32.2 us
  local copies, waits for them, and re-layouts: 6.93 us -> 5.24 us
    ppermute x0 -> x1, waiting for transfers between devices: none -> 9.09 us  [on_device(): paired = lax.ppermute(padded, 'seq', [(i, i ^ 2) for i in range(seq)])]
    ppermute x2 -> x1, waiting for transfers between devices: 10.2 us -> 3.93 us  [on_device(): more = lax.ppermute(rows, 'seq', [(i, i ^ 2 * step) for i in range(seq)])]
    ppermute x7, waiting for transfers between devices: 10.4 us -> 4.28 us  [across(): return lax.ppermute(value, 'batch', [(i, i ^ bit) for i in range(batch)])]
    ppermute x2 -> x1, starting transfers between devices: 7.18 us -> 4.66 us  [on_device(): more = lax.ppermute(rows, 'seq', [(i, i ^ 2 * step) for i in range(seq)])]
    ppermute x9, waiting for transfers between devices: 1.36 us -> 3.81 us  [swap(): return lax.ppermute(value, 'seq', [(i, i ^ 1) for i in range(seq)])]
    ppermute x2, waiting for transfers between devices: 11.9 us -> 10.1 us  [ahead(): lax.ppermute(value, 'seq', [(i, i + 2 * by) for i in range(seq - 2 * by)])]
    ppermute x3, waiting for transfers between devices: 5.86 us -> 4.76 us  [on_device(): lax.ppermute(parts[step], 'seq', [(i, (i + 2 * step) % seq) for i in rang...]
  transfers between devices with their start and end apart: 23 -> 23, of which waited for: 10 -> 11; matrix products, arithmetic and copies ran while one was open for 3% -> 2% of each run, Pallas kernels for 3% -> 15%
where the time goes in v4:
time: 94.5 us; the launch traced here: 93.9 us
  waiting for transfers between devices  36 us (38%)
  starting transfers between devices  32.2 us (34%)
  Pallas kernels  18.2 us (19%)
  local copies, waits for them, and re-layouts  5.24 us (6%)
  other arithmetic  1.43 us (2%)
    ppermute x7, starting transfers between devices, across(): return lax.ppermute(value, 'batch', [(i, i ^ bit) for i in range(batch)])  11.4 us
    pallas_call x1, Pallas kernels, attend(): pl.pallas_call(functools.partial(attend_kernel, blocks, split), out_shape...  11.3 us
    ppermute x2, waiting for transfers between devices, ahead(): lax.ppermute(value, 'seq', [(i, i + 2 * by) for i in range(seq - 2 * by)])  10.1 us
    ppermute x2, starting transfers between devices, ahead(): lax.ppermute(value, 'seq', [(i, i + 2 * by) for i in range(seq - 2 * by)])  9.44 us
    ppermute x1, waiting for transfers between devices, on_device(): paired = lax.ppermute(padded, 'seq', [(i, i ^ 2) for i in range(seq)])  9.09 us
    ppermute x3, waiting for transfers between devices, on_device(): lax.ppermute(parts[step], 'seq', [(i, (i + 2 * step) % seq) for i in rang...  4.76 us
    ppermute x1, starting transfers between devices, on_device(): more = lax.ppermute(rows, 'seq', [(i, i ^ 2 * step) for i in range(seq)])  4.66 us
    ppermute x3, starting transfers between devices, on_device(): lax.ppermute(parts[step], 'seq', [(i, (i + 2 * step) % seq) for i in rang...  4.55 us
  transfers between devices with their start and end apart: 23, of which 11 were waited for; matrix products, arithmetic and copies ran while one was open for 2% of the time, Pallas kernels for 15%

profile of v4, /device:TPU:0, one launch (start us, length us, event | category | flops | bytes accessed | tf_op | source)
XLA Modules:
  0.0 93.9 jit_solution(7397082383801330184)
XLA Ops:
  0.7 1.5 %copy-done = bf16[1024,1024]{1,0:T(8,128)(2,1)S(1)} copy-done((bf16[1024,1024]{1,0:T(8,128)(2,1)S(1)}, bf16[1024,1024]{1,0:T(8,128)(2,1)}, u32[]{:S(2)}) %copy-start) | copy-done | bytes 2097176
  2.3 3.0 %collective-permute-start.1 = (bf16[1024,512]{1,0:T(8,128)(2,1)S(1)}, bf16[1024,512]{1,0:T(8,128)(2,1)S(1)}, u32[]{:S(2)}, u32[]{:S(2)}) collective-permute-start(bf16[1024,512]{1,0:T(8,128)(2,1)S(1)} %constant_dynamic-slice_fusion.refs_6_), channel_id=1, source_target_pairs={{0,2},{1,3},{2,0},{3,1},{4,6},{5,7},{6,4},{7,5},{8,10},{9,11},{10,... | collective-permute-start | bytes 3145736 | tf_op jit(solution)/shard_map/ppermute | solution.py:327
  5.4 1.5 %collective-permute-start.3 = (bf16[1024,512]{1,0:T(8,128)(2,1)S(1)}, bf16[1024,512]{1,0:T(8,128)(2,1)S(1)}, u32[]{:S(2)}, u32[]{:S(2)}) collective-permute-start(bf16[1024,512]{1,0:T(8,128)(2,1)S(1)} %constant_dynamic-slice_fusion.refs_6_), channel_id=1, source_target_pairs={{0,1},{1,0},{2,3},{3,2},{4,5},{5,4},{6,7},{7,6},{8,9},{9,8},{10,11... | collective-permute-start | bytes 3145736 | tf_op jit(solution)/shard_map/ppermute | solution.py:327
  6.9 4.3 %collective-permute-start.7 = (bf16[2,128,1024]{2,1,0:T(8,128)(2,1)}, bf16[2,128,1024]{2,1,0:T(8,128)(2,1)}, u32[]{:S(2)}, u32[]{:S(2)}) collective-permute-start(bf16[2,128,1024]{2,1,0:T(8,128)(2,1)} %events_ref.1), channel_id=1, source_target_pairs={{0,8},{4,12},{8,16},{12,20},{16,24},{20,28},{1,9},{5,13},{9,17},{1... | collective-permute-start | bytes 1572872 | tf_op jit(solution)/shard_map/ppermute | solution.py:330
  11.1 10.1 %collective-permute-done.7.refs_2_ = bf16[2,128,1024]{2,1,0:T(8,128)(2,1)} collective-permute-done((bf16[2,128,1024]{2,1,0:T(8,128)(2,1)}, bf16[2,128,1024]{2,1,0:T(8,128)(2,1)}, u32[]{:S(2)}, u32[]{:S(2)}) %collective-permute-start.7) | collective-permute-done | bytes 524320 | tf_op jit(solution)/shard_map/ppermute | solution.py:330
  21.3 5.2 %collective-permute-start.10 = (bf16[2,128,1024]{2,1,0:T(8,128)(2,1)}, bf16[2,128,1024]{2,1,0:T(8,128)(2,1)}, u32[]{:S(2)}, u32[]{:S(2)}) collective-permute-start(bf16[2,128,1024]{2,1,0:T(8,128)(2,1)} %collective-permute-done.7.refs_2_), channel_id=1, source_target_pairs={{0,8},{4,12},{8,16},{12,20},{16,24},{20,28},{1,9},{5,13},{9,17},{1... | collective-permute-start | bytes 1572872 | tf_op jit(solution)/shard_map/ppermute | solution.py:330
  27.4 1.2 %collective-permute-done.1.refs_8_ = bf16[1024,512]{1,0:T(8,128)(2,1)S(1)} collective-permute-done((bf16[1024,512]{1,0:T(8,128)(2,1)S(1)}, bf16[1024,512]{1,0:T(8,128)(2,1)S(1)}, u32[]{:S(2)}, u32[]{:S(2)}) %collective-permute-start.1) | collective-permute-done | bytes 1048608 | tf_op jit(solution)/shard_map/ppermute | solution.py:327
  28.6 1.8 %collective-permute-start.2 = (bf16[512,512]{1,0:T(8,128)(2,1)S(1)}, bf16[512,512]{1,0:T(8,128)(2,1)}, u32[]{:S(2)}, u32[]{:S(2)}) collective-permute-start(bf16[512,512]{1,0:T(8,128)(2,1)S(1)} %slice.8), channel_id=1, source_target_pairs={{0,1},{1,0},{2,3},{3,2},{4,5},{5,4},{6,7},{7,6},{8,9},{9,8},{10,11... | collective-permute-start | bytes 1572872 | tf_op jit(solution)/shard_map/ppermute | solution.py:327
  31.2 1.5 %collective-permute-start.4 = (bf16[512,512]{1,0:T(8,128)(2,1)}, bf16[512,512]{1,0:T(8,128)(2,1)}, u32[]{:S(2)}, u32[]{:S(2)}) collective-permute-start(bf16[512,512]{1,0:T(8,128)(2,1)} %slice.9), channel_id=1, source_target_pairs={{0,2},{1,3},{2,0},{3,1},{4,6},{5,7},{6,4},{7,5},{8,10},{9,11},{10,... | collective-permute-start | bytes 1572872 | tf_op jit(solution)/shard_map/ppermute | solution.py:327
  32.8 9.1 %collective-permute-done = bf16[144,1024]{1,0:T(8,128)(2,1)S(1)} collective-permute-done((bf16[144,1024]{1,0:T(8,128)(2,1)S(1)}, bf16[144,1024]{1,0:T(8,128)(2,1)S(1)}, u32[]{:S(2)}, u32[]{:S(2)}) %collective-permute-start) | collective-permute-done | bytes 294944 | tf_op jit(solution)/shard_map/ppermute | solution.py:394
  44.1 1.1 %collective-permute-start.5 = (bf16[2,144,1024]{2,1,0:T(8,128)(2,1)S(1)}, bf16[2,144,1024]{2,1,0:T(8,128)(2,1)S(1)}, u32[]{:S(2)}, u32[]{:S(2)}) collective-permute-start(bf16[2,144,1024]{2,1,0:T(8,128)(2,1)S(1)} %pad_maximum_fusion.refs_0_), channel_id=1, source_target_pairs={{0,1},{1,0},{2,3},{3,2},{4,5},{5,4},{6,7},{7,6},{8,9},{9,8},{10,11... | collective-permute-start | bytes 1769480 | tf_op jit(solution)/shard_map/ppermute | solution.py:327
  46.1 11.3 %attend.1 = (bf16[2,2,128,512]{3,2,1,0:T(8,128)(2,1)}, bf16[2,2,128,512]{3,2,1,0:T(8,128)(2,1)}) custom-call(s32[3]{0:T(128)} %pad_add_fusion.tag_ref, s32[2,8]{1,0:T(2,128)} %seg_ref.1, bf16[2,128,1024]{2,1,0:T(8,128)(2,1)} %events_ref.1, bf16[2,128,1024]{2,1,0:T(8,128)(2,1)} %collective-permute-done.8.refs_1_, ...), custom_call_target="tpu_custom_call" | custom-call | flops 5905580032 | bytes 4194304 | tf_op jit(solution)/shard_map/attend/pallas_call | solution.py:141
  57.5 1.5 %collective-permute-start.14 = (bf16[2,144,1024]{2,1,0:T(8,128)(2,1)S(1)}, bf16[2,144,1024]{2,1,0:T(8,128)(2,1)S(1)}, u32[]{:S(2)}, u32[]{:S(2)}) collective-permute-start(bf16[2,144,1024]{2,1,0:T(8,128)(2,1)S(1)} %pad_maximum_fusion.refs_0_), channel_id=1, source_target_pairs={{0,3},{1,2},{2,1},{3,0},{4,7},{5,6},{6,5},{7,4},{8,11},{9,10},{10,... | collective-permute-start | bytes 1769480 | tf_op jit(solution)/shard_map/ppermute | solution.py:327
  59.7 1.6 %copy-done.1 = bf16[1024,1024]{1,0:T(8,128)(2,1)S(1)} copy-done((bf16[1024,1024]{1,0:T(8,128)(2,1)S(1)}, bf16[1024,1024]{1,0:T(8,128)(2,1)}, u32[]{:S(2)}) %copy-start.1) | copy-done | bytes 2097176
  61.3 1.0 %copy-done.2 = bf16[2,2,128,512]{3,2,1,0:T(8,128)(2,1)S(1)} copy-done((bf16[2,2,128,512]{3,2,1,0:T(8,128)(2,1)S(1)}, bf16[2,2,128,512]{3,2,1,0:T(8,128)(2,1)}, u32[]{:S(2)}) %copy-start.2) | copy-done | bytes 524312
  62.3 3.1 %finish.1 = (bf16[2,128,1024]{2,1,0:T(8,128)(2,1)}, bf16[64,1024]{1,0:T(8,128)(2,1)S(1)}, bf16[64,1024]{1,0:T(8,128)(2,1)S(1)}) custom-call(s32[3]{0:T(128)S(1)} %copy-done.3, s32[2,64]{1,0:T(2,128)S(1)} %bitcast.15, bf16[2,128,1024]{2,1,0:T(8,128)(2,1)} %events_ref.1, bf16[1024,1024]{1,0:T(8,128)(2,1)S(1)} %copy-done.1, ...), custom_call_target="tpu_custom_call" | custom-call | flops 536870912 | bytes 5242880 | tf_op jit(solution)/shard_map/finish/pallas_call | solution.py:222
  65.6 1.2 %collective-permute-done.13 = bf16[64,1024]{1,0:T(8,128)(2,1)S(1)} collective-permute-done((bf16[64,1024]{1,0:T(8,128)(2,1)S(1)}, bf16[64,1024]{1,0:T(8,128)(2,1)S(1)}, u32[]{:S(2)}, u32[]{:S(2)}) %collective-permute-start.13) | collective-permute-done | bytes 131104 | tf_op jit(solution)/shard_map/ppermute | solution.py:324
  66.8 4.7 %collective-permute-start.15 = (bf16[64,1024]{1,0:T(8,128)(2,1)S(1)}, bf16[64,1024]{1,0:T(8,128)(2,1)S(1)}, u32[]{:S(2)}, u32[]{:S(2)}) collective-permute-start(bf16[64,1024]{1,0:T(8,128)(2,1)S(1)} %add.24.rows_ref), channel_id=1, source_target_pairs={{0,16},{4,20},{8,24},{12,28},{16,0},{20,4},{24,8},{28,12},{1,17},{... | collective-permute-start | bytes 393224 | tf_op jit(solution)/shard_map/ppermute | solution.py:413
  72.0 2.2 %collective-permute-done.14.refs_3_ = bf16[2,144,1024]{2,1,0:T(8,128)(2,1)S(1)} collective-permute-done((bf16[2,144,1024]{2,1,0:T(8,128)(2,1)S(1)}, bf16[2,144,1024]{2,1,0:T(8,128)(2,1)S(1)}, u32[]{:S(2)}, u32[]{:S(2)}) %collective-permute-start.14) | collective-permute-done | bytes 589856 | tf_op jit(solution)/shard_map/ppermute | solution.py:327
  74.2 3.9 %collective-permute-done.15.more_ref = bf16[64,1024]{1,0:T(8,128)(2,1)S(1)} collective-permute-done((bf16[64,1024]{1,0:T(8,128)(2,1)S(1)}, bf16[64,1024]{1,0:T(8,128)(2,1)S(1)}, u32[]{:S(2)}, u32[]{:S(2)}) %collective-permute-start.15) | collective-permute-done | bytes 131104 | tf_op jit(solution)/shard_map/ppermute | solution.py:413
  78.1 2.0 %collective-permute-done.19.refs_7_ = bf16[2,144,1024]{2,1,0:T(8,128)(2,1)S(1)} collective-permute-done((bf16[2,144,1024]{2,1,0:T(8,128)(2,1)S(1)}, bf16[2,144,1024]{2,1,0:T(8,128)(2,1)S(1)}, u32[]{:S(2)}, u32[]{:S(2)}) %collective-permute-start.19) | collective-permute-done | bytes 589856 | tf_op jit(solution)/shard_map/ppermute | solution.py:324
  80.1 3.8 %score.1 = (f32[8,2,1024]{2,1,0:T(2,128)S(1)}, f32[8,2,1024]{2,1,0:T(2,128)S(1)}, f32[8,2,1024]{2,1,0:T(2,128)S(1)}, f32[8,2,1024]{2,1,0:T(2,128)S(1)}) custom-call(s32[3]{0:T(128)S(1)} %copy-done.3, bf16[64,1024]{1,0:T(8,128)(2,1)S(1)} %add.24.rows_ref, bf16[64,1024]{1,0:T(8,128)(2,1)S(1)} %collective-permute-done.15.more_ref, s32[2,64]{1,0:T(2,128)S(1)} %bitcast.17, ...), custom_call_target="tpu_custom_call" | custom-call | flops 268435456 | bytes 3145728 | tf_op jit(solution)/shard_map/score/pallas_call | solution.py:296
  84.7 3.4 %collective-permute-start.20 = (f32[8,2,1024]{2,1,0:T(2,128)S(1)}, f32[8,2,1024]{2,1,0:T(2,128)S(1)}, u32[]{:S(2)}, u32[]{:S(2)}) collective-permute-start(f32[8,2,1024]{2,1,0:T(2,128)S(1)} %get-tuple-element.35), channel_id=1, source_target_pairs={{0,8},{4,12},{8,16},{12,20},{16,24},{20,28},{24,0},{28,4},{1,9},{5... | collective-permute-start | bytes 196616 | tf_op jit(solution)/shard_map/ppermute | solution.py:422
  88.5 4.0 %collective-permute-done.21 = f32[8,2,1024]{2,1,0:T(2,128)S(1)} collective-permute-done((f32[8,2,1024]{2,1,0:T(2,128)S(1)}, f32[8,2,1024]{2,1,0:T(2,128)S(1)}, u32[]{:S(2)}, u32[]{:S(2)}) %collective-permute-start.21) | collective-permute-done | bytes 65568 | tf_op jit(solution)/shard_map/ppermute | solution.py:422
  (55 shorter events, 9.1 us)
Async XLA Ops:
  0.6 25.8 %copy-start.10 = (bf16[128]{0:T(256)(128)(2,1)S(1)}, bf16[128]{0:T(256)(128)(2,1)}, u32[]{:S(2)}) copy-start(bf16[128]{0:T(256)(128)(2,1)} %param.12) | copy-start | bytes 772
  2.3 26.2 %collective-permute-start.1 = (bf16[1024,512]{1,0:T(8,128)(2,1)S(1)}, bf16[1024,512]{1,0:T(8,128)(2,1)S(1)}, u32[]{:S(2)}, u32[]{:S(2)}) collective-permute-start(bf16[1024,512]{1,0:T(8,128)(2,1)S(1)} %constant_dynamic-slice_fusion.refs_6_), channel_id=1, source_target_pairs={{0,2},{1,3},{2,0},{3,1},{4,6},{5,7},{6,4},{7,5},{8,10},{9,11},{10,... | collective-permute-start | bytes 3145736 | tf_op jit(solution)/shard_map/ppermute | solution.py:327
  5.4 25.0 %collective-permute-start.3 = (bf16[1024,512]{1,0:T(8,128)(2,1)S(1)}, bf16[1024,512]{1,0:T(8,128)(2,1)S(1)}, u32[]{:S(2)}, u32[]{:S(2)}) collective-permute-start(bf16[1024,512]{1,0:T(8,128)(2,1)S(1)} %constant_dynamic-slice_fusion.refs_6_), channel_id=1, source_target_pairs={{0,1},{1,0},{2,3},{3,2},{4,5},{5,4},{6,7},{7,6},{8,9},{9,8},{10,11... | collective-permute-start | bytes 3145736 | tf_op jit(solution)/shard_map/ppermute | solution.py:327
  6.9 14.4 %collective-permute-start.7 = (bf16[2,128,1024]{2,1,0:T(8,128)(2,1)}, bf16[2,128,1024]{2,1,0:T(8,128)(2,1)}, u32[]{:S(2)}, u32[]{:S(2)}) collective-permute-start(bf16[2,128,1024]{2,1,0:T(8,128)(2,1)} %events_ref.1), channel_id=1, source_target_pairs={{0,8},{4,12},{8,16},{12,20},{16,24},{20,28},{1,9},{5,13},{9,17},{1... | collective-permute-start | bytes 1572872 | tf_op jit(solution)/shard_map/ppermute | solution.py:330
  21.3 20.6 %collective-permute-start.10 = (bf16[2,128,1024]{2,1,0:T(8,128)(2,1)}, bf16[2,128,1024]{2,1,0:T(8,128)(2,1)}, u32[]{:S(2)}, u32[]{:S(2)}) collective-permute-start(bf16[2,128,1024]{2,1,0:T(8,128)(2,1)} %collective-permute-done.7.refs_2_), channel_id=1, source_target_pairs={{0,8},{4,12},{8,16},{12,20},{16,24},{20,28},{1,9},{5,13},{9,17},{1... | collective-permute-start | bytes 1572872 | tf_op jit(solution)/shard_map/ppermute | solution.py:330
  26.5 15.4 %collective-permute-start = (bf16[144,1024]{1,0:T(8,128)(2,1)S(1)}, bf16[144,1024]{1,0:T(8,128)(2,1)S(1)}, u32[]{:S(2)}, u32[]{:S(2)}) collective-permute-start(bf16[144,1024]{1,0:T(8,128)(2,1)S(1)} %get-tuple-element.39), channel_id=1, source_target_pairs={{0,8},{4,12},{8,0},{12,4},{16,24},{20,28},{24,16},{28,20},{1,9},{5... | collective-permute-start | bytes 884744 | tf_op jit(solution)/shard_map/ppermute | solution.py:394
  28.6 14.5 %collective-permute-start.2 = (bf16[512,512]{1,0:T(8,128)(2,1)S(1)}, bf16[512,512]{1,0:T(8,128)(2,1)}, u32[]{:S(2)}, u32[]{:S(2)}) collective-permute-start(bf16[512,512]{1,0:T(8,128)(2,1)S(1)} %slice.8), channel_id=1, source_target_pairs={{0,1},{1,0},{2,3},{3,2},{4,5},{5,4},{6,7},{7,6},{8,9},{9,8},{10,11... | collective-permute-start | bytes 1572872 | tf_op jit(solution)/shard_map/ppermute | solution.py:327
  31.2 12.8 %collective-permute-start.4 = (bf16[512,512]{1,0:T(8,128)(2,1)}, bf16[512,512]{1,0:T(8,128)(2,1)}, u32[]{:S(2)}, u32[]{:S(2)}) collective-permute-start(bf16[512,512]{1,0:T(8,128)(2,1)} %slice.9), channel_id=1, source_target_pairs={{0,2},{1,3},{2,0},{3,1},{4,6},{5,7},{6,4},{7,5},{8,10},{9,11},{10,... | collective-permute-start | bytes 1572872 | tf_op jit(solution)/shard_map/ppermute | solution.py:327
  32.8 13.4 %collective-permute-start.8 = (bf16[2,128,1024]{2,1,0:T(8,128)(2,1)}, bf16[2,128,1024]{2,1,0:T(8,128)(2,1)}, u32[]{:S(2)}, u32[]{:S(2)}) collective-permute-start(bf16[2,128,1024]{2,1,0:T(8,128)(2,1)} %events_ref.1), channel_id=1, source_target_pairs={{0,4},{4,0},{8,12},{12,8},{16,20},{20,16},{24,28},{28,24},{1,5},{5... | collective-permute-start | bytes 1572872 | tf_op jit(solution)/shard_map/ppermute | solution.py:324
  41.9 4.3 %collective-permute-start.9 = (bf16[2,128,1024]{2,1,0:T(8,128)(2,1)}, bf16[2,128,1024]{2,1,0:T(8,128)(2,1)}, u32[]{:S(2)}, u32[]{:S(2)}) collective-permute-start(bf16[2,128,1024]{2,1,0:T(8,128)(2,1)} %collective-permute-done.7.refs_2_), channel_id=1, source_target_pairs={{0,4},{4,0},{8,12},{12,8},{16,20},{20,16},{24,28},{28,24},{1,5},{5... | collective-permute-start | bytes 1572872 | tf_op jit(solution)/shard_map/ppermute | solution.py:324
  41.9 4.3 %collective-permute-start.11 = (bf16[2,128,1024]{2,1,0:T(8,128)(2,1)}, bf16[2,128,1024]{2,1,0:T(8,128)(2,1)}, u32[]{:S(2)}, u32[]{:S(2)}) collective-permute-start(bf16[2,128,1024]{2,1,0:T(8,128)(2,1)} %collective-permute-done.10.refs_4_), channel_id=1, source_target_pairs={{0,4},{4,0},{8,12},{12,8},{16,20},{20,16},{24,28},{28,24},{1,5},{5... | collective-permute-start | bytes 1572872 | tf_op jit(solution)/shard_map/ppermute | solution.py:324
  44.1 15.0 %collective-permute-start.5 = (bf16[2,144,1024]{2,1,0:T(8,128)(2,1)S(1)}, bf16[2,144,1024]{2,1,0:T(8,128)(2,1)S(1)}, u32[]{:S(2)}, u32[]{:S(2)}) collective-permute-start(bf16[2,144,1024]{2,1,0:T(8,128)(2,1)S(1)} %pad_maximum_fusion.refs_0_), channel_id=1, source_target_pairs={{0,1},{1,0},{2,3},{3,2},{4,5},{5,4},{6,7},{7,6},{8,9},{9,8},{10,11... | collective-permute-start | bytes 1769480 | tf_op jit(solution)/shard_map/ppermute | solution.py:327
  45.2 13.9 %collective-permute-start.6 = (bf16[2,144,1024]{2,1,0:T(8,128)(2,1)S(1)}, bf16[2,144,1024]{2,1,0:T(8,128)(2,1)}, u32[]{:S(2)}, u32[]{:S(2)}) collective-permute-start(bf16[2,144,1024]{2,1,0:T(8,128)(2,1)S(1)} %pad_maximum_fusion.refs_0_), channel_id=1, source_target_pairs={{0,2},{1,3},{2,0},{3,1},{4,6},{5,7},{6,4},{7,5},{8,10},{9,11},{10,... | collective-permute-start | bytes 1769480 | tf_op jit(solution)/shard_map/ppermute | solution.py:327
  57.5 2.2 %collective-permute-start.12 = (bf16[2,2,128,512]{3,2,1,0:T(8,128)(2,1)}, bf16[2,2,128,512]{3,2,1,0:T(8,128)(2,1)S(1)}, u32[]{:S(2)}, u32[]{:S(2)}) collective-permute-start(bf16[2,2,128,512]{3,2,1,0:T(8,128)(2,1)} %get-tuple-element.25), channel_id=1, source_target_pairs={{0,4},{4,0},{8,12},{12,8},{16,20},{20,16},{24,28},{28,24},{1,5},{5... | collective-permute-start | bytes 1572872 | tf_op jit(solution)/shard_map/ppermute | solution.py:324
  57.5 16.6 %collective-permute-start.14 = (bf16[2,144,1024]{2,1,0:T(8,128)(2,1)S(1)}, bf16[2,144,1024]{2,1,0:T(8,128)(2,1)S(1)}, u32[]{:S(2)}, u32[]{:S(2)}) collective-permute-start(bf16[2,144,1024]{2,1,0:T(8,128)(2,1)S(1)} %pad_maximum_fusion.refs_0_), channel_id=1, source_target_pairs={{0,3},{1,2},{2,1},{3,0},{4,7},{5,6},{6,5},{7,4},{8,11},{9,10},{10,... | collective-permute-start | bytes 1769480 | tf_op jit(solution)/shard_map/ppermute | solution.py:327
  65.4 1.4 %collective-permute-start.13 = (bf16[64,1024]{1,0:T(8,128)(2,1)S(1)}, bf16[64,1024]{1,0:T(8,128)(2,1)S(1)}, u32[]{:S(2)}, u32[]{:S(2)}) collective-permute-start(bf16[64,1024]{1,0:T(8,128)(2,1)S(1)} %get-tuple-element.28), channel_id=1, source_target_pairs={{0,4},{4,0},{8,12},{12,8},{16,20},{20,16},{24,28},{28,24},{1,5},{5... | collective-permute-start | bytes 393224 | tf_op jit(solution)/shard_map/ppermute | solution.py:324
  66.8 11.3 %collective-permute-start.15 = (bf16[64,1024]{1,0:T(8,128)(2,1)S(1)}, bf16[64,1024]{1,0:T(8,128)(2,1)S(1)}, u32[]{:S(2)}, u32[]{:S(2)}) collective-permute-start(bf16[64,1024]{1,0:T(8,128)(2,1)S(1)} %add.24.rows_ref), channel_id=1, source_target_pairs={{0,16},{4,20},{8,24},{12,28},{16,0},{20,4},{24,8},{28,12},{1,17},{... | collective-permute-start | bytes 393224 | tf_op jit(solution)/shard_map/ppermute | solution.py:413
  71.5 6.6 %collective-permute-start.16 = (bf16[2,144,1024]{2,1,0:T(8,128)(2,1)S(1)}, bf16[2,144,1024]{2,1,0:T(8,128)(2,1)S(1)}, u32[]{:S(2)}, u32[]{:S(2)}) collective-permute-start(bf16[2,144,1024]{2,1,0:T(8,128)(2,1)S(1)} %pad_maximum_fusion.refs_0_), channel_id=1, source_target_pairs={{0,4},{4,0},{8,12},{12,8},{16,20},{20,16},{24,28},{28,24},{1,5},{5... | collective-permute-start | bytes 1769480 | tf_op jit(solution)/shard_map/ppermute | solution.py:324
  71.5 6.6 %collective-permute-start.17 = (bf16[2,144,1024]{2,1,0:T(8,128)(2,1)S(1)}, bf16[2,144,1024]{2,1,0:T(8,128)(2,1)S(1)}, u32[]{:S(2)}, u32[]{:S(2)}) collective-permute-start(bf16[2,144,1024]{2,1,0:T(8,128)(2,1)S(1)} %collective-permute-done.5.refs_1_), channel_id=1, source_target_pairs={{0,4},{4,0},{8,12},{12,8},{16,20},{20,16},{24,28},{28,24},{1,5},{5... | collective-permute-start | bytes 1769480 | tf_op jit(solution)/shard_map/ppermute | solution.py:324
  72.0 6.1 %collective-permute-start.18 = (bf16[2,144,1024]{2,1,0:T(8,128)(2,1)}, bf16[2,144,1024]{2,1,0:T(8,128)(2,1)S(1)}, u32[]{:S(2)}, u32[]{:S(2)}) collective-permute-start(bf16[2,144,1024]{2,1,0:T(8,128)(2,1)} %collective-permute-done.6.refs_2_), channel_id=1, source_target_pairs={{0,4},{4,0},{8,12},{12,8},{16,20},{20,16},{24,28},{28,24},{1,5},{5... | collective-permute-start | bytes 1769480 | tf_op jit(solution)/shard_map/ppermute | solution.py:324
  78.1 2.0 %collective-permute-start.19 = (bf16[2,144,1024]{2,1,0:T(8,128)(2,1)S(1)}, bf16[2,144,1024]{2,1,0:T(8,128)(2,1)S(1)}, u32[]{:S(2)}, u32[]{:S(2)}) collective-permute-start(bf16[2,144,1024]{2,1,0:T(8,128)(2,1)S(1)} %collective-permute-done.14.refs_3_), channel_id=1, source_target_pairs={{0,4},{4,0},{8,12},{12,8},{16,20},{20,16},{24,28},{28,24},{1,5},{5... | collective-permute-start | bytes 1769480 | tf_op jit(solution)/shard_map/ppermute | solution.py:324
  84.0 8.6 %collective-permute-start.21 = (f32[8,2,1024]{2,1,0:T(2,128)S(1)}, f32[8,2,1024]{2,1,0:T(2,128)S(1)}, u32[]{:S(2)}, u32[]{:S(2)}) collective-permute-start(f32[8,2,1024]{2,1,0:T(2,128)S(1)} %get-tuple-element.36), channel_id=1, source_target_pairs={{0,16},{4,20},{8,24},{12,28},{16,0},{20,4},{24,8},{28,12},{1,17},{... | collective-permute-start | bytes 196616 | tf_op jit(solution)/shard_map/ppermute | solution.py:422
  84.7 7.8 %collective-permute-start.20 = (f32[8,2,1024]{2,1,0:T(2,128)S(1)}, f32[8,2,1024]{2,1,0:T(2,128)S(1)}, u32[]{:S(2)}, u32[]{:S(2)}) collective-permute-start(f32[8,2,1024]{2,1,0:T(2,128)S(1)} %get-tuple-element.35), channel_id=1, source_target_pairs={{0,8},{4,12},{8,16},{12,20},{16,24},{20,28},{24,0},{28,4},{1,9},{5... | collective-permute-start | bytes 196616 | tf_op jit(solution)/shard_map/ppermute | solution.py:422
  88.1 5.1 %collective-permute-start.22 = (f32[8,2,1024]{2,1,0:T(2,128)S(1)}, f32[8,2,1024]{2,1,0:T(2,128)S(1)}, u32[]{:S(2)}, u32[]{:S(2)}) collective-permute-start(f32[8,2,1024]{2,1,0:T(2,128)S(1)} %get-tuple-element.37), channel_id=1, source_target_pairs={{0,24},{4,28},{8,0},{12,4},{16,8},{20,12},{24,16},{28,20},{1,25},{... | collective-permute-start | bytes 196616 | tf_op jit(solution)/shard_map/ppermute | solution.py:422
  (10 other events, 134.7 us)

commit v5 on v4

--- a/solution.py
+++ b/solution.py
@@ -152,7 +152,7 @@
             pltpu.SemaphoreType.DMA((blocks,)),
             pltpu.SemaphoreType.DMA((len(split),)),
         ],
-        compiler_params=pltpu.CompilerParams(vmem_limit_bytes=60 * MIB),
+        compiler_params=pltpu.CompilerParams(vmem_limit_bytes=57 * MIB),
         cost_estimate=pl.CostEstimate(
             flops=flops, bytes_accessed=4 * 1024 * 1024, transcendentals=hist * here * 2 * here * blocks * cols // HD
         ),

time: 94.5 us -> 92.2 us (0.976)
  local copies, waits for them, and re-layouts: 5.24 us -> 2.8 us
  other arithmetic: 1.43 us -> 2.41 us
    unnamed x22, local copies, waits for them, and re-layouts: 4.22 us -> 2.63 us
    ppermute x1, waiting for transfers between devices: 3.93 us -> 2.69 us  [on_device(): more = lax.ppermute(rows, 'seq', [(i, i ^ 2 * step) for i in range(seq)])]
    ppermute x7, waiting for transfers between devices: 4.28 us -> 5.25 us  [across(): return lax.ppermute(value, 'batch', [(i, i ^ bit) for i in range(batch)])]
    another operation x2, other arithmetic: 0.09 us -> 1.06 us  [on_device(): both = jnp.stack([padded, paired])]
  transfers between devices with their start and end apart: 23 -> 23, of which waited for: 11 -> 11; matrix products, arithmetic and copies ran while one was open for 2% -> 2% of each run, Pallas kernels for 15% -> 16%
where the time goes in v5:
time: 92.2 us; the launch traced here: 91.9 us
  waiting for transfers between devices  35.8 us (39%)
  starting transfers between devices  32.4 us (35%)
  Pallas kernels  17.6 us (19%)
  local copies, waits for them, and re-layouts  2.8 us (3%)
  other arithmetic  2.41 us (3%)
    ppermute x7, starting transfers between devices, across(): return lax.ppermute(value, 'batch', [(i, i ^ bit) for i in range(batch)])  11.5 us
    pallas_call x1, Pallas kernels, attend(): pl.pallas_call(functools.partial(attend_kernel, blocks, split), out_shape...  11.3 us
    ppermute x2, waiting for transfers between devices, ahead(): lax.ppermute(value, 'seq', [(i, i + 2 * by) for i in range(seq - 2 * by)])  10.1 us
    ppermute x1, waiting for transfers between devices, on_device(): paired = lax.ppermute(padded, 'seq', [(i, i ^ 2) for i in range(seq)])  9.87 us
    ppermute x2, starting transfers between devices, ahead(): lax.ppermute(value, 'seq', [(i, i + 2 * by) for i in range(seq - 2 * by)])  9.47 us
    ppermute x3, starting transfers between devices, on_device(): lax.ppermute(parts[step], 'seq', [(i, (i + 2 * step) % seq) for i in rang...  5.47 us
    ppermute x7, waiting for transfers between devices, across(): return lax.ppermute(value, 'batch', [(i, i ^ bit) for i in range(batch)])  5.25 us
    ppermute x3, waiting for transfers between devices, on_device(): lax.ppermute(parts[step], 'seq', [(i, (i + 2 * step) % seq) for i in rang...  4.51 us
  transfers between devices with their start and end apart: 23, of which 11 were waited for; matrix products, arithmetic and copies ran while one was open for 2% of the time, Pallas kernels for 16%

profile of v5, /device:TPU:0, one launch (start us, length us, event | category | flops | bytes accessed | tf_op | source)
XLA Modules:
  0.0 91.9 jit_solution(8226269326645610180)
XLA Ops:
  0.7 1.5 %copy-done = bf16[1024,1024]{1,0:T(8,128)(2,1)S(1)} copy-done((bf16[1024,1024]{1,0:T(8,128)(2,1)S(1)}, bf16[1024,1024]{1,0:T(8,128)(2,1)}, u32[]{:S(2)}) %copy-start) | copy-done | bytes 2097176
  2.3 3.0 %collective-permute-start.1 = (bf16[1024,512]{1,0:T(8,128)(2,1)S(1)}, bf16[1024,512]{1,0:T(8,128)(2,1)S(1)}, u32[]{:S(2)}, u32[]{:S(2)}) collective-permute-start(bf16[1024,512]{1,0:T(8,128)(2,1)S(1)} %constant_dynamic-slice_fusion.refs_6_), channel_id=1, source_target_pairs={{0,2},{1,3},{2,0},{3,1},{4,6},{5,7},{6,4},{7,5},{8,10},{9,11},{10,... | collective-permute-start | bytes 3145736 | tf_op jit(solution)/shard_map/ppermute | solution.py:327
  5.4 1.5 %collective-permute-start.3 = (bf16[1024,512]{1,0:T(8,128)(2,1)S(1)}, bf16[1024,512]{1,0:T(8,128)(2,1)S(1)}, u32[]{:S(2)}, u32[]{:S(2)}) collective-permute-start(bf16[1024,512]{1,0:T(8,128)(2,1)S(1)} %constant_dynamic-slice_fusion.refs_6_), channel_id=1, source_target_pairs={{0,1},{1,0},{2,3},{3,2},{4,5},{5,4},{6,7},{7,6},{8,9},{9,8},{10,11... | collective-permute-start | bytes 3145736 | tf_op jit(solution)/shard_map/ppermute | solution.py:327
  6.9 4.3 %collective-permute-start.7 = (bf16[2,128,1024]{2,1,0:T(8,128)(2,1)}, bf16[2,128,1024]{2,1,0:T(8,128)(2,1)}, u32[]{:S(2)}, u32[]{:S(2)}) collective-permute-start(bf16[2,128,1024]{2,1,0:T(8,128)(2,1)} %events_ref.1), channel_id=1, source_target_pairs={{0,8},{4,12},{8,16},{12,20},{16,24},{20,28},{1,9},{5,13},{9,17},{1... | collective-permute-start | bytes 1572872 | tf_op jit(solution)/shard_map/ppermute | solution.py:330
  11.1 10.1 %collective-permute-done.7.refs_2_ = bf16[2,128,1024]{2,1,0:T(8,128)(2,1)} collective-permute-done((bf16[2,128,1024]{2,1,0:T(8,128)(2,1)}, bf16[2,128,1024]{2,1,0:T(8,128)(2,1)}, u32[]{:S(2)}, u32[]{:S(2)}) %collective-permute-start.7) | collective-permute-done | bytes 524320 | tf_op jit(solution)/shard_map/ppermute | solution.py:330
  21.3 5.2 %collective-permute-start.10 = (bf16[2,128,1024]{2,1,0:T(8,128)(2,1)}, bf16[2,128,1024]{2,1,0:T(8,128)(2,1)}, u32[]{:S(2)}, u32[]{:S(2)}) collective-permute-start(bf16[2,128,1024]{2,1,0:T(8,128)(2,1)} %collective-permute-done.7.refs_2_), channel_id=1, source_target_pairs={{0,8},{4,12},{8,16},{12,20},{16,24},{20,28},{1,9},{5,13},{9,17},{1... | collective-permute-start | bytes 1572872 | tf_op jit(solution)/shard_map/ppermute | solution.py:330
  27.4 1.2 %collective-permute-done.1.refs_8_ = bf16[1024,512]{1,0:T(8,128)(2,1)S(1)} collective-permute-done((bf16[1024,512]{1,0:T(8,128)(2,1)S(1)}, bf16[1024,512]{1,0:T(8,128)(2,1)S(1)}, u32[]{:S(2)}, u32[]{:S(2)}) %collective-permute-start.1) | collective-permute-done | bytes 1048608 | tf_op jit(solution)/shard_map/ppermute | solution.py:327
  28.6 1.8 %collective-permute-start.2 = (bf16[512,512]{1,0:T(8,128)(2,1)S(1)}, bf16[512,512]{1,0:T(8,128)(2,1)}, u32[]{:S(2)}, u32[]{:S(2)}) collective-permute-start(bf16[512,512]{1,0:T(8,128)(2,1)S(1)} %slice.8), channel_id=1, source_target_pairs={{0,1},{1,0},{2,3},{3,2},{4,5},{5,4},{6,7},{7,6},{8,9},{9,8},{10,11... | collective-permute-start | bytes 1572872 | tf_op jit(solution)/shard_map/ppermute | solution.py:327
  30.4 1.6 %collective-permute-start.4 = (bf16[512,512]{1,0:T(8,128)(2,1)S(1)}, bf16[512,512]{1,0:T(8,128)(2,1)}, u32[]{:S(2)}, u32[]{:S(2)}) collective-permute-start(bf16[512,512]{1,0:T(8,128)(2,1)S(1)} %slice.9), channel_id=1, source_target_pairs={{0,2},{1,3},{2,0},{3,1},{4,6},{5,7},{6,4},{7,5},{8,10},{9,11},{10,... | collective-permute-start | bytes 1572872 | tf_op jit(solution)/shard_map/ppermute | solution.py:327
  32.0 9.9 %collective-permute-done = bf16[144,1024]{1,0:T(8,128)(2,1)} collective-permute-done((bf16[144,1024]{1,0:T(8,128)(2,1)S(1)}, bf16[144,1024]{1,0:T(8,128)(2,1)}, u32[]{:S(2)}, u32[]{:S(2)}) %collective-permute-start) | collective-permute-done | bytes 294944 | tf_op jit(solution)/shard_map/ppermute | solution.py:394
  43.0 1.0 %pad_maximum_fusion.refs_0_ = bf16[2,144,1024]{2,1,0:T(8,128)(2,1)S(1)} fusion(bf16[1,144,1024]{2,1,0:T(8,128)(2,1)} %bitcast.5, bf16[1,144,1024]{2,1,0:T(8,128)(2,1)S(1)} %get-tuple-element.38), kind=kLoop, calls=%fused_computation.1 | loop fusion | flops 294912 | bytes 1179648 | tf_op jit(solution)/shard_map/stack | solution.py:395
  45.2 11.3 %attend.1 = (bf16[2,2,128,512]{3,2,1,0:T(8,128)(2,1)}, bf16[2,2,128,512]{3,2,1,0:T(8,128)(2,1)}) custom-call(s32[3]{0:T(128)} %pad_add_fusion.tag_ref, s32[2,8]{1,0:T(2,128)} %seg_ref.1, bf16[2,128,1024]{2,1,0:T(8,128)(2,1)} %events_ref.1, bf16[2,128,1024]{2,1,0:T(8,128)(2,1)} %collective-permute-done.8.refs_1_, ...), custom_call_target="tpu_custom_call" | custom-call | flops 5905580032 | bytes 4194304 | tf_op jit(solution)/shard_map/attend/pallas_call | solution.py:141
  56.6 2.5 %collective-permute-start.14 = (bf16[2,144,1024]{2,1,0:T(8,128)(2,1)S(1)}, bf16[2,144,1024]{2,1,0:T(8,128)(2,1)S(1)}, u32[]{:S(2)}, u32[]{:S(2)}) collective-permute-start(bf16[2,144,1024]{2,1,0:T(8,128)(2,1)S(1)} %pad_maximum_fusion.refs_0_), channel_id=1, source_target_pairs={{0,3},{1,2},{2,1},{3,0},{4,7},{5,6},{6,5},{7,4},{8,11},{9,10},{10,... | collective-permute-start | bytes 1769480 | tf_op jit(solution)/shard_map/ppermute | solution.py:327
  59.8 1.0 %copy-done.2 = bf16[2,2,128,512]{3,2,1,0:T(8,128)(2,1)S(1)} copy-done((bf16[2,2,128,512]{3,2,1,0:T(8,128)(2,1)S(1)}, bf16[2,2,128,512]{3,2,1,0:T(8,128)(2,1)}, u32[]{:S(2)}) %copy-start.2) | copy-done | bytes 524312
  60.8 3.1 %finish.1 = (bf16[2,128,1024]{2,1,0:T(8,128)(2,1)}, bf16[64,1024]{1,0:T(8,128)(2,1)S(1)}, bf16[64,1024]{1,0:T(8,128)(2,1)S(1)}) custom-call(s32[3]{0:T(128)S(1)} %copy-done.3, s32[2,64]{1,0:T(2,128)S(1)} %bitcast.15, bf16[2,128,1024]{2,1,0:T(8,128)(2,1)} %events_ref.1, bf16[1024,1024]{1,0:T(8,128)(2,1)S(1)} %copy-done.1, ...), custom_call_target="tpu_custom_call" | custom-call | flops 536870912 | bytes 5242880 | tf_op jit(solution)/shard_map/finish/pallas_call | solution.py:222
  64.0 1.3 %collective-permute-done.13 = bf16[64,1024]{1,0:T(8,128)(2,1)S(1)} collective-permute-done((bf16[64,1024]{1,0:T(8,128)(2,1)S(1)}, bf16[64,1024]{1,0:T(8,128)(2,1)S(1)}, u32[]{:S(2)}, u32[]{:S(2)}) %collective-permute-start.13) | collective-permute-done | bytes 131104 | tf_op jit(solution)/shard_map/ppermute | solution.py:324
  65.4 3.9 %collective-permute-start.15 = (bf16[64,1024]{1,0:T(8,128)(2,1)S(1)}, bf16[64,1024]{1,0:T(8,128)(2,1)S(1)}, u32[]{:S(2)}, u32[]{:S(2)}) collective-permute-start(bf16[64,1024]{1,0:T(8,128)(2,1)S(1)} %add.24.rows_ref), channel_id=1, source_target_pairs={{0,16},{4,20},{8,24},{12,28},{16,0},{20,4},{24,8},{28,12},{1,17},{... | collective-permute-start | bytes 393224 | tf_op jit(solution)/shard_map/ppermute | solution.py:413
  69.8 3.4 %collective-permute-done.14.refs_3_ = bf16[2,144,1024]{2,1,0:T(8,128)(2,1)S(1)} collective-permute-done((bf16[2,144,1024]{2,1,0:T(8,128)(2,1)S(1)}, bf16[2,144,1024]{2,1,0:T(8,128)(2,1)S(1)}, u32[]{:S(2)}, u32[]{:S(2)}) %collective-permute-start.14) | collective-permute-done | bytes 589856 | tf_op jit(solution)/shard_map/ppermute | solution.py:327
  73.2 2.7 %collective-permute-done.15.more_ref = bf16[64,1024]{1,0:T(8,128)(2,1)S(1)} collective-permute-done((bf16[64,1024]{1,0:T(8,128)(2,1)S(1)}, bf16[64,1024]{1,0:T(8,128)(2,1)S(1)}, u32[]{:S(2)}, u32[]{:S(2)}) %collective-permute-start.15) | collective-permute-done | bytes 131104 | tf_op jit(solution)/shard_map/ppermute | solution.py:413
  75.9 2.0 %collective-permute-done.19.refs_7_ = bf16[2,144,1024]{2,1,0:T(8,128)(2,1)S(1)} collective-permute-done((bf16[2,144,1024]{2,1,0:T(8,128)(2,1)S(1)}, bf16[2,144,1024]{2,1,0:T(8,128)(2,1)S(1)}, u32[]{:S(2)}, u32[]{:S(2)}) %collective-permute-start.19) | collective-permute-done | bytes 589856 | tf_op jit(solution)/shard_map/ppermute | solution.py:324
  77.9 3.3 %score.1 = (f32[8,2,1024]{2,1,0:T(2,128)S(1)}, f32[8,2,1024]{2,1,0:T(2,128)S(1)}, f32[8,2,1024]{2,1,0:T(2,128)S(1)}, f32[8,2,1024]{2,1,0:T(2,128)S(1)}) custom-call(s32[3]{0:T(128)S(1)} %copy-done.3, bf16[64,1024]{1,0:T(8,128)(2,1)S(1)} %add.24.rows_ref, bf16[64,1024]{1,0:T(8,128)(2,1)S(1)} %collective-permute-done.15.more_ref, s32[2,64]{1,0:T(2,128)S(1)} %bitcast.17, ...), custom_call_target="tpu_custom_call" | custom-call | flops 268435456 | bytes 3145728 | tf_op jit(solution)/shard_map/score/pallas_call | solution.py:296
  81.2 1.6 %collective-permute-start.21 = (f32[8,2,1024]{2,1,0:T(2,128)S(1)}, f32[8,2,1024]{2,1,0:T(2,128)S(1)}, u32[]{:S(2)}, u32[]{:S(2)}) collective-permute-start(f32[8,2,1024]{2,1,0:T(2,128)S(1)} %get-tuple-element.36), channel_id=1, source_target_pairs={{0,16},{4,20},{8,24},{12,28},{16,0},{20,4},{24,8},{28,12},{1,17},{... | collective-permute-start | bytes 196616 | tf_op jit(solution)/shard_map/ppermute | solution.py:422
  82.9 3.8 %collective-permute-start.20 = (f32[8,2,1024]{2,1,0:T(2,128)S(1)}, f32[8,2,1024]{2,1,0:T(2,128)S(1)}, u32[]{:S(2)}, u32[]{:S(2)}) collective-permute-start(f32[8,2,1024]{2,1,0:T(2,128)S(1)} %get-tuple-element.35), channel_id=1, source_target_pairs={{0,8},{4,12},{8,16},{12,20},{16,24},{20,28},{24,0},{28,4},{1,9},{5... | collective-permute-start | bytes 196616 | tf_op jit(solution)/shard_map/ppermute | solution.py:422
  86.7 3.6 %collective-permute-done.20 = f32[8,2,1024]{2,1,0:T(2,128)S(1)} collective-permute-done((f32[8,2,1024]{2,1,0:T(2,128)S(1)}, f32[8,2,1024]{2,1,0:T(2,128)S(1)}, u32[]{:S(2)}, u32[]{:S(2)}) %collective-permute-start.20) | collective-permute-done | bytes 65568 | tf_op jit(solution)/shard_map/ppermute | solution.py:422
  (55 shorter events, 6.4 us)
Async XLA Ops:
  0.6 25.8 %copy-start.10 = (bf16[128]{0:T(256)(128)(2,1)S(1)}, bf16[128]{0:T(256)(128)(2,1)}, u32[]{:S(2)}) copy-start(bf16[128]{0:T(256)(128)(2,1)} %param.12) | copy-start | bytes 772
  2.3 26.2 %collective-permute-start.1 = (bf16[1024,512]{1,0:T(8,128)(2,1)S(1)}, bf16[1024,512]{1,0:T(8,128)(2,1)S(1)}, u32[]{:S(2)}, u32[]{:S(2)}) collective-permute-start(bf16[1024,512]{1,0:T(8,128)(2,1)S(1)} %constant_dynamic-slice_fusion.refs_6_), channel_id=1, source_target_pairs={{0,2},{1,3},{2,0},{3,1},{4,6},{5,7},{6,4},{7,5},{8,10},{9,11},{10,... | collective-permute-start | bytes 3145736 | tf_op jit(solution)/shard_map/ppermute | solution.py:327
  5.4 25.0 %collective-permute-start.3 = (bf16[1024,512]{1,0:T(8,128)(2,1)S(1)}, bf16[1024,512]{1,0:T(8,128)(2,1)S(1)}, u32[]{:S(2)}, u32[]{:S(2)}) collective-permute-start(bf16[1024,512]{1,0:T(8,128)(2,1)S(1)} %constant_dynamic-slice_fusion.refs_6_), channel_id=1, source_target_pairs={{0,1},{1,0},{2,3},{3,2},{4,5},{5,4},{6,7},{7,6},{8,9},{9,8},{10,11... | collective-permute-start | bytes 3145736 | tf_op jit(solution)/shard_map/ppermute | solution.py:327
  6.9 14.4 %collective-permute-start.7 = (bf16[2,128,1024]{2,1,0:T(8,128)(2,1)}, bf16[2,128,1024]{2,1,0:T(8,128)(2,1)}, u32[]{:S(2)}, u32[]{:S(2)}) collective-permute-start(bf16[2,128,1024]{2,1,0:T(8,128)(2,1)} %events_ref.1), channel_id=1, source_target_pairs={{0,8},{4,12},{8,16},{12,20},{16,24},{20,28},{1,9},{5,13},{9,17},{1... | collective-permute-start | bytes 1572872 | tf_op jit(solution)/shard_map/ppermute | solution.py:330
  21.3 20.6 %collective-permute-start.10 = (bf16[2,128,1024]{2,1,0:T(8,128)(2,1)}, bf16[2,128,1024]{2,1,0:T(8,128)(2,1)}, u32[]{:S(2)}, u32[]{:S(2)}) collective-permute-start(bf16[2,128,1024]{2,1,0:T(8,128)(2,1)} %collective-permute-done.7.refs_2_), channel_id=1, source_target_pairs={{0,8},{4,12},{8,16},{12,20},{16,24},{20,28},{1,9},{5,13},{9,17},{1... | collective-permute-start | bytes 1572872 | tf_op jit(solution)/shard_map/ppermute | solution.py:330
  26.5 15.3 %collective-permute-start = (bf16[144,1024]{1,0:T(8,128)(2,1)S(1)}, bf16[144,1024]{1,0:T(8,128)(2,1)}, u32[]{:S(2)}, u32[]{:S(2)}) collective-permute-start(bf16[144,1024]{1,0:T(8,128)(2,1)S(1)} %get-tuple-element.39), channel_id=1, source_target_pairs={{0,8},{4,12},{8,0},{12,4},{16,24},{20,28},{24,16},{28,20},{1,9},{5... | collective-permute-start | bytes 884744 | tf_op jit(solution)/shard_map/ppermute | solution.py:394
  28.6 15.5 %collective-permute-start.2 = (bf16[512,512]{1,0:T(8,128)(2,1)S(1)}, bf16[512,512]{1,0:T(8,128)(2,1)}, u32[]{:S(2)}, u32[]{:S(2)}) collective-permute-start(bf16[512,512]{1,0:T(8,128)(2,1)S(1)} %slice.8), channel_id=1, source_target_pairs={{0,1},{1,0},{2,3},{3,2},{4,5},{5,4},{6,7},{7,6},{8,9},{9,8},{10,11... | collective-permute-start | bytes 1572872 | tf_op jit(solution)/shard_map/ppermute | solution.py:327
  30.4 13.7 %collective-permute-start.4 = (bf16[512,512]{1,0:T(8,128)(2,1)S(1)}, bf16[512,512]{1,0:T(8,128)(2,1)}, u32[]{:S(2)}, u32[]{:S(2)}) collective-permute-start(bf16[512,512]{1,0:T(8,128)(2,1)S(1)} %slice.9), channel_id=1, source_target_pairs={{0,2},{1,3},{2,0},{3,1},{4,6},{5,7},{6,4},{7,5},{8,10},{9,11},{10,... | collective-permute-start | bytes 1572872 | tf_op jit(solution)/shard_map/ppermute | solution.py:327
  32.0 13.2 %collective-permute-start.8 = (bf16[2,128,1024]{2,1,0:T(8,128)(2,1)}, bf16[2,128,1024]{2,1,0:T(8,128)(2,1)}, u32[]{:S(2)}, u32[]{:S(2)}) collective-permute-start(bf16[2,128,1024]{2,1,0:T(8,128)(2,1)} %events_ref.1), channel_id=1, source_target_pairs={{0,4},{4,0},{8,12},{12,8},{16,20},{20,16},{24,28},{28,24},{1,5},{5... | collective-permute-start | bytes 1572872 | tf_op jit(solution)/shard_map/ppermute | solution.py:324
  41.9 3.4 %collective-permute-start.9 = (bf16[2,128,1024]{2,1,0:T(8,128)(2,1)}, bf16[2,128,1024]{2,1,0:T(8,128)(2,1)}, u32[]{:S(2)}, u32[]{:S(2)}) collective-permute-start(bf16[2,128,1024]{2,1,0:T(8,128)(2,1)} %collective-permute-done.7.refs_2_), channel_id=1, source_target_pairs={{0,4},{4,0},{8,12},{12,8},{16,20},{20,16},{24,28},{28,24},{1,5},{5... | collective-permute-start | bytes 1572872 | tf_op jit(solution)/shard_map/ppermute | solution.py:324
  41.9 3.4 %collective-permute-start.11 = (bf16[2,128,1024]{2,1,0:T(8,128)(2,1)}, bf16[2,128,1024]{2,1,0:T(8,128)(2,1)}, u32[]{:S(2)}, u32[]{:S(2)}) collective-permute-start(bf16[2,128,1024]{2,1,0:T(8,128)(2,1)} %collective-permute-done.10.refs_4_), channel_id=1, source_target_pairs={{0,4},{4,0},{8,12},{12,8},{16,20},{20,16},{24,28},{28,24},{1,5},{5... | collective-permute-start | bytes 1572872 | tf_op jit(solution)/shard_map/ppermute | solution.py:324
  44.1 15.4 %collective-permute-start.5 = (bf16[2,144,1024]{2,1,0:T(8,128)(2,1)S(1)}, bf16[2,144,1024]{2,1,0:T(8,128)(2,1)S(1)}, u32[]{:S(2)}, u32[]{:S(2)}) collective-permute-start(bf16[2,144,1024]{2,1,0:T(8,128)(2,1)S(1)} %pad_maximum_fusion.refs_0_), channel_id=1, source_target_pairs={{0,1},{1,0},{2,3},{3,2},{4,5},{5,4},{6,7},{7,6},{8,9},{9,8},{10,11... | collective-permute-start | bytes 1769480 | tf_op jit(solution)/shard_map/ppermute | solution.py:327
  44.7 15.0 %collective-permute-start.6 = (bf16[2,144,1024]{2,1,0:T(8,128)(2,1)S(1)}, bf16[2,144,1024]{2,1,0:T(8,128)(2,1)S(1)}, u32[]{:S(2)}, u32[]{:S(2)}) collective-permute-start(bf16[2,144,1024]{2,1,0:T(8,128)(2,1)S(1)} %pad_maximum_fusion.refs_0_), channel_id=1, source_target_pairs={{0,2},{1,3},{2,0},{3,1},{4,6},{5,7},{6,4},{7,5},{8,10},{9,11},{10,... | collective-permute-start | bytes 1769480 | tf_op jit(solution)/shard_map/ppermute | solution.py:327
  56.5 3.2 %collective-permute-start.12 = (bf16[2,2,128,512]{3,2,1,0:T(8,128)(2,1)}, bf16[2,2,128,512]{3,2,1,0:T(8,128)(2,1)S(1)}, u32[]{:S(2)}, u32[]{:S(2)}) collective-permute-start(bf16[2,2,128,512]{3,2,1,0:T(8,128)(2,1)} %get-tuple-element.25), channel_id=1, source_target_pairs={{0,4},{4,0},{8,12},{12,8},{16,20},{20,16},{24,28},{28,24},{1,5},{5... | collective-permute-start | bytes 1572872 | tf_op jit(solution)/shard_map/ppermute | solution.py:324
  56.6 16.6 %collective-permute-start.14 = (bf16[2,144,1024]{2,1,0:T(8,128)(2,1)S(1)}, bf16[2,144,1024]{2,1,0:T(8,128)(2,1)S(1)}, u32[]{:S(2)}, u32[]{:S(2)}) collective-permute-start(bf16[2,144,1024]{2,1,0:T(8,128)(2,1)S(1)} %pad_maximum_fusion.refs_0_), channel_id=1, source_target_pairs={{0,3},{1,2},{2,1},{3,0},{4,7},{5,6},{6,5},{7,4},{8,11},{9,10},{10,... | collective-permute-start | bytes 1769480 | tf_op jit(solution)/shard_map/ppermute | solution.py:327
  63.9 1.4 %collective-permute-start.13 = (bf16[64,1024]{1,0:T(8,128)(2,1)S(1)}, bf16[64,1024]{1,0:T(8,128)(2,1)S(1)}, u32[]{:S(2)}, u32[]{:S(2)}) collective-permute-start(bf16[64,1024]{1,0:T(8,128)(2,1)S(1)} %get-tuple-element.28), channel_id=1, source_target_pairs={{0,4},{4,0},{8,12},{12,8},{16,20},{20,16},{24,28},{28,24},{1,5},{5... | collective-permute-start | bytes 393224 | tf_op jit(solution)/shard_map/ppermute | solution.py:324
  65.4 10.6 %collective-permute-start.15 = (bf16[64,1024]{1,0:T(8,128)(2,1)S(1)}, bf16[64,1024]{1,0:T(8,128)(2,1)S(1)}, u32[]{:S(2)}, u32[]{:S(2)}) collective-permute-start(bf16[64,1024]{1,0:T(8,128)(2,1)S(1)} %add.24.rows_ref), channel_id=1, source_target_pairs={{0,16},{4,20},{8,24},{12,28},{16,0},{20,4},{24,8},{28,12},{1,17},{... | collective-permute-start | bytes 393224 | tf_op jit(solution)/shard_map/ppermute | solution.py:413
  69.3 6.6 %collective-permute-start.16 = (bf16[2,144,1024]{2,1,0:T(8,128)(2,1)S(1)}, bf16[2,144,1024]{2,1,0:T(8,128)(2,1)S(1)}, u32[]{:S(2)}, u32[]{:S(2)}) collective-permute-start(bf16[2,144,1024]{2,1,0:T(8,128)(2,1)S(1)} %pad_maximum_fusion.refs_0_), channel_id=1, source_target_pairs={{0,4},{4,0},{8,12},{12,8},{16,20},{20,16},{24,28},{28,24},{1,5},{5... | collective-permute-start | bytes 1769480 | tf_op jit(solution)/shard_map/ppermute | solution.py:324
  69.3 6.6 %collective-permute-start.17 = (bf16[2,144,1024]{2,1,0:T(8,128)(2,1)S(1)}, bf16[2,144,1024]{2,1,0:T(8,128)(2,1)S(1)}, u32[]{:S(2)}, u32[]{:S(2)}) collective-permute-start(bf16[2,144,1024]{2,1,0:T(8,128)(2,1)S(1)} %collective-permute-done.5.refs_1_), channel_id=1, source_target_pairs={{0,4},{4,0},{8,12},{12,8},{16,20},{20,16},{24,28},{28,24},{1,5},{5... | collective-permute-start | bytes 1769480 | tf_op jit(solution)/shard_map/ppermute | solution.py:324
  69.8 6.1 %collective-permute-start.18 = (bf16[2,144,1024]{2,1,0:T(8,128)(2,1)S(1)}, bf16[2,144,1024]{2,1,0:T(8,128)(2,1)S(1)}, u32[]{:S(2)}, u32[]{:S(2)}) collective-permute-start(bf16[2,144,1024]{2,1,0:T(8,128)(2,1)S(1)} %collective-permute-done.6.refs_2_), channel_id=1, source_target_pairs={{0,4},{4,0},{8,12},{12,8},{16,20},{20,16},{24,28},{28,24},{1,5},{5... | collective-permute-start | bytes 1769480 | tf_op jit(solution)/shard_map/ppermute | solution.py:324
  75.9 2.0 %collective-permute-start.19 = (bf16[2,144,1024]{2,1,0:T(8,128)(2,1)S(1)}, bf16[2,144,1024]{2,1,0:T(8,128)(2,1)S(1)}, u32[]{:S(2)}, u32[]{:S(2)}) collective-permute-start(bf16[2,144,1024]{2,1,0:T(8,128)(2,1)S(1)} %collective-permute-done.14.refs_3_), channel_id=1, source_target_pairs={{0,4},{4,0},{8,12},{12,8},{16,20},{20,16},{24,28},{28,24},{1,5},{5... | collective-permute-start | bytes 1769480 | tf_op jit(solution)/shard_map/ppermute | solution.py:324
  81.2 5.5 %collective-permute-start.21 = (f32[8,2,1024]{2,1,0:T(2,128)S(1)}, f32[8,2,1024]{2,1,0:T(2,128)S(1)}, u32[]{:S(2)}, u32[]{:S(2)}) collective-permute-start(f32[8,2,1024]{2,1,0:T(2,128)S(1)} %get-tuple-element.36), channel_id=1, source_target_pairs={{0,16},{4,20},{8,24},{12,28},{16,0},{20,4},{24,8},{28,12},{1,17},{... | collective-permute-start | bytes 196616 | tf_op jit(solution)/shard_map/ppermute | solution.py:422
  82.9 7.5 %collective-permute-start.20 = (f32[8,2,1024]{2,1,0:T(2,128)S(1)}, f32[8,2,1024]{2,1,0:T(2,128)S(1)}, u32[]{:S(2)}, u32[]{:S(2)}) collective-permute-start(f32[8,2,1024]{2,1,0:T(2,128)S(1)} %get-tuple-element.35), channel_id=1, source_target_pairs={{0,8},{4,12},{8,16},{12,20},{16,24},{20,28},{24,0},{28,4},{1,9},{5... | collective-permute-start | bytes 196616 | tf_op jit(solution)/shard_map/ppermute | solution.py:422
  86.6 4.6 %collective-permute-start.22 = (f32[8,2,1024]{2,1,0:T(2,128)S(1)}, f32[8,2,1024]{2,1,0:T(2,128)S(1)}, u32[]{:S(2)}, u32[]{:S(2)}) collective-permute-start(f32[8,2,1024]{2,1,0:T(2,128)S(1)} %get-tuple-element.37), channel_id=1, source_target_pairs={{0,24},{4,28},{8,0},{12,4},{16,8},{20,12},{24,16},{28,20},{1,25},{... | collective-permute-start | bytes 196616 | tf_op jit(solution)/shard_map/ppermute | solution.py:422
  (10 other events, 145.9 us)

commit v6 on v5

--- a/solution.py
+++ b/solution.py
@@ -338,11 +338,13 @@
             own = lax.dynamic_slice_in_dim(w_in, offset, cols, 1)
             offset = offset + cols
             if not chunks:
-                over_x, over_y = across(own, 1), across(own, 2)
-                first = [own, over_x, over_y]
-                top = across(over_y[: width // 2], 1)
-                bottom = across(over_x[width // 2 :], 2)
-                chunks.append((first + [top, bottom], (0, 1, 2, 3, 3)))
+                upper, lower = own[: width // 2], own[width // 2 :]
+                over_y = [across(upper, 2), across(lower, 2)]
+                over_x = [across(upper, 1), across(lower, 1)]
+                first = [own]
+                top = across(over_y[0], 1)
+                bottom = across(over_x[1], 2)
+                chunks.append((first + over_x + over_y + [top, bottom], (0, 1, 1, 2, 2, 3, 3)))
             else:
                 own, _ = lax.optimization_barrier((own, chunks[0][0]))
                 chunks.append(([own] + [across(own, bit) for bit in (1, 2, 3)], (0, 1, 2, 3)))

time: 92.2 us -> 101 us (1.095)
  starting transfers between devices: 32.4 us -> 37.8 us
  waiting for transfers between devices: 35.8 us -> 38.4 us
  local copies, waits for them, and re-layouts: 2.8 us -> 4.71 us
  other arithmetic: 2.41 us -> 1.4 us
    ppermute x7 -> x9, waiting for transfers between devices: 5.25 us -> 11.1 us  [across(): return lax.ppermute(value, 'batch', [(i, i ^ bit) for i in range(batch)])]
    ppermute x1, waiting for transfers between devices: 2.69 us -> 0.01 us  [on_device(): more = lax.ppermute(rows, 'seq', [(i, i ^ 2 * step) for i in range(seq)])]
    ppermute x2, waiting for transfers between devices: 10.1 us -> 7.49 us  [ahead(): lax.ppermute(value, 'seq', [(i, i + 2 * by) for i in range(seq - 2 * by)])]
    ppermute x3, starting transfers between devices: 5.47 us -> 7.97 us  [on_device(): lax.ppermute(parts[step], 'seq', [(i, (i + 2 * step) % seq) for i in rang...]
    dynamic_slice x1, local copies, waits for them, and re-layouts: 0.1 us -> 2.44 us  [on_device(): own = lax.dynamic_slice_in_dim(w_in, offset, cols, 1)]
    ppermute x1, waiting for transfers between devices: 9.87 us -> 11.5 us  [on_device(): paired = lax.ppermute(padded, 'seq', [(i, i ^ 2) for i in range(seq)])]
    ppermute x2, starting transfers between devices: 9.47 us -> 10.9 us  [ahead(): lax.ppermute(value, 'seq', [(i, i + 2 * by) for i in range(seq - 2 * by)])]
    ppermute x7 -> x9, starting transfers between devices: 11.5 us -> 12.6 us  [across(): return lax.ppermute(value, 'batch', [(i, i ^ bit) for i in range(batch)])]
  transfers between devices with their start and end apart: 23 -> 25, of which waited for: 11 -> 10; matrix products, arithmetic and copies ran while one was open for 2% -> 1% of each run, Pallas kernels for 16% -> 14%
where the time goes in v6:
time: 101 us
  waiting for transfers between devices  38.4 us (38%)
  starting transfers between devices  37.8 us (37%)
  Pallas kernels  17.6 us (17%)
  local copies, waits for them, and re-layouts  4.71 us (5%)
  other arithmetic  1.4 us (1%)
    ppermute x9, starting transfers between devices, across(): return lax.ppermute(value, 'batch', [(i, i ^ bit) for i in range(batch)])  12.6 us
    ppermute x1, waiting for transfers between devices, on_device(): paired = lax.ppermute(padded, 'seq', [(i, i ^ 2) for i in range(seq)])  11.5 us
    pallas_call x1, Pallas kernels, attend(): pl.pallas_call(functools.partial(attend_kernel, blocks, split), out_shape...  11.3 us
    ppermute x9, waiting for transfers between devices, across(): return lax.ppermute(value, 'batch', [(i, i ^ bit) for i in range(batch)])  11.1 us
    ppermute x2, starting transfers between devices, ahead(): lax.ppermute(value, 'seq', [(i, i + 2 * by) for i in range(seq - 2 * by)])  10.9 us
    ppermute x3, starting transfers between devices, on_device(): lax.ppermute(parts[step], 'seq', [(i, (i + 2 * step) % seq) for i in rang...  7.97 us
    ppermute x2, waiting for transfers between devices, ahead(): lax.ppermute(value, 'seq', [(i, i + 2 * by) for i in range(seq - 2 * by)])  7.49 us
    ppermute x3, waiting for transfers between devices, on_device(): lax.ppermute(parts[step], 'seq', [(i, (i + 2 * step) % seq) for i in rang...  4.59 us
  transfers between devices with their start and end apart: 25, of which 10 were waited for; matrix products, arithmetic and copies ran while one was open for 1% of the time, Pallas kernels for 14%

profile of v6, /device:TPU:0, one launch (start us, length us, event | category | flops | bytes accessed | tf_op | source)
XLA Modules:
  0.0 100.9 jit_solution(15303200778117892231)
XLA Ops:
  0.7 2.4 %constant_dynamic-slice_fusion.1.refs_6_ = bf16[1024,512]{1,0:T(8,128)(2,1)} fusion(bf16[1024,1024]{1,0:T(8,128)(2,1)} %param.9, s32[]{:T(128)S(6)} %select_n.16), kind=kLoop, calls=%fused_computation.7 | loop fusion | bytes 2097156 | tf_op jit(solution)/shard_map/dynamic_slice | solution.py:338
  3.1 5.7 %collective-permute-start.7 = (bf16[2,128,1024]{2,1,0:T(8,128)(2,1)}, bf16[2,128,1024]{2,1,0:T(8,128)(2,1)}, u32[]{:S(2)}, u32[]{:S(2)}) collective-permute-start(bf16[2,128,1024]{2,1,0:T(8,128)(2,1)} %events_ref.1), channel_id=1, source_target_pairs={{0,8},{4,12},{8,16},{12,20},{16,24},{20,28},{1,9},{5,13},{9,17},{1... | collective-permute-start | bytes 1572872 | tf_op jit(solution)/shard_map/ppermute | solution.py:330
  9.0 1.6 %collective-permute-start.1 = (bf16[512,512]{1,0:T(8,128)(2,1)S(1)}, bf16[512,512]{1,0:T(8,128)(2,1)S(1)}, u32[]{:S(2)}, u32[]{:S(2)}) collective-permute-start(bf16[512,512]{1,0:T(8,128)(2,1)S(1)} %get-tuple-element.39), channel_id=1, source_target_pairs={{0,2},{1,3},{2,0},{3,1},{4,6},{5,7},{6,4},{7,5},{8,10},{9,11},{10,... | collective-permute-start | bytes 1572872 | tf_op jit(solution)/shard_map/ppermute | solution.py:327
  10.5 1.5 %collective-permute-start.3 = (bf16[512,512]{1,0:T(8,128)(2,1)S(1)}, bf16[512,512]{1,0:T(8,128)(2,1)S(1)}, u32[]{:S(2)}, u32[]{:S(2)}) collective-permute-start(bf16[512,512]{1,0:T(8,128)(2,1)S(1)} %get-tuple-element.38), channel_id=1, source_target_pairs={{0,1},{1,0},{2,3},{3,2},{4,5},{5,4},{6,7},{7,6},{8,9},{9,8},{10,11... | collective-permute-start | bytes 1572872 | tf_op jit(solution)/shard_map/ppermute | solution.py:327
  12.0 7.5 %collective-permute-done.7.refs_2_ = bf16[2,128,1024]{2,1,0:T(8,128)(2,1)} collective-permute-done((bf16[2,128,1024]{2,1,0:T(8,128)(2,1)}, bf16[2,128,1024]{2,1,0:T(8,128)(2,1)}, u32[]{:S(2)}, u32[]{:S(2)}) %collective-permute-start.7) | collective-permute-done | bytes 524320 | tf_op jit(solution)/shard_map/ppermute | solution.py:330
  19.5 5.2 %collective-permute-start.10 = (bf16[2,128,1024]{2,1,0:T(8,128)(2,1)}, bf16[2,128,1024]{2,1,0:T(8,128)(2,1)}, u32[]{:S(2)}, u32[]{:S(2)}) collective-permute-start(bf16[2,128,1024]{2,1,0:T(8,128)(2,1)} %collective-permute-done.7.refs_2_), channel_id=1, source_target_pairs={{0,8},{4,12},{8,16},{12,20},{16,24},{20,28},{1,9},{5,13},{9,17},{1... | collective-permute-start | bytes 1572872 | tf_op jit(solution)/shard_map/ppermute | solution.py:330
  24.7 1.5 %collective-permute-start.2 = (bf16[512,512]{1,0:T(8,128)(2,1)S(1)}, bf16[512,512]{1,0:T(8,128)(2,1)S(1)}, u32[]{:S(2)}, u32[]{:S(2)}) collective-permute-start(bf16[512,512]{1,0:T(8,128)(2,1)S(1)} %collective-permute-done.1.refs_9_), channel_id=1, source_target_pairs={{0,1},{1,0},{2,3},{3,2},{4,5},{5,4},{6,7},{7,6},{8,9},{9,8},{10,11... | collective-permute-start | bytes 1572872 | tf_op jit(solution)/shard_map/ppermute | solution.py:327
  26.2 1.5 %collective-permute-start.4 = (bf16[512,512]{1,0:T(8,128)(2,1)S(1)}, bf16[512,512]{1,0:T(8,128)(2,1)S(1)}, u32[]{:S(2)}, u32[]{:S(2)}) collective-permute-start(bf16[512,512]{1,0:T(8,128)(2,1)S(1)} %collective-permute-done.3.refs_8_), channel_id=1, source_target_pairs={{0,2},{1,3},{2,0},{3,1},{4,6},{5,7},{6,4},{7,5},{8,10},{9,11},{10,... | collective-permute-start | bytes 1572872 | tf_op jit(solution)/shard_map/ppermute | solution.py:327
  29.3 11.5 %collective-permute-done = bf16[144,1024]{1,0:T(8,128)(2,1)S(1)} collective-permute-done((bf16[144,1024]{1,0:T(8,128)(2,1)S(1)}, bf16[144,1024]{1,0:T(8,128)(2,1)S(1)}, u32[]{:S(2)}, u32[]{:S(2)}) %collective-permute-start) | collective-permute-done | bytes 294944 | tf_op jit(solution)/shard_map/ppermute | solution.py:396
  40.7 1.5 %collective-permute-start.13 = (bf16[512,512]{1,0:T(8,128)(2,1)S(1)}, bf16[512,512]{1,0:T(8,128)(2,1)}, u32[]{:S(2)}, u32[]{:S(2)}) collective-permute-start(bf16[512,512]{1,0:T(8,128)(2,1)S(1)} %get-tuple-element.38), channel_id=1, source_target_pairs={{0,2},{1,3},{2,0},{3,1},{4,6},{5,7},{6,4},{7,5},{8,10},{9,11},{10,... | collective-permute-start | bytes 1572872 | tf_op jit(solution)/shard_map/ppermute | solution.py:327
  45.1 3.5 %collective-permute-done.12.refs_7_ = bf16[512,512]{1,0:T(8,128)(2,1)} collective-permute-done((bf16[512,512]{1,0:T(8,128)(2,1)S(1)}, bf16[512,512]{1,0:T(8,128)(2,1)}, u32[]{:S(2)}, u32[]{:S(2)}) %collective-permute-start.12) | collective-permute-done | bytes 524320 | tf_op jit(solution)/shard_map/ppermute | solution.py:327
  48.6 1.5 %collective-permute-start.5 = (bf16[2,144,1024]{2,1,0:T(8,128)(2,1)S(1)}, bf16[2,144,1024]{2,1,0:T(8,128)(2,1)S(1)}, u32[]{:S(2)}, u32[]{:S(2)}) collective-permute-start(bf16[2,144,1024]{2,1,0:T(8,128)(2,1)S(1)} %pad_maximum_fusion.refs_0_), channel_id=1, source_target_pairs={{0,1},{1,0},{2,3},{3,2},{4,5},{5,4},{6,7},{7,6},{8,9},{9,8},{10,11... | collective-permute-start | bytes 1769480 | tf_op jit(solution)/shard_map/ppermute | solution.py:327
  50.1 2.8 %collective-permute-done.13.refs_10_ = bf16[512,512]{1,0:T(8,128)(2,1)} collective-permute-done((bf16[512,512]{1,0:T(8,128)(2,1)S(1)}, bf16[512,512]{1,0:T(8,128)(2,1)}, u32[]{:S(2)}, u32[]{:S(2)}) %collective-permute-start.13) | collective-permute-done | bytes 524320 | tf_op jit(solution)/shard_map/ppermute | solution.py:327
  52.8 1.5 %collective-permute-start.6 = (bf16[2,144,1024]{2,1,0:T(8,128)(2,1)S(1)}, bf16[2,144,1024]{2,1,0:T(8,128)(2,1)S(1)}, u32[]{:S(2)}, u32[]{:S(2)}) collective-permute-start(bf16[2,144,1024]{2,1,0:T(8,128)(2,1)S(1)} %pad_maximum_fusion.refs_0_), channel_id=1, source_target_pairs={{0,2},{1,3},{2,0},{3,1},{4,6},{5,7},{6,4},{7,5},{8,10},{9,11},{10,... | collective-permute-start | bytes 1769480 | tf_op jit(solution)/shard_map/ppermute | solution.py:327
  54.4 11.3 %attend.1 = (bf16[2,2,128,512]{3,2,1,0:T(8,128)(2,1)}, bf16[2,2,128,512]{3,2,1,0:T(8,128)(2,1)}) custom-call(s32[3]{0:T(128)} %pad_add_fusion.tag_ref, s32[2,8]{1,0:T(2,128)} %seg_ref.1, bf16[2,128,1024]{2,1,0:T(8,128)(2,1)} %events_ref.1, bf16[2,128,1024]{2,1,0:T(8,128)(2,1)} %collective-permute-done.8.refs_1_, ...), custom_call_target="tpu_custom_call" | custom-call | flops 5905580032 | bytes 4194304 | tf_op jit(solution)/shard_map/attend/pallas_call | solution.py:141
  65.7 1.5 %collective-permute-start.16 = (bf16[2,144,1024]{2,1,0:T(8,128)(2,1)S(1)}, bf16[2,144,1024]{2,1,0:T(8,128)(2,1)S(1)}, u32[]{:S(2)}, u32[]{:S(2)}) collective-permute-start(bf16[2,144,1024]{2,1,0:T(8,128)(2,1)S(1)} %pad_maximum_fusion.refs_0_), channel_id=1, source_target_pairs={{0,3},{1,2},{2,1},{3,0},{4,7},{5,6},{6,5},{7,4},{8,11},{9,10},{10,... | collective-permute-start | bytes 1769480 | tf_op jit(solution)/shard_map/ppermute | solution.py:327
  68.9 3.1 %finish.1 = (bf16[2,128,1024]{2,1,0:T(8,128)(2,1)}, bf16[64,1024]{1,0:T(8,128)(2,1)S(1)}, bf16[64,1024]{1,0:T(8,128)(2,1)S(1)}) custom-call(s32[3]{0:T(128)S(1)} %copy-done.2, s32[2,64]{1,0:T(2,128)S(1)} %bitcast.15, bf16[2,128,1024]{2,1,0:T(8,128)(2,1)} %events_ref.1, bf16[1024,1024]{1,0:T(8,128)(2,1)S(1)} %copy-done, ...), custom_call_target="tpu_custom_call" | custom-call | flops 536870912 | bytes 5242880 | tf_op jit(solution)/shard_map/finish/pallas_call | solution.py:222
  73.4 3.6 %collective-permute-start.17 = (bf16[64,1024]{1,0:T(8,128)(2,1)S(1)}, bf16[64,1024]{1,0:T(8,128)(2,1)S(1)}, u32[]{:S(2)}, u32[]{:S(2)}) collective-permute-start(bf16[64,1024]{1,0:T(8,128)(2,1)S(1)} %add.24.rows_ref), channel_id=1, source_target_pairs={{0,16},{4,20},{8,24},{12,28},{16,0},{20,4},{24,8},{28,12},{1,17},{... | collective-permute-start | bytes 393224 | tf_op jit(solution)/shard_map/ppermute | solution.py:415
  77.6 4.8 %collective-permute-done.16.refs_3_ = bf16[2,144,1024]{2,1,0:T(8,128)(2,1)S(1)} collective-permute-done((bf16[2,144,1024]{2,1,0:T(8,128)(2,1)S(1)}, bf16[2,144,1024]{2,1,0:T(8,128)(2,1)S(1)}, u32[]{:S(2)}, u32[]{:S(2)}) %collective-permute-start.16) | collective-permute-done | bytes 589856 | tf_op jit(solution)/shard_map/ppermute | solution.py:327
  82.4 2.0 %collective-permute-done.21.refs_7_ = bf16[2,144,1024]{2,1,0:T(8,128)(2,1)S(1)} collective-permute-done((bf16[2,144,1024]{2,1,0:T(8,128)(2,1)S(1)}, bf16[2,144,1024]{2,1,0:T(8,128)(2,1)S(1)}, u32[]{:S(2)}, u32[]{:S(2)}) %collective-permute-start.21) | collective-permute-done | bytes 589856 | tf_op jit(solution)/shard_map/ppermute | solution.py:324
  84.4 3.3 %score.1 = (f32[8,2,1024]{2,1,0:T(2,128)S(1)}, f32[8,2,1024]{2,1,0:T(2,128)S(1)}, f32[8,2,1024]{2,1,0:T(2,128)S(1)}, f32[8,2,1024]{2,1,0:T(2,128)S(1)}) custom-call(s32[3]{0:T(128)S(1)} %copy-done.2, bf16[64,1024]{1,0:T(8,128)(2,1)S(1)} %add.24.rows_ref, bf16[64,1024]{1,0:T(8,128)(2,1)S(1)} %collective-permute-done.17.more_ref, s32[2,64]{1,0:T(2,128)S(1)} %bitcast.17, ...), custom_call_target="tpu_custom_call" | custom-call | flops 268435456 | bytes 3145728 | tf_op jit(solution)/shard_map/score/pallas_call | solution.py:296
  87.7 3.6 %collective-permute-start.23 = (f32[8,2,1024]{2,1,0:T(2,128)S(1)}, f32[8,2,1024]{2,1,0:T(2,128)S(1)}, u32[]{:S(2)}, u32[]{:S(2)}) collective-permute-start(f32[8,2,1024]{2,1,0:T(2,128)S(1)} %get-tuple-element.36), channel_id=1, source_target_pairs={{0,16},{4,20},{8,24},{12,28},{16,0},{20,4},{24,8},{28,12},{1,17},{... | collective-permute-start | bytes 196616 | tf_op jit(solution)/shard_map/ppermute | solution.py:424
  91.3 4.4 %collective-permute-start.22 = (f32[8,2,1024]{2,1,0:T(2,128)S(1)}, f32[8,2,1024]{2,1,0:T(2,128)S(1)}, u32[]{:S(2)}, u32[]{:S(2)}) collective-permute-start(f32[8,2,1024]{2,1,0:T(2,128)S(1)} %get-tuple-element.35), channel_id=1, source_target_pairs={{0,8},{4,12},{8,16},{12,20},{16,24},{20,28},{24,0},{28,4},{1,9},{5... | collective-permute-start | bytes 196616 | tf_op jit(solution)/shard_map/ppermute | solution.py:424
  95.6 3.7 %collective-permute-done.22 = f32[8,2,1024]{2,1,0:T(2,128)S(1)} collective-permute-done((f32[8,2,1024]{2,1,0:T(2,128)S(1)}, f32[8,2,1024]{2,1,0:T(2,128)S(1)}, u32[]{:S(2)}, u32[]{:S(2)}) %collective-permute-start.22) | collective-permute-done | bytes 65568 | tf_op jit(solution)/shard_map/ppermute | solution.py:424
  (60 shorter events, 9.7 us)
Async XLA Ops:
  3.1 16.4 %collective-permute-start.7 = (bf16[2,128,1024]{2,1,0:T(8,128)(2,1)}, bf16[2,128,1024]{2,1,0:T(8,128)(2,1)}, u32[]{:S(2)}, u32[]{:S(2)}) collective-permute-start(bf16[2,128,1024]{2,1,0:T(8,128)(2,1)} %events_ref.1), channel_id=1, source_target_pairs={{0,8},{4,12},{8,16},{12,20},{16,24},{20,28},{1,9},{5,13},{9,17},{1... | collective-permute-start | bytes 1572872 | tf_op jit(solution)/shard_map/ppermute | solution.py:330
  9.0 15.7 %collective-permute-start.1 = (bf16[512,512]{1,0:T(8,128)(2,1)S(1)}, bf16[512,512]{1,0:T(8,128)(2,1)S(1)}, u32[]{:S(2)}, u32[]{:S(2)}) collective-permute-start(bf16[512,512]{1,0:T(8,128)(2,1)S(1)} %get-tuple-element.39), channel_id=1, source_target_pairs={{0,2},{1,3},{2,0},{3,1},{4,6},{5,7},{6,4},{7,5},{8,10},{9,11},{10,... | collective-permute-start | bytes 1572872 | tf_op jit(solution)/shard_map/ppermute | solution.py:327
  10.5 15.7 %collective-permute-start.3 = (bf16[512,512]{1,0:T(8,128)(2,1)S(1)}, bf16[512,512]{1,0:T(8,128)(2,1)S(1)}, u32[]{:S(2)}, u32[]{:S(2)}) collective-permute-start(bf16[512,512]{1,0:T(8,128)(2,1)S(1)} %get-tuple-element.38), channel_id=1, source_target_pairs={{0,1},{1,0},{2,3},{3,2},{4,5},{5,4},{6,7},{7,6},{8,9},{9,8},{10,11... | collective-permute-start | bytes 1572872 | tf_op jit(solution)/shard_map/ppermute | solution.py:327
  19.5 22.7 %collective-permute-start.10 = (bf16[2,128,1024]{2,1,0:T(8,128)(2,1)}, bf16[2,128,1024]{2,1,0:T(8,128)(2,1)}, u32[]{:S(2)}, u32[]{:S(2)}) collective-permute-start(bf16[2,128,1024]{2,1,0:T(8,128)(2,1)} %collective-permute-done.7.refs_2_), channel_id=1, source_target_pairs={{0,8},{4,12},{8,16},{12,20},{16,24},{20,28},{1,9},{5,13},{9,17},{1... | collective-permute-start | bytes 1572872 | tf_op jit(solution)/shard_map/ppermute | solution.py:330
  24.7 17.6 %collective-permute-start.2 = (bf16[512,512]{1,0:T(8,128)(2,1)S(1)}, bf16[512,512]{1,0:T(8,128)(2,1)S(1)}, u32[]{:S(2)}, u32[]{:S(2)}) collective-permute-start(bf16[512,512]{1,0:T(8,128)(2,1)S(1)} %collective-permute-done.1.refs_9_), channel_id=1, source_target_pairs={{0,1},{1,0},{2,3},{3,2},{4,5},{5,4},{6,7},{7,6},{8,9},{9,8},{10,11... | collective-permute-start | bytes 1572872 | tf_op jit(solution)/shard_map/ppermute | solution.py:327
  26.2 16.6 %collective-permute-start.4 = (bf16[512,512]{1,0:T(8,128)(2,1)S(1)}, bf16[512,512]{1,0:T(8,128)(2,1)S(1)}, u32[]{:S(2)}, u32[]{:S(2)}) collective-permute-start(bf16[512,512]{1,0:T(8,128)(2,1)S(1)} %collective-permute-done.3.refs_8_), channel_id=1, source_target_pairs={{0,2},{1,3},{2,0},{3,1},{4,6},{5,7},{6,4},{7,5},{8,10},{9,11},{10,... | collective-permute-start | bytes 1572872 | tf_op jit(solution)/shard_map/ppermute | solution.py:327
  27.8 12.9 %collective-permute-start = (bf16[144,1024]{1,0:T(8,128)(2,1)S(1)}, bf16[144,1024]{1,0:T(8,128)(2,1)S(1)}, u32[]{:S(2)}, u32[]{:S(2)}) collective-permute-start(bf16[144,1024]{1,0:T(8,128)(2,1)S(1)} %get-tuple-element.41), channel_id=1, source_target_pairs={{0,8},{4,12},{8,0},{12,4},{16,24},{20,28},{24,16},{28,20},{1,9},{5... | collective-permute-start | bytes 884744 | tf_op jit(solution)/shard_map/ppermute | solution.py:396
  28.7 19.8 %collective-permute-start.12 = (bf16[512,512]{1,0:T(8,128)(2,1)S(1)}, bf16[512,512]{1,0:T(8,128)(2,1)}, u32[]{:S(2)}, u32[]{:S(2)}) collective-permute-start(bf16[512,512]{1,0:T(8,128)(2,1)S(1)} %get-tuple-element.39), channel_id=1, source_target_pairs={{0,1},{1,0},{2,3},{3,2},{4,5},{5,4},{6,7},{7,6},{8,9},{9,8},{10,11... | collective-permute-start | bytes 1572872 | tf_op jit(solution)/shard_map/ppermute | solution.py:327
  40.7 12.1 %collective-permute-start.13 = (bf16[512,512]{1,0:T(8,128)(2,1)S(1)}, bf16[512,512]{1,0:T(8,128)(2,1)}, u32[]{:S(2)}, u32[]{:S(2)}) collective-permute-start(bf16[512,512]{1,0:T(8,128)(2,1)S(1)} %get-tuple-element.38), channel_id=1, source_target_pairs={{0,2},{1,3},{2,0},{3,1},{4,6},{5,7},{6,4},{7,5},{8,10},{9,11},{10,... | collective-permute-start | bytes 1572872 | tf_op jit(solution)/shard_map/ppermute | solution.py:327
  42.3 12.1 %collective-permute-start.8 = (bf16[2,128,1024]{2,1,0:T(8,128)(2,1)}, bf16[2,128,1024]{2,1,0:T(8,128)(2,1)}, u32[]{:S(2)}, u32[]{:S(2)}) collective-permute-start(bf16[2,128,1024]{2,1,0:T(8,128)(2,1)} %events_ref.1), channel_id=1, source_target_pairs={{0,4},{4,0},{8,12},{12,8},{16,20},{20,16},{24,28},{28,24},{1,5},{5... | collective-permute-start | bytes 1572872 | tf_op jit(solution)/shard_map/ppermute | solution.py:324
  42.3 12.1 %collective-permute-start.9 = (bf16[2,128,1024]{2,1,0:T(8,128)(2,1)}, bf16[2,128,1024]{2,1,0:T(8,128)(2,1)}, u32[]{:S(2)}, u32[]{:S(2)}) collective-permute-start(bf16[2,128,1024]{2,1,0:T(8,128)(2,1)} %collective-permute-done.7.refs_2_), channel_id=1, source_target_pairs={{0,4},{4,0},{8,12},{12,8},{16,20},{20,16},{24,28},{28,24},{1,5},{5... | collective-permute-start | bytes 1572872 | tf_op jit(solution)/shard_map/ppermute | solution.py:324
  43.9 10.5 %collective-permute-start.11 = (bf16[2,128,1024]{2,1,0:T(8,128)(2,1)}, bf16[2,128,1024]{2,1,0:T(8,128)(2,1)}, u32[]{:S(2)}, u32[]{:S(2)}) collective-permute-start(bf16[2,128,1024]{2,1,0:T(8,128)(2,1)} %collective-permute-done.10.refs_4_), channel_id=1, source_target_pairs={{0,4},{4,0},{8,12},{12,8},{16,20},{20,16},{24,28},{28,24},{1,5},{5... | collective-permute-start | bytes 1572872 | tf_op jit(solution)/shard_map/ppermute | solution.py:324
  48.6 18.7 %collective-permute-start.5 = (bf16[2,144,1024]{2,1,0:T(8,128)(2,1)S(1)}, bf16[2,144,1024]{2,1,0:T(8,128)(2,1)S(1)}, u32[]{:S(2)}, u32[]{:S(2)}) collective-permute-start(bf16[2,144,1024]{2,1,0:T(8,128)(2,1)S(1)} %pad_maximum_fusion.refs_0_), channel_id=1, source_target_pairs={{0,1},{1,0},{2,3},{3,2},{4,5},{5,4},{6,7},{7,6},{8,9},{9,8},{10,11... | collective-permute-start | bytes 1769480 | tf_op jit(solution)/shard_map/ppermute | solution.py:327
  52.8 14.4 %collective-permute-start.6 = (bf16[2,144,1024]{2,1,0:T(8,128)(2,1)S(1)}, bf16[2,144,1024]{2,1,0:T(8,128)(2,1)S(1)}, u32[]{:S(2)}, u32[]{:S(2)}) collective-permute-start(bf16[2,144,1024]{2,1,0:T(8,128)(2,1)S(1)} %pad_maximum_fusion.refs_0_), channel_id=1, source_target_pairs={{0,2},{1,3},{2,0},{3,1},{4,6},{5,7},{6,4},{7,5},{8,10},{9,11},{10,... | collective-permute-start | bytes 1769480 | tf_op jit(solution)/shard_map/ppermute | solution.py:327
  65.6 2.2 %collective-permute-start.14 = (bf16[2,2,128,512]{3,2,1,0:T(8,128)(2,1)}, bf16[2,2,128,512]{3,2,1,0:T(8,128)(2,1)S(1)}, u32[]{:S(2)}, u32[]{:S(2)}) collective-permute-start(bf16[2,2,128,512]{3,2,1,0:T(8,128)(2,1)} %get-tuple-element.25), channel_id=1, source_target_pairs={{0,4},{4,0},{8,12},{12,8},{16,20},{20,16},{24,28},{28,24},{1,5},{5... | collective-permute-start | bytes 1572872 | tf_op jit(solution)/shard_map/ppermute | solution.py:324
  65.7 16.6 %collective-permute-start.16 = (bf16[2,144,1024]{2,1,0:T(8,128)(2,1)S(1)}, bf16[2,144,1024]{2,1,0:T(8,128)(2,1)S(1)}, u32[]{:S(2)}, u32[]{:S(2)}) collective-permute-start(bf16[2,144,1024]{2,1,0:T(8,128)(2,1)S(1)} %pad_maximum_fusion.refs_0_), channel_id=1, source_target_pairs={{0,3},{1,2},{2,1},{3,0},{4,7},{5,6},{6,5},{7,4},{8,11},{9,10},{10,... | collective-permute-start | bytes 1769480 | tf_op jit(solution)/shard_map/ppermute | solution.py:327
  73.4 8.9 %collective-permute-start.17 = (bf16[64,1024]{1,0:T(8,128)(2,1)S(1)}, bf16[64,1024]{1,0:T(8,128)(2,1)S(1)}, u32[]{:S(2)}, u32[]{:S(2)}) collective-permute-start(bf16[64,1024]{1,0:T(8,128)(2,1)S(1)} %add.24.rows_ref), channel_id=1, source_target_pairs={{0,16},{4,20},{8,24},{12,28},{16,0},{20,4},{24,8},{28,12},{1,17},{... | collective-permute-start | bytes 393224 | tf_op jit(solution)/shard_map/ppermute | solution.py:415
  77.0 5.3 %collective-permute-start.18 = (bf16[2,144,1024]{2,1,0:T(8,128)(2,1)S(1)}, bf16[2,144,1024]{2,1,0:T(8,128)(2,1)S(1)}, u32[]{:S(2)}, u32[]{:S(2)}) collective-permute-start(bf16[2,144,1024]{2,1,0:T(8,128)(2,1)S(1)} %pad_maximum_fusion.refs_0_), channel_id=1, source_target_pairs={{0,4},{4,0},{8,12},{12,8},{16,20},{20,16},{24,28},{28,24},{1,5},{5... | collective-permute-start | bytes 1769480 | tf_op jit(solution)/shard_map/ppermute | solution.py:324
  77.0 5.3 %collective-permute-start.19 = (bf16[2,144,1024]{2,1,0:T(8,128)(2,1)S(1)}, bf16[2,144,1024]{2,1,0:T(8,128)(2,1)S(1)}, u32[]{:S(2)}, u32[]{:S(2)}) collective-permute-start(bf16[2,144,1024]{2,1,0:T(8,128)(2,1)S(1)} %collective-permute-done.5.refs_1_), channel_id=1, source_target_pairs={{0,4},{4,0},{8,12},{12,8},{16,20},{20,16},{24,28},{28,24},{1,5},{5... | collective-permute-start | bytes 1769480 | tf_op jit(solution)/shard_map/ppermute | solution.py:324
  77.5 4.8 %collective-permute-start.20 = (bf16[2,144,1024]{2,1,0:T(8,128)(2,1)S(1)}, bf16[2,144,1024]{2,1,0:T(8,128)(2,1)S(1)}, u32[]{:S(2)}, u32[]{:S(2)}) collective-permute-start(bf16[2,144,1024]{2,1,0:T(8,128)(2,1)S(1)} %collective-permute-done.6.refs_2_), channel_id=1, source_target_pairs={{0,4},{4,0},{8,12},{12,8},{16,20},{20,16},{24,28},{28,24},{1,5},{5... | collective-permute-start | bytes 1769480 | tf_op jit(solution)/shard_map/ppermute | solution.py:324
  82.4 2.0 %collective-permute-start.21 = (bf16[2,144,1024]{2,1,0:T(8,128)(2,1)S(1)}, bf16[2,144,1024]{2,1,0:T(8,128)(2,1)S(1)}, u32[]{:S(2)}, u32[]{:S(2)}) collective-permute-start(bf16[2,144,1024]{2,1,0:T(8,128)(2,1)S(1)} %collective-permute-done.16.refs_3_), channel_id=1, source_target_pairs={{0,4},{4,0},{8,12},{12,8},{16,20},{20,16},{24,28},{28,24},{1,5},{5... | collective-permute-start | bytes 1769480 | tf_op jit(solution)/shard_map/ppermute | solution.py:324
  87.7 8.0 %collective-permute-start.23 = (f32[8,2,1024]{2,1,0:T(2,128)S(1)}, f32[8,2,1024]{2,1,0:T(2,128)S(1)}, u32[]{:S(2)}, u32[]{:S(2)}) collective-permute-start(f32[8,2,1024]{2,1,0:T(2,128)S(1)} %get-tuple-element.36), channel_id=1, source_target_pairs={{0,16},{4,20},{8,24},{12,28},{16,0},{20,4},{24,8},{28,12},{1,17},{... | collective-permute-start | bytes 196616 | tf_op jit(solution)/shard_map/ppermute | solution.py:424
  91.3 8.1 %collective-permute-start.22 = (f32[8,2,1024]{2,1,0:T(2,128)S(1)}, f32[8,2,1024]{2,1,0:T(2,128)S(1)}, u32[]{:S(2)}, u32[]{:S(2)}) collective-permute-start(f32[8,2,1024]{2,1,0:T(2,128)S(1)} %get-tuple-element.35), channel_id=1, source_target_pairs={{0,8},{4,12},{8,16},{12,20},{16,24},{20,28},{24,0},{28,4},{1,9},{5... | collective-permute-start | bytes 196616 | tf_op jit(solution)/shard_map/ppermute | solution.py:424
  95.6 4.6 %collective-permute-start.24 = (f32[8,2,1024]{2,1,0:T(2,128)S(1)}, f32[8,2,1024]{2,1,0:T(2,128)S(1)}, u32[]{:S(2)}, u32[]{:S(2)}) collective-permute-start(f32[8,2,1024]{2,1,0:T(2,128)S(1)} %get-tuple-element.37), channel_id=1, source_target_pairs={{0,24},{4,28},{8,0},{12,4},{16,8},{20,12},{24,16},{28,20},{1,25},{... | collective-permute-start | bytes 196616 | tf_op jit(solution)/shard_map/ppermute | solution.py:424
  (13 other events, 211.3 us)
